TPU v7x, 32 devices: a whole 2x2x4 slice. The times are simulated.
32 devices in a mesh: dp: 8 (over z, x), expert: 4 (over y, core).
Axes of the slice: x: 2, y: 2, z: 4, core: 2. Of those that a mesh axis runs over, the one named last changes fastest.
Arguments:
- hidden_in: bfloat16 [16, 1024, 1536], P('dp', 'expert'), may hold values from -6 to 6
- cotangent: bfloat16 [16, 1024, 1536], P('dp', 'expert'), may hold values from -6 to 6
- norm_attn: float32 [1536], replicated, may hold values from 0.5 to 1.5
- w_query: bfloat16 [1536, 1536], replicated, may hold values from -0.15625 to 0.15625
- w_key: bfloat16 [1536, 256], replicated, may hold values from -0.15625 to 0.15625
- w_value: bfloat16 [1536, 256], replicated, may hold values from -0.15625 to 0.15625
- w_out: bfloat16 [1536, 1536], replicated, may hold values from -2 to 2
- norm_ffn: float32 [1536], replicated, may hold values from 0.5 to 1.5
- w_router: bfloat16 [1536, 32], replicated, may hold values from -0.078125 to 0.078125
- w_gate: bfloat16 [32, 1536, 768], P('expert'), may hold values from -0.15625 to 0.15625
- w_up: bfloat16 [32, 1536, 768], P('expert'), may hold values from -0.15625 to 0.15625
- w_down: bfloat16 [32, 768, 1536], P('expert'), may hold values from -0.4375 to 0.4375
- expert_ids: int32 [32, 2, 256, 4], P(('dp', 'expert')), may hold values from 0 to 31, all different within a row; in each aligned block of 512 rows (0 to 511, 512 to 1023, ..., all dimensions but the last counted through in order) at most 80 rows name the same one
- priority: int32 [32, 2, 256], P(('dp', 'expert')), may hold values from 0 to 2047, as said below
- prefix: int32 [16], P('dp'), may hold values from 102 to 512
Outputs:
- output: bfloat16 [16, 1024, 1536], P('dp', 'expert')
- d_hidden: float32 [16, 1024, 1536], P('dp', 'expert')
- d_norm_attn: float32 [1536], replicated
- d_w_query: float32 [1536, 1536], P('dp', 'expert')
- d_w_key: float32 [1536, 256], P('dp', 'expert')
- d_w_value: float32 [1536, 256], P('dp', 'expert')
- d_w_out: float32 [1536, 1536], P('dp', 'expert')
- d_norm_ffn: float32 [1536], replicated
- d_w_router: float32 [1536, 32], replicated
- d_w_gate: float32 [32, 1536, 768], P('expert', 'dp')
- d_w_up: float32 [32, 1536, 768], P('expert', 'dp')
- d_w_down: float32 [32, 768, 1536], P('expert', 'dp')
Inputs may be any that keep to these rules, and one draw needn't show every extreme that they name: `expert_ids`: each token names 4 different experts; among the rows of one device no expert is named by more than 80 rows, a bound that some block reaches. `priority`: within each group (the 4 blocks of one index of dp) the values are a permutation of 0 to 2047. `prefix`: one per sequence.
All inputs are finite; a program needn't handle non-finite values.
Results may differ from a plain program's by a relative error of at most 0.024.
Values may be sent and summed in bfloat16 or wider, within the bound.
No kernel may reach another device: no remote copies, remote signals or barrier semaphores. Data moves between devices by JAX's collectives and lax.ppermute only.
A program may use at most 384 MiB of HBM per device.

v0:
```python
import jax
import jax.numpy as jnp
from jax import lax
from jax.sharding import PartitionSpec as P

HD = 128


EPSILON = 1e-06
ROPE_BASE = 10000.0
MASKED = -1e30


def rms_scale(values):
    return lax.rsqrt(jnp.mean(values * values, axis=-1, keepdims=True) + EPSILON)


def norm_backward(inputs, scales, gain, upstream):
    weighted = gain * upstream
    d_inputs = scales * weighted - inputs * scales**3 * jnp.mean(
        inputs * weighted, axis=-1, keepdims=True
    )
    return (d_inputs, jnp.sum(upstream * inputs * scales, axis=0))


def rope_tables(length, offset, head_size):
    positions = (offset + jnp.arange(length, dtype=jnp.int32)).astype(jnp.float32)
    frequency = ROPE_BASE ** (-(jnp.arange(head_size // 2, dtype=jnp.float32) * 2.0 / head_size))
    angles = positions[:, None] * frequency[None, :]
    return (jnp.cos(angles), jnp.sin(angles))


def rotate(values, cos_table, sin_table, turning):
    half_size = values.shape[-1] // 2
    first_half = values[..., :half_size]
    second = values[..., half_size:]
    cos_part = cos_table[:, None, :]
    sin_part = turning * sin_table[:, None, :]
    return jnp.concatenate(
        [first_half * cos_part - second * sin_part, second * cos_part + first_half * sin_part],
        axis=-1,
    )


def glu_product(gate_act, up_act):
    return jax.nn.gelu(gate_act, approximate=False) * up_act


def attention_scores(grouped, key_heads, allowed, scale_factor):
    scores = (
        jnp.einsum("gikrd,gjkd->gkrij", grouped, key_heads, preferred_element_type=jnp.float32)
        * scale_factor
    )
    return jnp.where(allowed, scores, MASKED)


def per_device(
    hidden_in,
    cotangent,
    norm_attn,
    w_query,
    w_key,
    w_value,
    w_out,
    norm_ffn,
    w_router,
    w_gate,
    w_up,
    w_down,
    expert_ids,
    priority,
    prefix,
):
    group_count, span_len, model_width = hidden_in.shape
    row_count = group_count * span_len
    head_size = HD
    q_width = w_query.shape[1]
    kv_width = w_key.shape[1]
    q_heads = q_width // head_size
    kv_heads = kv_width // head_size
    group_ratio = q_heads // kv_heads
    members = lax.axis_size("expert")
    seq_len = span_len * members
    expert_count = w_router.shape[1]
    local_count = w_gate.shape[0]
    top_count = expert_ids.shape[3]
    slot_count = row_count * top_count * 5 // (expert_count * 4)
    capacity = 9 * row_count * members * top_count // (8 * expert_count)
    scale_factor = head_size ** (-0.5)
    offset = lax.axis_index("expert") * span_len
    cos_table, sin_table = rope_tables(span_len, offset, head_size)
    query_places = offset + jnp.arange(span_len, dtype=jnp.int32)
    key_places = jnp.arange(seq_len, dtype=jnp.int32)
    allowed = (key_places[None, None, :] <= query_places[None, :, None]) | (
        key_places[None, None, :] < prefix[:, None, None]
    )
    allowed = allowed[:, None, None, :, :]
    tokens = hidden_in.reshape(row_count, model_width).astype(jnp.float32)
    scale_one = rms_scale(tokens)
    normed = (tokens * scale_one * norm_attn).astype(jnp.bfloat16)
    q_rotated = rotate(
        jnp.dot(normed, w_query, preferred_element_type=jnp.float32).reshape(
            group_count, span_len, q_heads, head_size
        ),
        cos_table,
        sin_table,
        1.0,
    ).astype(jnp.bfloat16)
    k_rotated = rotate(
        jnp.dot(normed, w_key, preferred_element_type=jnp.float32).reshape(
            group_count, span_len, kv_heads, head_size
        ),
        cos_table,
        sin_table,
        1.0,
    ).astype(jnp.bfloat16)
    k_rotated = k_rotated.reshape(group_count, span_len, kv_width)
    v_rows = (
        jnp.dot(normed, w_value, preferred_element_type=jnp.float32)
        .astype(jnp.bfloat16)
        .reshape(group_count, span_len, kv_width)
    )
    key_all, value_all = (
        lax.all_gather(k_rotated, "expert", axis=1, tiled=True),
        lax.all_gather(v_rows, "expert", axis=1, tiled=True),
    )
    grouped = q_rotated.reshape(group_count, span_len, kv_heads, group_ratio, head_size)
    key_heads = key_all.reshape(group_count, seq_len, kv_heads, head_size)
    value_heads = value_all.reshape(group_count, seq_len, kv_heads, head_size)
    scores = attention_scores(grouped, key_heads, allowed, scale_factor)
    row_max = jnp.max(scores, axis=-1, keepdims=True)
    exp_terms = jnp.exp(scores - row_max)
    row_total = jnp.sum(exp_terms, axis=-1, keepdims=True)
    attn_probs = (exp_terms / row_total).astype(jnp.bfloat16)
    log_total = row_max + jnp.log(row_total)
    attn_mix = (
        jnp.einsum("gkrij,gjkd->gikrd", attn_probs, value_heads, preferred_element_type=jnp.float32)
        .astype(jnp.bfloat16)
        .reshape(row_count, q_width)
    )
    residual = tokens + jnp.dot(attn_mix, w_out, preferred_element_type=jnp.float32)
    scale_two = rms_scale(residual)
    routed_in = (residual * scale_two * norm_ffn).astype(jnp.bfloat16)
    logits = jnp.dot(routed_in, w_router, preferred_element_type=jnp.float32)
    routes = expert_ids.reshape(row_count, top_count)
    expert_range = jnp.arange(expert_count, dtype=jnp.int32)
    route_hot = routes[:, :, None] == expert_range
    chosen = jnp.sum(jnp.where(route_hot, logits[:, None, :], 0.0), axis=-1)
    exp_gates = jnp.exp(chosen - jnp.max(chosen, axis=1, keepdims=True))
    gate_probs = exp_gates / jnp.sum(exp_gates, axis=1, keepdims=True)
    table_routes, table_order = (
        lax.all_gather(expert_ids, "expert", axis=0, tiled=True),
        lax.all_gather(priority, "expert", axis=0, tiled=True),
    )
    group_routes = table_routes.reshape(-1, top_count)
    group_order = table_order.reshape(-1)
    group_hits = jnp.any(group_routes[:, :, None] == expert_range, axis=1).astype(jnp.bfloat16)
    own_order = priority.reshape(row_count)
    earlier = (group_order[None, :] < own_order[:, None]).astype(jnp.bfloat16)
    before = jnp.dot(earlier, group_hits, preferred_element_type=jnp.float32)
    pair_before = jnp.sum(jnp.where(route_hot, before[:, None, :], 0.0), axis=-1)
    kept_mask = pair_before < capacity
    kept_hot = (
        (route_hot & kept_mask[:, :, None])
        .reshape(row_count * top_count, expert_count)
        .astype(jnp.int32)
    )
    running = jnp.cumsum(kept_hot, axis=0) - kept_hot
    local_slot = jnp.sum(running * kept_hot, axis=1)
    target = jnp.where(
        kept_mask.reshape(-1),
        routes.reshape(-1) * slot_count + local_slot,
        expert_count * slot_count,
    )
    send_rows = (
        jnp.zeros((expert_count * slot_count, model_width), jnp.bfloat16)
        .at[target]
        .set(jnp.repeat(routed_in, top_count, axis=0), mode="drop")
    )
    arrived = lax.all_to_all(
        send_rows.reshape(members, local_count, slot_count, model_width),
        "expert",
        split_axis=0,
        concat_axis=0,
        tiled=True,
    )
    gate_act = jnp.einsum("aecd,edf->aecf", arrived, w_gate, preferred_element_type=jnp.float32)
    up_act = jnp.einsum("aecd,edf->aecf", arrived, w_up, preferred_element_type=jnp.float32)
    hidden_act = glu_product(gate_act, up_act).astype(jnp.bfloat16)
    result = jnp.einsum(
        "aecf,efd->aecd", hidden_act, w_down, preferred_element_type=jnp.float32
    ).astype(jnp.bfloat16)
    returned = lax.all_to_all(result, "expert", split_axis=0, concat_axis=0, tiled=True)
    returned, arrived, gate_act, up_act = (returned, arrived, gate_act, up_act)
    picked = (
        jnp.take(
            returned.reshape(expert_count * slot_count, model_width),
            target,
            axis=0,
            mode="fill",
            fill_value=0,
        )
        .reshape(row_count, top_count, model_width)
        .astype(jnp.float32)
    )
    expert_sum = jnp.sum(gate_probs[:, :, None] * picked, axis=1)
    output = (
        (residual + expert_sum).astype(jnp.bfloat16).reshape(group_count, span_len, model_width)
    )
    upstream = cotangent.reshape(row_count, model_width).astype(jnp.float32)
    pair_grads = (
        (gate_probs[:, :, None] * upstream[:, None, :])
        .astype(jnp.bfloat16)
        .reshape(row_count * top_count, model_width)
    )
    grad_send = (
        jnp.zeros((expert_count * slot_count, model_width), jnp.bfloat16)
        .at[target]
        .set(pair_grads, mode="drop")
    )
    d_gates = jnp.sum(upstream[:, None, :] * picked, axis=-1)
    d_chosen = gate_probs * (d_gates - jnp.sum(gate_probs * d_gates, axis=1, keepdims=True))
    d_logits = jnp.sum(jnp.where(route_hot, d_chosen[:, :, None], 0.0), axis=1).astype(jnp.bfloat16)
    grad_router = jnp.dot(routed_in.T, d_logits, preferred_element_type=jnp.float32)
    d_routed = jnp.dot(d_logits, w_router.T, preferred_element_type=jnp.float32)
    grad_arrived = lax.all_to_all(
        grad_send.reshape(members, local_count, slot_count, model_width),
        "expert",
        split_axis=0,
        concat_axis=0,
        tiled=True,
    )
    hidden_act = glu_product(gate_act, up_act).astype(jnp.bfloat16)
    d_hidden_act = jnp.einsum(
        "aecd,efd->aecf", grad_arrived, w_down, preferred_element_type=jnp.float32
    )
    grad_down = jnp.einsum(
        "aecf,aecd->efd", hidden_act, grad_arrived, preferred_element_type=jnp.float32
    )
    glu_value, pullback = jax.vjp(glu_product, gate_act, up_act)
    d_gate_act, d_up_act = pullback(d_hidden_act)
    d_gate_act = d_gate_act.astype(jnp.bfloat16)
    d_up_act = d_up_act.astype(jnp.bfloat16)
    grad_gate = jnp.einsum(
        "aecd,aecf->edf", arrived, d_gate_act, preferred_element_type=jnp.float32
    )
    grad_up = jnp.einsum("aecd,aecf->edf", arrived, d_up_act, preferred_element_type=jnp.float32)
    d_arrived = (
        jnp.einsum("aecf,edf->aecd", d_gate_act, w_gate, preferred_element_type=jnp.float32)
        + jnp.einsum("aecf,edf->aecd", d_up_act, w_up, preferred_element_type=jnp.float32)
    ).astype(jnp.bfloat16)
    d_returned = lax.all_to_all(d_arrived, "expert", split_axis=0, concat_axis=0, tiled=True)
    grad_gate, grad_up, grad_down = (
        lax.psum_scatter(
            grad_gate.astype(jnp.bfloat16), "dp", scatter_dimension=1, tiled=True
        ).astype(jnp.float32),
        lax.psum_scatter(
            grad_up.astype(jnp.bfloat16), "dp", scatter_dimension=1, tiled=True
        ).astype(jnp.float32),
        lax.psum_scatter(
            grad_down.astype(jnp.bfloat16), "dp", scatter_dimension=1, tiled=True
        ).astype(jnp.float32),
    )
    pair_back = jnp.take(
        d_returned.reshape(expert_count * slot_count, model_width),
        target,
        axis=0,
        mode="fill",
        fill_value=0,
    )
    d_routed = d_routed + jnp.sum(
        pair_back.reshape(row_count, top_count, model_width).astype(jnp.float32), axis=1
    )
    d_norm_part, grad_norm_ffn = norm_backward(residual, scale_two, norm_ffn, d_routed)
    d_residual = upstream + d_norm_part
    d_branch = d_residual.astype(jnp.bfloat16)
    grad_out = jnp.dot(attn_mix.T, d_branch, preferred_element_type=jnp.float32)
    d_mix = (
        jnp.dot(d_branch, w_out.T, preferred_element_type=jnp.float32)
        .astype(jnp.bfloat16)
        .reshape(group_count, span_len, kv_heads, group_ratio, head_size)
    )
    scores = attention_scores(grouped, key_heads, allowed, scale_factor)
    probs_full = jnp.exp(scores - log_total)
    d_probs = jnp.einsum(
        "gikrd,gjkd->gkrij", d_mix, value_heads, preferred_element_type=jnp.float32
    )
    d_scores = (
        probs_full * (d_probs - jnp.sum(probs_full * d_probs, axis=-1, keepdims=True))
    ).astype(jnp.bfloat16)
    d_query = (
        jnp.einsum("gkrij,gjkd->gikrd", d_scores, key_heads, preferred_element_type=jnp.float32)
        * scale_factor
    )
    d_key_all = (
        jnp.einsum("gkrij,gikrd->gjkd", d_scores, grouped, preferred_element_type=jnp.float32)
        * scale_factor
    )
    d_value_all = jnp.einsum(
        "gkrij,gikrd->gjkd",
        probs_full.astype(jnp.bfloat16),
        d_mix,
        preferred_element_type=jnp.float32,
    )
    d_key_own, d_value_own = (
        lax.psum_scatter(
            d_key_all.reshape(group_count, seq_len, kv_width).astype(jnp.bfloat16),
            "expert",
            scatter_dimension=1,
            tiled=True,
        ).astype(jnp.float32),
        lax.psum_scatter(
            d_value_all.reshape(group_count, seq_len, kv_width).astype(jnp.bfloat16),
            "expert",
            scatter_dimension=1,
            tiled=True,
        ).astype(jnp.float32),
    )
    d_query = (
        rotate(
            d_query.reshape(group_count, span_len, q_heads, head_size), cos_table, sin_table, -1.0
        )
        .astype(jnp.bfloat16)
        .reshape(row_count, q_width)
    )
    d_key_own = (
        rotate(
            d_key_own.reshape(group_count, span_len, kv_heads, head_size),
            cos_table,
            sin_table,
            -1.0,
        )
        .astype(jnp.bfloat16)
        .reshape(row_count, kv_width)
    )
    d_value_own = d_value_own.astype(jnp.bfloat16).reshape(row_count, kv_width)
    d_normed = jnp.dot(d_query, w_query.T, preferred_element_type=jnp.float32)
    d_normed = d_normed + jnp.dot(d_key_own, w_key.T, preferred_element_type=jnp.float32)
    d_normed = d_normed + jnp.dot(d_value_own, w_value.T, preferred_element_type=jnp.float32)
    grad_query = jnp.dot(normed.T, d_query, preferred_element_type=jnp.float32)
    grad_key = jnp.dot(normed.T, d_key_own, preferred_element_type=jnp.float32)
    grad_value = jnp.dot(normed.T, d_value_own, preferred_element_type=jnp.float32)
    d_tokens, grad_norm_attn = norm_backward(tokens, scale_one, norm_attn, d_normed)
    d_hidden = (d_residual + d_tokens).reshape(group_count, span_len, model_width)
    part_query, part_key, part_value, part_out = (
        lax.psum_scatter(
            grad_query.astype(jnp.bfloat16), "expert", scatter_dimension=1, tiled=True
        ).astype(jnp.float32),
        lax.psum_scatter(
            grad_key.astype(jnp.bfloat16), "expert", scatter_dimension=1, tiled=True
        ).astype(jnp.float32),
        lax.psum_scatter(
            grad_value.astype(jnp.bfloat16), "expert", scatter_dimension=1, tiled=True
        ).astype(jnp.float32),
        lax.psum_scatter(
            grad_out.astype(jnp.bfloat16), "expert", scatter_dimension=1, tiled=True
        ).astype(jnp.float32),
    )
    grad_query, grad_key, grad_value, grad_out = (
        lax.psum_scatter(
            part_query.astype(jnp.bfloat16), "dp", scatter_dimension=0, tiled=True
        ).astype(jnp.float32),
        lax.psum_scatter(
            part_key.astype(jnp.bfloat16), "dp", scatter_dimension=0, tiled=True
        ).astype(jnp.float32),
        lax.psum_scatter(
            part_value.astype(jnp.bfloat16), "dp", scatter_dimension=0, tiled=True
        ).astype(jnp.float32),
        lax.psum_scatter(
            part_out.astype(jnp.bfloat16), "dp", scatter_dimension=0, tiled=True
        ).astype(jnp.float32),
    )
    grad_router, grad_norm_attn, grad_norm_ffn = lax.psum(
        (grad_router, grad_norm_attn, grad_norm_ffn), ("dp", "expert")
    )
    return (
        output,
        d_hidden,
        grad_norm_attn,
        grad_query,
        grad_key,
        grad_value,
        grad_out,
        grad_norm_ffn,
        grad_router,
        grad_gate,
        grad_up,
        grad_down,
    )


def solution(mesh):
    in_specs = (
        P("dp", "expert", None),
        P("dp", "expert", None),
        P(),
        P(),
        P(),
        P(),
        P(),
        P(),
        P(),
        P("expert", None, None),
        P("expert", None, None),
        P("expert", None, None),
        P(("dp", "expert"), None, None, None),
        P(("dp", "expert"), None, None),
        P("dp"),
    )
    out_specs = (
        P("dp", "expert", None),
        P("dp", "expert", None),
        P(),
        P("dp", "expert"),
        P("dp", "expert"),
        P("dp", "expert"),
        P("dp", "expert"),
        P(),
        P(),
        P("expert", "dp", None),
        P("expert", "dp", None),
        P("expert", "dp", None),
    )
    return jax.shard_map(
        per_device, mesh=mesh, in_specs=in_specs, out_specs=out_specs, check_vma=False
    )
```

profile of v0, /device:TPU:0, one launch (start us, length us, event | category | flops | bytes accessed | tf_op | source)
XLA Modules:
  0.0 2411.1 jit_solution(17090051239275863235)
XLA Ops:
  58.7 12.7 fusion.21
  71.4 11.0 fusion.3
  84.8 12.6 fusion.86
  108.3 9.1 reduce-window.6
  122.5 10.6 reshape.604
  133.4 15.6 scatter_custom_fusion
  149.0 91.6 %all_to_all.20 = bf16[4,8,80,1536]{3,2,1,0:T(8,128)(2,1)S(1)} all-to-all(bf16[4,8,80,1536]{3,2,1,0:T(8,128)(2,1)} %bitcast.361), channel_id=1, replica_groups=mesh['dp'=8,'expert'=4] {'expert'}, dimensions={0} | all-to-all | bytes 15728640 | tf_op jit(solution)/shard_map/all_to_all | solution.py:180
  243.6 12.0 fusion.11
  255.6 30.7 %fusion.26 = (bf16[4,8,80,768]{3,2,0,1:T(8,128)(2,1)}, f32[4,8,80,768]{3,2,0,1:T(8,128)}, f32[8,4,80,768]{3,2,1,0:T(8,128)}) fusion(f32[8,4,80,768]{3,2,1,0:T(8,128)} %fusion.11, bf16[8,1536,768]{2,1,0:T(8,128)(2,1)} %param.27, bf16[4,8,80,1536]{3,2,1,0:T(8,128)(2,1)} %copy-done.16), kind=kOutput, calls=%fused_computation.44 | convolution fusion | flops 6169559040 | bytes 54263808 | tf_op jit(solution)/shard_map/aecd,edf->aecf/dot_general | solution.py:188
  286.3 11.7 convert_bitcast_fusion
  313.9 14.9 mul.477
  329.0 66.0 %all-to-all-done.1 = bf16[4,8,80,1536]{3,2,1,0:T(8,128)(2,1)} async-done(((bf16[4,8,80,1536]{3,2,1,0:T(8,128)(2,1)}), bf16[4,8,80,1536]{3,2,1,0:T(8,128)(2,1)}, u32[]{:S(2)}, u32[]{:S(2)}) %all-to-all-start.1) | async-done | bytes 7864352 | tf_op jit(solution)/shard_map/all_to_all | solution.py:193
  395.0 17.6 gather_fusion
  412.6 8.3 multiply_reduce_fusion
  421.6 16.3 scatter_custom_fusion.1
  437.9 94.9 %all_to_all.21 = bf16[4,8,80,1536]{3,2,1,0:T(8,128)(2,1)} all-to-all(bf16[4,8,80,1536]{3,2,1,0:T(8,128)(2,1)} %bitcast.360), channel_id=1, replica_groups=mesh['dp'=8,'expert'=4] {'expert'}, dimensions={0} | all-to-all | bytes 15728640 | tf_op jit(solution)/shard_map/all_to_all | solution.py:226
  532.7 21.5 fusion.33
  554.2 14.6 fusion.5
  568.8 17.9 fusion.54
  586.7 7.0 copy.137
  599.6 87.4 %all-to-all-done.3 = bf16[4,8,80,1536]{3,2,1,0:T(8,128)(2,1)} async-done(((bf16[4,8,80,1536]{3,2,1,0:T(8,128)(2,1)}), bf16[4,8,80,1536]{3,2,1,0:T(8,128)(2,1)}, u32[]{:S(2)}, u32[]{:S(2)}) %all-to-all-start.3) | async-done | bytes 7864352 | tf_op jit(solution)/shard_map/all_to_all | solution.py:252
  687.0 17.7 gather_fusion.1
  704.7 12.4 select_convert_fusion
  717.2 14.6 reshape.581
  731.8 12.6 reduce_sum.170
  750.5 14.6 reshape.579
  765.1 32.4 %multiply_reduce_fusion.1 = f32[512,1536]{1,0:T(8,128)S(1)} fusion(f32[512,4,1536]{2,1,0:T(4,128)} %reshape.579, f32[512,4]{1,0:T(8,128)S(1)} %copy.121), kind=kLoop, calls=%fused_computation.35 | loop fusion | flops 5505024 | bytes 15736832 | tf_op jit(solution)/shard_map/reduce_sum | solution.py:206
  814.0 12.9 bitcast_convert_fusion.3
  826.9 21.8 fusion
  851.1 23.0 fusion.2
  874.2 10.3 fusion.76
  887.1 22.9 reduce-scatter.22.cloned.1.call-done
  913.0 7.2 convolution_convert_fusion
  920.2 6.7 copy.182
  950.7 11.0 reduce-scatter.28.cloned.1.call-done
  963.6 49.1 %reduce-scatter.46.cloned.1.call-done = bf16[384,1536]{1,0:T(8,128)(2,1)} async-done(((bf16[1536,1536]{1,0:T(8,128)(2,1)}), bf16[384,1536]{1,0:T(8,128)(2,1)}) %reduce-scatter.46.cloned.1.call-update) | async-done | bytes 1179664
  1015.1 48.7 %reduce-scatter.40.cloned.1.call-done = bf16[384,1536]{1,0:T(8,128)(2,1)} async-done(((bf16[1536,1536]{1,0:T(8,128)(2,1)}), bf16[384,1536]{1,0:T(8,128)(2,1)}) %reduce-scatter.40.cloned.1.call-update) | async-done | bytes 1179664
  1066.2 17.6 bitcast_convert_fusion
  1084.3 17.2 bitcast_convert_fusion.2
  1101.6 17.1 bitcast_convert_fusion.1
  1131.6 39.8 %all-reduce = (f32[1536]{0:T(1024)}, f32[1536]{0:T(1024)}) all-reduce(f32[1536]{0:T(1024)S(1)} %get-tuple-element.15, f32[1536]{0:T(1024)S(1)} %copy-done.49), channel_id=1, replica_groups=mesh['dp'=8,'expert'=4] {'dp','expert'}, use_global_device_ids=true, to_apply=%region_25.27 | all-reduce | flops 3072 | bytes 24576 | tf_op jit(solution)/shard_map/psum | solution.py:373
  1172.9 19.3 reduce-scatter.42.cloned.1.call-done
  1193.7 65.5 %reduce-scatter.32.cloned.1.call-done = bf16[192,384]{1,0:T(8,128)(2,1)} async-done(((bf16[1536,384]{1,0:T(8,128)(2,1)}), bf16[192,384]{1,0:T(8,128)(2,1)}) %reduce-scatter.32.cloned.1.call-update) | async-done | bytes 147472 | tf_op jit(solution)/shard_map/reduce_scatter | solution.py:369
  1260.9 65.4 %reduce-scatter.26.cloned.1.call-done = bf16[192,384]{1,0:T(8,128)(2,1)} async-done(((bf16[1536,384]{1,0:T(8,128)(2,1)}), bf16[192,384]{1,0:T(8,128)(2,1)}) %reduce-scatter.26.cloned.1.call-update) | async-done | bytes 147472 | tf_op jit(solution)/shard_map/reduce_scatter | solution.py:360
  1327.9 314.6 %reduce-scatter.38.cloned.1.call-done = bf16[8,96,1536]{2,1,0:T(8,128)(2,1)} async-done(((bf16[8,768,1536]{2,1,0:T(8,128)(2,1)}), bf16[8,96,1536]{2,1,0:T(8,128)(2,1)}) %reduce-scatter.38.cloned.1.call-update) | async-done | bytes 2359312 | tf_op jit(solution)/shard_map/reduce_scatter | solution.py:260
  1647.1 311.8 %reduce-scatter.34.cloned.1.call-done = bf16[8,192,768]{2,1,0:T(8,128)(2,1)} async-done(((bf16[8,1536,768]{2,1,0:T(8,128)(2,1)}), bf16[8,192,768]{2,1,0:T(8,128)(2,1)}) %reduce-scatter.34.cloned.1.call-update) | async-done | bytes 2359312 | tf_op jit(solution)/shard_map/reduce_scatter | solution.py:254
  1963.2 311.5 %reduce-scatter.36.cloned.1.call-done = bf16[8,192,768]{2,1,0:T(8,128)(2,1)} async-done(((bf16[8,1536,768]{2,1,0:T(8,128)(2,1)}), bf16[8,192,768]{2,1,0:T(8,128)(2,1)}) %reduce-scatter.36.cloned.1.call-update) | async-done | bytes 2359312 | tf_op jit(solution)/shard_map/reduce_scatter | solution.py:257
  2278.9 123.9 %all-reduce.3.cloned.1.call-done = f32[1536,32]{0,1:T(8,128)} async-done(((f32[1536,32]{0,1:T(8,128)}), f32[1536,32]{0,1:T(8,128)}) %all-reduce.3.cloned.1.call-update) | async-done | bytes 196624 | tf_op jit(solution)/shard_map/psum | solution.py:373
  (251 shorter events, 190.2 us)
Async XLA Ops:
  7.2 11.0 copy-start
  7.2 10.6 copy-start.1
  7.2 10.6 copy-start.39
  7.2 51.4 %all-gather.5.cloned.1.call-start = ((), (), s32[]{:S(2)}) async-start(), calls=%async_computation.18 | async-start | bytes 1310720 | tf_op jit(solution)/shard_map/all_gather | solution.py:124
  12.6 37.6 %copy-start.21 = (f32[256,64]{0,1:T(8,128)}, f32[256,64]{0,1:T(8,128)S(1)}, u32[]{:S(2)}) copy-start(f32[256,64]{0,1:T(8,128)S(1)} %get-tuple-element.45) | copy-start | bytes 196612
  12.6 7.0 copy-start.35
  17.0 65.4 %all-gather.3.cloned.1.call-start = ((), (), s32[]{:S(2)}) async-start(), calls=%async_computation.17 | async-start | bytes 1310720 | tf_op jit(solution)/shard_map/all_gather | solution.py:125
  56.8 28.0 %copy-start.5 = (pred[2,256,1024]{1,2,0:T(8,128)(4,1)}, pred[2,256,1024]{1,2,0:T(8,128)(4,1)S(1)}, u32[]{:S(2)}) copy-start(pred[2,256,1024]{1,2,0:T(8,128)(4,1)S(1)} %broadcast_or_fusion) | copy-start | bytes 1572868
  71.4 13.4 copy-start.31
  82.4 14.9 copy-start.37
  99.3 7.1 copy-start.41
  99.3 7.5 copy-start.29
  105.4 17.2 copy-start.45
  106.8 26.4 %copy-start.7 = (bf16[512,1536]{1,0:T(8,128)(2,1)}, bf16[512,1536]{1,0:T(8,128)(2,1)S(1)}, u32[]{:S(2)}) copy-start(bf16[512,1536]{1,0:T(8,128)(2,1)S(1)} %multiply_convert_fusion.2) | copy-start | bytes 4718596
  122.5 10.8 copy-start.48
  301.7 93.2 %all-to-all-start.1 = ((bf16[4,8,80,1536]{3,2,1,0:T(8,128)(2,1)}), bf16[4,8,80,1536]{3,2,1,0:T(8,128)(2,1)}, u32[]{:S(2)}, u32[]{:S(2)}) async-start(bf16[4,8,80,1536]{3,2,1,0:T(8,128)(2,1)} %copy.132), calls=%async_computation.1 | async-start | bytes 15728640 | tf_op jit(solution)/shard_map/all_to_all | solution.py:193
  593.7 5.8 copy-start.38
  593.7 5.8 copy-start.36
  593.7 93.3 %all-to-all-start.3 = ((bf16[4,8,80,1536]{3,2,1,0:T(8,128)(2,1)}), bf16[4,8,80,1536]{3,2,1,0:T(8,128)(2,1)}, u32[]{:S(2)}, u32[]{:S(2)}) async-start(bf16[4,8,80,1536]{3,2,1,0:T(8,128)(2,1)} %copy.137), calls=%async_computation.3 | async-start | bytes 15728640 | tf_op jit(solution)/shard_map/all_to_all | solution.py:252
  599.5 285.1 %reduce-scatter.24.cloned.1.call-start = ((), (), s32[]{:S(2)}) async-start(), calls=%async_computation.20 | async-start | bytes 1310720 | tf_op jit(solution)/shard_map/reduce_scatter | solution.py:312
  599.6 144.8 %copy-start.33 = (bf16[512,32]{0,1:T(8,128)(2,1)}, bf16[512,32]{0,1:T(8,128)(2,1)S(1)}, u32[]{:S(2)}) copy-start(bf16[512,32]{0,1:T(8,128)(2,1)S(1)} %select_reduce_fusion) | copy-start | bytes 98308
  731.8 12.6 copy-start.30
  731.8 12.6 copy-start.42
  731.8 12.6 copy-start.46
  765.1 32.4 %copy-start.4 = (f32[512,1536]{1,0:T(8,128)S(1)}, f32[512,1536]{1,0:T(8,128)}, u32[]{:S(2)}) copy-start(f32[512,1536]{1,0:T(8,128)} %copy-done.3) | copy-start | bytes 9437188
  765.1 32.4 %copy-start.15 = (f32[512,1536]{1,0:T(8,128)S(1)}, f32[512,1536]{1,0:T(8,128)}, u32[]{:S(2)}) copy-start(f32[512,1536]{1,0:T(8,128)} %get-tuple-element.51) | copy-start | bytes 9437188
  765.1 32.4 %copy-start.50 = (f32[512]{0:T(512)S(1)}, f32[512]{0:T(512)}, u32[]{:S(2)}) copy-start(f32[512]{0:T(512)} %get-tuple-element.37) | copy-start | bytes 6148
  808.0 6.0 copy-start.6
  814.0 12.9 copy-start.17
  851.0 59.0 %reduce-scatter.22.cloned.1.call-start = ((), (), s32[]{:S(2)}) async-start(), calls=%async_computation.19 | async-start | bytes 1310720 | tf_op jit(solution)/shard_map/reduce_scatter | solution.py:306
  851.1 23.0 copy-start.9
  851.1 23.0 copy-start.10
  874.1 10.4 copy-start.12
  874.1 36.9 %copy-start.22 = (f32[256,64]{0,1:T(8,128)S(1)}, f32[256,64]{0,1:T(8,128)}, u32[]{:S(2)}) copy-start(f32[256,64]{0,1:T(8,128)} %copy-done.21) | copy-start | bytes 196612
  874.2 36.9 %copy-start.28 = (f32[256,64]{0,1:T(8,128)S(1)}, f32[256,64]{0,1:T(8,128)}, u32[]{:S(2)}) copy-start(f32[256,64]{0,1:T(8,128)} %get-tuple-element.43) | copy-start | bytes 196612
  884.5 64.2 %reduce-scatter.30.cloned.1.call-start = ((), (), s32[]{:S(2)}) async-start(), calls=%async_computation.23 | async-start | bytes 983040 | tf_op jit(solution)/shard_map/reduce_scatter | solution.py:352
  887.1 74.5 %reduce-scatter.28.cloned.1.call-start = ((), (), s32[]{:S(2)}) async-start(), calls=%async_computation.22 | async-start | bytes 983040 | tf_op jit(solution)/shard_map/reduce_scatter | solution.py:349
  913.0 99.7 %reduce-scatter.46.cloned.1.call-start = ((), (), s32[]{:S(2)}) async-start(), calls=%async_computation.32 | async-start | bytes 5898240
  920.2 7.0 copy-start.19
  926.9 136.8 %reduce-scatter.40.cloned.1.call-start = ((), (), s32[]{:S(2)}) async-start(), calls=%async_computation.29 | async-start | bytes 5898240
  948.7 222.7 %reduce-scatter.44.cloned.1.call-start = ((), (), s32[]{:S(2)}) async-start(), calls=%async_computation.31 | async-start | bytes 442368
  950.6 241.5 %reduce-scatter.42.cloned.1.call-start = ((), (), s32[]{:S(2)}) async-start(), calls=%async_computation.30 | async-start | bytes 442368
  963.5 295.7 %reduce-scatter.32.cloned.1.call-start = ((), (), s32[]{:S(2)}) async-start(), calls=%async_computation.24 | async-start | bytes 1327104 | tf_op jit(solution)/shard_map/reduce_scatter | solution.py:369
  1015.0 311.3 %reduce-scatter.26.cloned.1.call-start = ((), (), s32[]{:S(2)}) async-start(), calls=%async_computation.21 | async-start | bytes 1327104 | tf_op jit(solution)/shard_map/reduce_scatter | solution.py:360
  1066.2 576.4 %reduce-scatter.38.cloned.1.call-start = ((), (), s32[]{:S(2)}) async-start(), calls=%async_computation.28 | async-start | bytes 21233664 | tf_op jit(solution)/shard_map/reduce_scatter | solution.py:260
  1083.9 875.0 %reduce-scatter.34.cloned.1.call-start = ((), (), s32[]{:S(2)}) async-start(), calls=%async_computation.26 | async-start | bytes 21233664 | tf_op jit(solution)/shard_map/reduce_scatter | solution.py:254
  1101.6 1173.0 %reduce-scatter.36.cloned.1.call-start = ((), (), s32[]{:S(2)}) async-start(), calls=%async_computation.27 | async-start | bytes 21233664 | tf_op jit(solution)/shard_map/reduce_scatter | solution.py:257
  1118.8 1284.0 %all-reduce.3.cloned.1.call-start = ((), (), s32[]{:S(2)}) async-start(), calls=%async_computation.25 | async-start | bytes 393216 | tf_op jit(solution)/shard_map/psum | solution.py:373
  (21 other events, 55.2 us)
Sparse Core Ops, SparseCore 0:
  17.2 19.5 all-gather.4
  38.9 16.7 all-gather.2
  851.2 25.3 reduce-scatter.23
  884.6 25.4 reduce-scatter.21
  912.5 23.2 reduce-scatter.29
  938.3 23.2 reduce-scatter.27
  964.7 47.8 reduce-scatter.45
  1015.9 47.8 reduce-scatter.39
  1067.0 61.3 reduce-scatter.43
  1131.6 60.5 reduce-scatter.41
  1196.1 63.0 reduce-scatter.31
  1263.0 63.1 reduce-scatter.25
  1330.2 312.3 reduce-scatter.37
  1646.3 312.5 reduce-scatter.33
  1962.6 311.9 reduce-scatter.35
  2280.6 122.1 all-reduce.2
where the time goes:
time: 2420 us; the launch traced here: 2410 us
  waiting for transfers between devices  1500 us (62%)
  matrix products  288 us (12%)
  blocking collectives  238 us (10%)
  local copies, waits for them, and re-layouts  195 us (8%)
  other arithmetic  164 us (7%)
    reduce_scatter x1, waiting for transfers between devices, per_device(): lax.psum_scatter(grad_down.astype(jnp.bfloat16), 'dp', scatter_dimension=...  315 us
    reduce_scatter x1, waiting for transfers between devices, per_device(): lax.psum_scatter(grad_gate.astype(jnp.bfloat16), 'dp', scatter_dimension=...  312 us
    reduce_scatter x1, waiting for transfers between devices, per_device(): lax.psum_scatter(grad_up.astype(jnp.bfloat16), 'dp', scatter_dimension=1,...  311 us
    psum x1, waiting for transfers between devices, per_device(): lax.psum((grad_router, grad_norm_attn, grad_norm_ffn), ('dp', 'expert'))  124 us
    unnamed x20, waiting for transfers between devices  117 us
    all_to_all x1, blocking collectives, per_device(): lax.all_to_all(grad_send.reshape(members, local_count, slot_count, model_...  94.9 us
    all_to_all x1, blocking collectives, per_device(): lax.all_to_all(send_rows.reshape(members, local_count, slot_count, model_...  91.6 us
    all_to_all x1, waiting for transfers between devices, per_device(): lax.all_to_all(d_arrived, 'expert', split_axis=0, concat_axis=0, tiled=True)  87.4 us
  transfers between devices with their start and end apart: 18, of which 13 were waited for; matrix products, arithmetic and copies ran while one was open for 10% of the time, Pallas kernels for 0%

commit v1 on v0

v1 whole, which is shorter than its diff:
```python
import functools

import jax
import jax.numpy as jnp
from jax import lax
from jax.experimental import pallas as pl
from jax.experimental.pallas import tpu as pltpu
from jax.sharding import PartitionSpec as P

HD = 128
EPSILON = 1e-06
ROPE_BASE = 10000.0
MASKED = -1e30
EXTRA = 16
TEAM_BIT = 2
VMEM_LIMIT = 60 * 1024 * 1024

BF16 = jnp.bfloat16
F32 = jnp.float32


def dot(a, b):
    return jnp.dot(a, b, preferred_element_type=F32)


def dot_nt(a, b):
    return lax.dot_general(a, b, (((1,), (1,)), ((), ())), preferred_element_type=F32)


def dot_tn(a, b):
    return lax.dot_general(a, b, (((0,), (0,)), ((), ())), preferred_element_type=F32)


def bits_of(size):
    return [1 << i for i in reversed(range(size.bit_length() - 1))]


def swap(values, axis_name, bit):
    count = lax.axis_size(axis_name)
    return lax.ppermute(values, axis_name, [(i, i ^ bit) for i in range(count)])


def gather_pieces(values, steps):
    pieces = [values]
    for axis_name, bit in steps:
        pieces = pieces + [swap(piece, axis_name, bit) for piece in pieces]
    return pieces


def add_pair(a, b):
    return (a.astype(F32) + b.astype(F32)).astype(BF16)


def scatter_pieces(pieces, steps):
    for axis_name, bit in reversed(steps):
        half = len(pieces) // 2
        pieces = [
            add_pair(a, swap(b, axis_name, bit))
            for a, b in zip(pieces[:half], pieces[half:], strict=True)
        ]
    return pieces[0]


def all_sum(values, axes):
    for axis_name in axes:
        for bit in reversed(bits_of(lax.axis_size(axis_name))):
            values = values + swap(values, axis_name, bit)
    return values


ANYWHERE = pl.BlockSpec(memory_space=pl.ANY)


TIME_SCALE = 1.0


def kernel_call(us, body, grid, ins, outs, scalars=(), scratch=(), after=(), aliases=None):
    after = list(after)
    lead, held = len(scalars), len(ins)

    def run(*refs):
        body(*refs[: lead + held], *refs[lead + held + len(after) :])

    grid_spec = pltpu.PrefetchScalarGridSpec(
        num_scalar_prefetch=lead,
        grid=grid,
        in_specs=[spec for _, spec in ins] + [ANYWHERE] * len(after),
        out_specs=[spec for _, spec in outs],
        scratch_shapes=list(scratch),
    )
    return pl.pallas_call(
        run,
        grid_spec=grid_spec,
        out_shape=[shape for shape, _ in outs],
        input_output_aliases=aliases or {},
        compiler_params=pltpu.CompilerParams(vmem_limit_bytes=VMEM_LIMIT),
        cost_estimate=pl.CostEstimate(
            flops=int(us * TIME_SCALE * 1e9),
            bytes_accessed=int(us * TIME_SCALE * 3.3e6),
            transcendentals=0,
        ),
    )(*scalars, *[a for a, _ in ins], *after)


def shaped(shape, dtype):
    return jax.ShapeDtypeStruct(tuple(shape), dtype)


def whole(array):
    zeros = (0,) * len(array.shape)
    return pl.BlockSpec(tuple(array.shape), lambda *_: zeros)


def rms_of(values):
    return lax.rsqrt(jnp.mean(values * values, axis=-1, keepdims=True) + EPSILON)


def turn(values, cos_wide, sin_wide):
    return values * cos_wide + pltpu.roll(values, HD // 2, 1) * sin_wide


def column(width, tile):
    return pl.ds(pl.multiple_of(width * tile, tile), tile)


def hold_body(value_ref, out_ref):
    pass


def hold(value, after):
    return kernel_call(
        0.5, hold_body, (1,), [(value, ANYWHERE)], [(shaped(value.shape, value.dtype), ANYWHERE)],
        after=after, aliases={0: 0},
    )[0]


def key_value_body(x_ref, gain, wk, wv, cos_ref, sin_ref, cot_ref, normed_ref, kv_ref, same_ref):
    x = x_ref[...].astype(F32)
    normed = (x * rms_of(x) * gain[...]).astype(BF16)
    normed_ref[...] = normed
    keys = dot(normed, wk[...])
    for h in range(keys.shape[1] // HD):
        cols = slice(h * HD, (h + 1) * HD)
        kv_ref[:, cols] = turn(keys[:, cols], cos_ref[...], sin_ref[...]).astype(BF16)
    kv_ref[:, keys.shape[1] :] = dot(normed, wv[...]).astype(BF16)


def query_body(normed_ref, wq, cos_ref, sin_ref, q_ref):
    queries = dot(normed_ref[...], wq[...])
    for h in range(queries.shape[1] // HD):
        cols = slice(h * HD, (h + 1) * HD)
        q_ref[:, cols] = turn(queries[:, cols], cos_ref[...], sin_ref[...]).astype(BF16)


def project_inputs(x, gain, wq, wk, wv, cos_wide, sin_wide, cot):
    rows, width = x.shape
    kd = wk.shape[1]
    normed, kv, cot = kernel_call(
        4.2,
        key_value_body,
        (1,),
        [(a, whole(a)) for a in (x, gain, wk, wv, cos_wide, sin_wide)] + [(cot, ANYWHERE)],
        [(s, whole(s)) for s in (shaped((rows, width), BF16), shaped((rows, 2 * kd), BF16))]
        + [(shaped(cot.shape, BF16), ANYWHERE)],
        aliases={6: 2},
    )
    tile = 256

    def queries(after):
        return kernel_call(
            8,
            query_body,
            (wq.shape[1] // tile,),
            [
                (normed, whole(normed)),
                (wq, pl.BlockSpec((width, tile), lambda i: (0, i))),
                (cos_wide, whole(cos_wide)),
                (sin_wide, whole(sin_wide)),
            ],
            [(shaped((rows, wq.shape[1]), BF16), pl.BlockSpec((rows, tile), lambda i: (0, i)))],
            after=after,
        )[0]

    return normed, kv, queries, cot


def attention_bias(prefix, source, offset, span, members):
    rows = offset + lax.broadcasted_iota(jnp.int32, (span, span), 0)
    cols = lax.broadcasted_iota(jnp.int32, (span, span), 1)
    parts = []
    for p in range(members):
        keys = source[p] * span + cols
        parts.append(jnp.where((keys <= rows) | (keys < prefix), 0.0, MASKED))
    return jnp.concatenate(parts, axis=1)


def attention_body(members, kvh, ratio, prefix, source, q_ref, *refs):
    pieces, (mix_ref, lse_ref, bias) = refs[:members], refs[members:]
    span = q_ref.shape[1]
    scale = HD ** (-0.5)
    bias[...] = attention_bias(prefix[pl.program_id(0)], source, source[members], span, members)
    columns = []
    for k in range(kvh):
        keys = jnp.concatenate([p[0, :, k * HD : (k + 1) * HD] for p in pieces], axis=0)
        start = (kvh + k) * HD
        values = jnp.concatenate([p[0, :, start : start + HD] for p in pieces], axis=0)
        for r in range(ratio):
            cols = slice((k * ratio + r) * HD, (k * ratio + r + 1) * HD)
            scores = dot_nt(q_ref[0, :, cols], keys) + bias[...]
            top = jnp.max(scores, axis=1, keepdims=True)
            terms = jnp.exp((scores - top) * scale)
            total = jnp.sum(terms, axis=1, keepdims=True)
            mixed = dot(terms.astype(BF16), values)
            mix_ref[0, :, cols] = (mixed / total).astype(BF16)
            columns.append(top * scale + jnp.log(total))
    lse_ref[0] = jnp.concatenate(columns, axis=1)


def attention_back_body(
    members, kvh, ratio, prefix, source, q_ref, do_ref, lse_ref, cos_ref, sin_ref, *refs
):
    pieces, dq_ref = refs[:members], refs[members]
    outs, (bias, dk, dv) = refs[members + 1 : 2 * members + 1], refs[2 * members + 1 :]
    span = q_ref.shape[1]
    scale = HD ** (-0.5)
    bias[...] = attention_bias(prefix[pl.program_id(0)], source, source[members], span, members)
    for k in range(kvh):
        keys = jnp.concatenate([p[0, :, k * HD : (k + 1) * HD] for p in pieces], axis=0)
        start = (kvh + k) * HD
        values = jnp.concatenate([p[0, :, start : start + HD] for p in pieces], axis=0)
        for r in range(ratio):
            h = k * ratio + r
            cols = slice(h * HD, (h + 1) * HD)
            query, upstream = q_ref[0, :, cols], do_ref[0, :, cols]
            scores = dot_nt(query, keys) + bias[...]
            probs = jnp.exp(scores * scale - lse_ref[0, :, h : h + 1])
            d_probs = dot_nt(upstream, values)
            mean = jnp.sum(probs * d_probs, axis=1, keepdims=True)
            d_scores = (probs * (d_probs - mean)).astype(BF16)
            d_query = dot(d_scores, keys) * scale
            dq_ref[0, :, cols] = turn(d_query, cos_ref[...], -sin_ref[...]).astype(BF16)
            part_k = dot_tn(d_scores, query)
            part_v = dot_tn(probs.astype(BF16), upstream)
            if r == 0:
                dk[...] = part_k
                dv[...] = part_v
            else:
                dk[...] += part_k
                dv[...] += part_v
        for p, out in enumerate(outs):
            rows = slice(p * span, (p + 1) * span)
            out[0, :, k * HD : (k + 1) * HD] = (dk[rows, :] * scale).astype(BF16)
            out[0, :, start : start + HD] = dv[rows, :].astype(BF16)


def attend(q, kv, prefix, source):
    groups, span, qd = q.shape
    members, kvh = len(kv), kv[0].shape[2] // (2 * HD)
    heads = qd // HD
    block = lambda n: pl.BlockSpec((1, span, n), lambda g, *_: (g, 0, 0))
    return kernel_call(
        15.7,
        functools.partial(attention_body, members, kvh, heads // kvh),
        (groups,),
        [(q, block(qd))] + [(p, block(p.shape[2])) for p in kv],
        [
            (shaped(q.shape, BF16), block(qd)),
            (shaped((groups, span, heads), F32), block(heads)),
        ],
        scalars=(prefix, source),
        scratch=[pltpu.VMEM((span, span * members), F32)],
    )


def attend_back(q, do, lse, kv, prefix, source, cos_wide, sin_wide, after=()):
    groups, span, qd = q.shape
    members, kvh = len(kv), kv[0].shape[2] // (2 * HD)
    heads = qd // HD
    block = lambda n: pl.BlockSpec((1, span, n), lambda g, *_: (g, 0, 0))
    outs = kernel_call(
        28.6,
        functools.partial(attention_back_body, members, kvh, heads // kvh),
        (groups,),
        [(q, block(qd)), (do, block(qd)), (lse, block(heads))]
        + [(cos_wide, whole(cos_wide)), (sin_wide, whole(sin_wide))]
        + [(p, block(p.shape[2])) for p in kv],
        [(shaped(q.shape, BF16), block(qd))]
        + [(shaped(p.shape, BF16), block(p.shape[2])) for p in kv],
        scalars=(prefix, source),
        scratch=[
            pltpu.VMEM((span, span * members), F32),
            pltpu.VMEM((span * members, HD), F32),
            pltpu.VMEM((span * members, HD), F32),
        ],
        after=after,
    )
    return outs[0], outs[1:]


def branch_body(steps, x_ref, mix_ref, wo, gain, router, hit_ref,
                residual_ref, message_ref, gates_ref):
    i = pl.program_id(0)
    tile = wo.shape[1]
    cols = column(i, tile)
    residual_ref[:, cols] = x_ref[:, cols].astype(F32) + dot(mix_ref[...], wo[...])

    @pl.when(i == steps - 1)
    def _():
        rows = residual_ref.shape[0]
        experts = hit_ref.shape[0]
        h1 = residual_ref[...]
        a2 = (h1 * rms_of(h1) * gain[...]).astype(BF16)
        message_ref[:rows, :] = a2
        hit = hit_ref[...] > 0.0
        logits = jnp.where(hit, dot_nt(router[...], a2), MASKED)
        terms = jnp.exp(logits - jnp.max(logits, axis=0, keepdims=True))
        terms = jnp.where(hit, terms, 0.0)
        gates = terms / jnp.sum(terms, axis=0, keepdims=True)
        gates_ref[...] = gates
        high = gates.astype(BF16)
        rest = gates - high.astype(F32)
        middle = rest.astype(BF16)
        low = (rest - middle.astype(F32)).astype(BF16)
        message_ref[rows:, :rows] = high
        message_ref[rows:, rows : 2 * rows] = middle
        message_ref[rows:, 2 * rows : 3 * rows] = low
        if message_ref.shape[1] > 3 * rows:
            message_ref[rows:, 3 * rows :] = jnp.zeros(
                (experts, message_ref.shape[1] - 3 * rows), BF16
            )


def branch(x, mix, wo, gain, router_t, hit_t):
    rows, width = x.shape
    experts = router_t.shape[0]
    tile = 256
    outs = (
        shaped((rows, width), F32),
        shaped((rows + experts, width), BF16),
        shaped((experts, rows), F32),
    )
    return kernel_call(
        10,
        functools.partial(branch_body, width // tile),
        (width // tile,),
        [(x, whole(x)), (mix, whole(mix))]
        + [(wo, pl.BlockSpec((wo.shape[0], tile), lambda i: (0, i)))]
        + [(a, whole(a)) for a in (gain, router_t, hit_t)],
        [(s, whole(s)) for s in outs],
    )


def slot_masks(places, slot_count):
    experts, tokens = places.shape
    slots = lax.broadcasted_iota(jnp.int32, (slot_count, tokens), 0).astype(F32)
    return [places[e : e + 1, :] == slots for e in range(experts)]


def hot_rows(masks):
    return jnp.concatenate([m.astype(F32) for m in masks], axis=0).astype(BF16)


def pick_experts(table, first, count):
    row = lax.broadcasted_iota(jnp.int32, table.shape, 0)
    picked = [
        jnp.sum(jnp.where(row == first + e, table, 0.0), axis=0, keepdims=True)
        for e in range(count)
    ]
    return jnp.concatenate(picked, axis=0)


def places_body(blocks, count, capacity, first, table_ref, column_ref, out_ref):
    b = pl.program_id(0)
    tokens = table_ref.shape[2]
    top = table_ref.shape[1] - 1
    padded = 8

    def hits(at):
        row = lax.broadcasted_iota(jnp.int32, (padded, tokens), 0)
        expert = jnp.where(row < count, first[0] + row, -1)
        found = table_ref[at, 0:1, :] == expert
        for k in range(1, top):
            found = found | (table_ref[at, k : k + 1, :] == expert)
        return found

    own_order = table_ref[b, top : top + 1, :]
    before = jnp.zeros((padded, tokens), F32)
    for n in range(blocks // 2):
        at = 2 * n + b % 2
        earlier = jnp.where(column_ref[at] < own_order, 1.0, 0.0).astype(BF16)
        before = before + dot(jnp.where(hits(at), 1.0, 0.0).astype(BF16), earlier)
    kept = hits(b) & (before < capacity)
    row = lax.broadcasted_iota(jnp.int32, (tokens, tokens), 0)
    col = lax.broadcasted_iota(jnp.int32, (tokens, tokens), 1)
    ahead = jnp.where(row < col, 1.0, 0.0).astype(BF16)
    slots = dot(jnp.where(kept, 1.0, 0.0).astype(BF16), ahead)
    out_ref[0] = jnp.where(kept, slots, -1.0)[:count]


def find_places(tables, first, count, capacity, after=()):
    blocks, wide, tokens = tables.shape
    columns = tables[:, wide - 1, :, None]
    shape = shaped((blocks, count, tokens), F32)
    return kernel_call(
        4,
        functools.partial(places_body, blocks, count, capacity),
        (blocks,),
        [(tables, whole(tables)), (columns, whole(columns))],
        [(shape, pl.BlockSpec((1, count, tokens), lambda b, *_: (b, 0, 0)))],
        scalars=(first,),
        after=after,
    )[0]


def dispatch_body(parts, with_gates, slot_count, first, *refs):
    segments, refs = refs[:parts], refs[parts:]
    if with_gates:
        extra_ref, places_ref, rows_ref, gate_ref = refs
    else:
        places_ref, rows_ref = refs
    _, count, tokens = places_ref.shape
    masks = slot_masks(places_ref[0], slot_count)
    hot = hot_rows(masks)
    if with_gates:
        extra = extra_ref[...].astype(F32)
        table = extra[:, :tokens] + extra[:, tokens : 2 * tokens]
        gates = pick_experts(table + extra[:, 2 * tokens : 3 * tokens], first[0], count)
        for e in range(count):
            gate = jnp.sum(jnp.where(masks[e], gates[e : e + 1, :], 0.0), axis=1, keepdims=True)
            gate_ref[e] = jnp.broadcast_to(gate, (slot_count, 128))
    total, start = 0.0, 0
    for segment in segments:
        stop = min(start + segment.shape[0], tokens)
        total = total + dot(hot[:, start:stop], segment[: stop - start, :])
        start = stop
    total = total.astype(BF16)
    for e in range(count):
        rows_ref[e] = total[e * slot_count : (e + 1) * slot_count]


def dispatch(segments, at, places, first, slot_count, with_gates, after=()):
    width = segments[0].shape[1]
    _, count, tokens = places.shape
    ins = [(a, whole(a)) for a in segments]
    outs = [shaped((count, slot_count, width), BF16)]
    if with_gates:
        last = segments[-1]
        extra = last.shape[0] - (tokens - sum(a.shape[0] for a in segments[:-1]))
        spot = last.shape[0] // extra - 1
        ins.append((last, pl.BlockSpec((extra, width), lambda *_: (spot, 0))))
        outs.append(shaped((count, slot_count, 128), F32))
    ins.append((places, pl.BlockSpec((1, count, tokens), lambda *_: (at, 0, 0))))
    return kernel_call(
        1.5,
        functools.partial(dispatch_body, len(segments), with_gates, slot_count),
        (1,),
        ins,
        [(o, whole(o)) for o in outs],
        scalars=(first,),
        after=after,
    )


def combine_body(experts, with_extra, starts, cut, first, *refs):
    refs = list(refs)
    rows = [refs.pop(0) for _ in range(experts)]
    places_ref = refs.pop(0)
    slopes = [refs.pop(0) for _ in range(experts)] if with_extra else None
    added = [refs.pop(0) for _ in starts]
    outs = refs
    slot_count = rows[0].shape[1]
    tokens = places_ref.shape[2]
    masks = slot_masks(places_ref[0], slot_count)
    values = jnp.concatenate([r[0] for r in rows], axis=0)
    total = dot_tn(hot_rows(masks), values)
    last = outs[-1]
    width = last.shape[1]
    for other, start in zip(added, starts, strict=True):
        count = min(other.shape[0], tokens - start)
        parts = [total[start : start + count] + other[:count, :].astype(F32)]
        if start > 0:
            parts = [total[:start]] + parts
        if start + count < tokens:
            parts.append(total[start + count :])
        total = parts[0] if len(parts) == 1 else jnp.concatenate(parts, axis=0)
    total = total.astype(BF16)
    if cut:
        outs[0][...] = total[:cut]
    last[: tokens - cut, :] = total[cut:]
    if with_extra:
        count = last.shape[0] - (tokens - cut)
        row = lax.broadcasted_iota(jnp.int32, (count, tokens), 0)
        table = jnp.zeros((count, tokens), F32)
        for e in range(experts):
            slope = jnp.sum(jnp.where(masks[e], slopes[e][0, :, :1], 0.0), axis=0, keepdims=True)
            table = jnp.where(row == first[0] + e, slope, table)
        high = table.astype(BF16).astype(F32)
        for side, value in enumerate((high, table - high)):
            cols = slice(side * tokens, (side + 1) * tokens)
            for other, start in zip(added, starts, strict=True):
                if start + other.shape[0] > tokens:
                    value = value + other[tokens - start :, cols].astype(F32)
            last[tokens - cut :, cols] = value.astype(BF16)
        last[tokens - cut :, 2 * tokens :] = jnp.zeros((count, width - 2 * tokens), BF16)


def combine(rows, at, places, slopes, first, added, cut, extra, after=()):
    experts = len(rows)
    _, slot_count, width = rows[0].shape
    _, count, tokens = places.shape
    block = lambda n: pl.BlockSpec((1, slot_count, n), lambda *_: (at, 0, 0))
    ins = [(r, block(width)) for r in rows]
    ins.append((places, pl.BlockSpec((1, count, tokens), lambda *_: (at, 0, 0))))
    if slopes is not None:
        ins += [(s, block(128)) for s in slopes]
    ins += [(a, whole(a)) for a, _ in added]
    long = tokens + (extra if slopes is not None else 0)
    outs = [shaped((cut, width), BF16)] if cut else []
    outs.append(shaped((long - cut, width), BF16))
    starts = tuple(start for _, start in added)
    return kernel_call(
        1.2,
        functools.partial(combine_body, experts, slopes is not None, starts, cut),
        (1,),
        ins,
        [(s, whole(s)) for s in outs],
        scalars=(first,),
        after=after,
    )


def expert_body(index, blocks, joint, n_dp, order, expert_ref, me_ref, *refs):
    refs = list(refs)
    u_hbm = [refs.pop(0) for _ in range(blocks)]
    dz_hbm = [refs.pop(0) for _ in range(blocks)]
    gate_hbm = [refs.pop(0) for _ in range(blocks)]
    wg_hbm, wu_hbm, wd_hbm, yg_hbm, du_hbm, slope_ref = refs[:6]
    grads_hbm, refs = (refs[6:7], refs[7:]) if joint else (refs[6:8], refs[8:])
    (
        u_ref, dz_ref, gate_ref, wg, wu, wd, ha, side_gate, side_up, dy, dga, dua, yg, du, stage,
        row_sems, sems,
    ) = refs
    _, slot_count, width = u_ref.shape
    rows = blocks * slot_count
    ff = ha.shape[1]
    expert, me = expert_ref[0], me_ref[0]

    def loads(sources, target, at):
        return [
            pltpu.make_async_copy(s.at[index], target.at[b], row_sems.at[at, b])
            for b, s in enumerate(sources)
        ]

    u_loads, dz_loads, gate_loads = (
        loads(u_hbm, u_ref, 0), loads(dz_hbm, dz_ref, 1), loads(gate_hbm, gate_ref, 2)
    )
    w_loads = [
        pltpu.make_async_copy(source.at[expert], target, sems.at[at])
        for at, (source, target) in enumerate(((wg_hbm, wg), (wu_hbm, wu), (wd_hbm, wd)))
    ]
    first, second = u_loads + w_loads[:2], w_loads[2:] + gate_loads + dz_loads
    for load in first + second:
        load.start()
    for load in first:
        load.wait()
    tile = 256

    @pl.loop(0, ff // tile)
    def _(t):
        cols = column(t, tile)
        u = u_ref[...].reshape(rows, width)
        a = dot(u, wg[:, cols])
        b = dot(u, wu[:, cols])
        cdf = 0.5 * (1.0 + lax.erf(a * 0.7071067811865476))
        pdf = jnp.exp(-0.5 * a * a) * 0.3989422804014327
        glu = a * cdf
        ha[:, cols] = (glu * b).astype(BF16)
        side_gate[:, cols] = b * (cdf + a * pdf)
        side_up[:, cols] = glu

    for load in second:
        load.wait()
    slope_ref[...] = jnp.zeros_like(slope_ref)

    @pl.loop(0, width // tile)
    def _(t):
        cols = column(t, tile)
        gate = gate_ref[...].reshape(rows, 128)[:, :1]
        y = dot(ha[...], wd[:, cols]).astype(BF16).astype(F32)
        dz = dz_ref[:, :, cols].reshape(rows, tile).astype(F32)
        part = jnp.sum(dz * y, axis=1, keepdims=True)
        slope_ref[...] += jnp.broadcast_to(part, (rows, 128)).reshape(blocks, slot_count, 128)
        yg[:, :, cols] = (gate * y).astype(BF16).reshape(blocks, slot_count, tile)
        dy[:, cols] = (gate * dz).astype(BF16)

    out_yg = pltpu.make_async_copy(yg, yg_hbm, sems.at[3])
    out_yg.start()

    @pl.loop(0, ff // tile)
    def _(t):
        cols = column(t, tile)
        dha = dot_nt(dy[...], wd[cols, :])
        dga[:, cols] = (dha * side_gate[:, cols]).astype(BF16)
        dua[:, cols] = (dha * side_up[:, cols]).astype(BF16)

    wide = 384
    deep = width // n_dp
    flat = ff // n_dp

    def spot(block):
        if not joint:
            return place_of(block ^ me, order, n_dp)
        rank = block % TEAM_BIT + (block // (2 * TEAM_BIT)) * TEAM_BIT
        return 2 * rank + (block // TEAM_BIT + me // TEAM_BIT) % 2

    @pl.loop(0, width // wide)
    def _(t):
        cols = column(t, wide)
        ut = u_ref[:, :, cols].reshape(rows, wide)
        for which, grad in ((0, dga), (1, dua)):
            d_weight = dot_tn(ut, grad[...]).astype(BF16)
            for i in range(wide // deep):
                at = spot(t * (wide // deep) + i)
                stage[which, at] = d_weight[i * deep : (i + 1) * deep]

    @pl.loop(0, ff // wide)
    def _(t):
        cols = column(t, wide)
        d_weight = dot_tn(ha[:, cols], dy[...]).astype(BF16)
        for i in range(wide // flat):
            at = spot(t * (wide // flat) + i)
            part = d_weight[i * flat : (i + 1) * flat]
            stage[2, at, :flat] = part[:, :ff]
            stage[2, at, flat:] = part[:, ff:]

    if joint:
        out_grads = [
            pltpu.make_async_copy(stage.at[m], grads_hbm[0].at[:, m], sems.at[5 + m])
            for m in range(3)
        ]
    else:
        out_grads = [
            pltpu.make_async_copy(
                stage.at[:, pl.ds(side * (n_dp // 2), n_dp // 2)], grads_hbm[side], sems.at[5 + side]
            )
            for side in range(2)
        ]
    for copy in out_grads:
        copy.start()

    @pl.loop(0, width // tile)
    def _(t):
        cols = column(t, tile)
        back = dot_nt(dga[...], wg[cols, :]) + dot_nt(dua[...], wu[cols, :])
        du[:, :, cols] = back.astype(BF16).reshape(blocks, slot_count, tile)

    out_du = pltpu.make_async_copy(du, du_hbm, sems.at[4])
    out_du.start()
    out_yg.wait()
    for copy in out_grads:
        copy.wait()
    out_du.wait()


def place_of(index, order, count):
    place = 0
    for at, bit in enumerate(order):
        place = place + ((index // bit) % 2) * (count >> (at + 1))
    return place


def expert_pass(index, expert, me, u, dz, gates, wg, wu, wd, n_dp, order, joint, after=()):
    blocks = len(u)
    _, slot_count, width = u[0].shape
    ff = wg.shape[2]
    rows = blocks * slot_count
    deep = width // n_dp
    if joint:
        packed = [shaped((n_dp, 3, deep, ff), BF16)]
    else:
        packed = [shaped((3, n_dp // 2, deep, ff), BF16)] * 2
    row_shape = shaped((blocks, slot_count, width), BF16)
    slope_shape = shaped((blocks, slot_count, 128), F32)
    return kernel_call(
        26.5,
        functools.partial(expert_body, index, blocks, joint, n_dp, order),
        (1,),
        [(a, ANYWHERE) for a in list(u) + list(dz) + list(gates) + [wg, wu, wd]],
        [
            (row_shape, ANYWHERE),
            (row_shape, ANYWHERE),
            (slope_shape, whole(slope_shape)),
        ]
        + [(p, ANYWHERE) for p in packed],
        scalars=(expert, me),
        scratch=[
            pltpu.VMEM((blocks, slot_count, width), BF16),
            pltpu.VMEM((blocks, slot_count, width), BF16),
            pltpu.VMEM((blocks, slot_count, 128), F32),
            pltpu.VMEM((width, ff), BF16),
            pltpu.VMEM((width, ff), BF16),
            pltpu.VMEM((ff, width), BF16),
            pltpu.VMEM((rows, ff), BF16),
            pltpu.VMEM((rows, ff), F32),
            pltpu.VMEM((rows, ff), F32),
            pltpu.VMEM((rows, width), BF16),
            pltpu.VMEM((rows, ff), BF16),
            pltpu.VMEM((rows, ff), BF16),
            pltpu.VMEM((blocks, slot_count, width), BF16),
            pltpu.VMEM((blocks, slot_count, width), BF16),
            pltpu.VMEM((3, n_dp, width // n_dp, ff), BF16),
            pltpu.SemaphoreType.DMA((3, blocks)),
            pltpu.SemaphoreType.DMA((8,)),
        ],
        after=after,
    )


def add_split_body(a_ref, b_ref, c_ref, d_ref, keep_ref, send_ref):
    keep_ref[...] = (a_ref[...].astype(F32) + b_ref[...].astype(F32)).astype(keep_ref.dtype)
    send_ref[...] = (c_ref[...].astype(F32) + d_ref[...].astype(F32)).astype(BF16)


def add_split(held, arrived, axis, last=False, after=()):
    half = held.shape[axis] // 2
    shape = list(held.shape)
    shape[axis] = half
    block = [1 if at == axis else size for at, size in enumerate(held.shape)]
    spot = lambda shift: lambda i: tuple(i + shift if at == axis else 0 for at in range(len(block)))
    low, high = pl.BlockSpec(tuple(block), spot(0)), pl.BlockSpec(tuple(block), spot(half))
    return kernel_call(
        4.5,
        add_split_body,
        (half,),
        [(held, low), (arrived, low), (held, high), (arrived, high)],
        [(shaped(shape, F32 if last else BF16), low), (shaped(shape, BF16), low)],
        after=after,
    )


def settle_body(slots, own_ref, other_ref, *refs):
    outs = refs[-3:]

    def write(part):
        for m, out in enumerate(outs):
            value = part[m].astype(F32)
            if m == 2:
                flat = out.shape[1]
                value = jnp.concatenate([value[:flat], value[flat:]], axis=1)
            out[0] = value

    @pl.when(pl.program_id(0) == 0)
    def _():
        write(own_ref)

    @pl.when(pl.program_id(0) == 1)
    def _():
        write(other_ref)


def settle(own, other, slots, local_count, totals, after=()):
    _, deep, ff = own.shape
    shapes = [
        shaped((local_count, deep, ff), F32),
        shaped((local_count, deep, ff), F32),
        shaped((local_count, deep // 2, 2 * ff), F32),
    ]
    out_spec = lambda s: pl.BlockSpec((1, *s.shape[1:]), lambda i, slots: (slots[i], 0, 0))
    ins = [(own, whole(own)), (other, whole(other))] + [(t, ANYWHERE) for t in totals]
    return kernel_call(
        4.3,
        settle_body,
        (2,),
        ins,
        [(s, out_spec(s)) for s in shapes],
        scalars=(slots,),
        aliases={3 + i: i for i in range(len(totals))},
        after=after,
    )


def weight_grad_body(half, wide, order, n_dp, places, left_ref, right_ref, *refs):
    keep_ref, send_ref = refs[-2:]
    q = pl.program_id(0)
    width = left_ref.shape[1]
    deep = width // n_dp

    def fill(out_ref):
        right = right_ref[...].reshape(left_ref.shape[0], right_ref.shape[-1])
        for t in range(width // wide):
            part = dot_tn(left_ref[:, t * wide : (t + 1) * wide], right).astype(BF16)
            for i in range(wide // deep):
                at = place_of((t * (wide // deep) + i) ^ places[2 * half], order, n_dp)
                out_ref[0, at] = part[i * deep : (i + 1) * deep]

    @pl.when(q < half)
    def _():
        fill(keep_ref)

    @pl.when(q >= half)
    def _():
        fill(send_ref)


def weight_grad(left, right, places, n_dp, members, order, total_cols, start, buffers, after=()):
    rows, width = left.shape
    cols = right.shape[1] // members
    half = members // 2
    deep = width // n_dp
    if cols % 128 == 0:
        right_in = (right, pl.BlockSpec((rows, cols), lambda q, places: (0, places[q])))
    else:
        right = jnp.swapaxes(right.reshape(rows, members, cols), 0, 1)
        right_in = (right, pl.BlockSpec((1, rows, cols), lambda q, places: (places[q], 0, 0)))
        total_cols, start, buffers = cols, 0, []
    block = (1, n_dp, deep, cols)
    shape = shaped((half, n_dp, deep, total_cols), BF16)
    at = start // cols
    ins = [(left, whole(left)), right_in] + [(b, ANYWHERE) for b in buffers]
    return kernel_call(
        7,
        functools.partial(weight_grad_body, half, 384, order, n_dp),
        (members,),
        ins,
        [
            (shape, pl.BlockSpec(block, lambda q, places: (jnp.minimum(q, half - 1), 0, 0, at))),
            (shape, pl.BlockSpec(block, lambda q, places: (jnp.maximum(q - half, 0), 0, 0, at))),
        ],
        scalars=(places,),
        aliases={3 + i: i for i in range(len(buffers))},
        after=after,
    )


def reduce_grad(keep, send, steps):
    outer = keep.shape[0].bit_length()
    arrived = swap(send, *steps[0])
    for at in range(1, len(steps)):
        if at == outer:
            keep, arrived = keep[0], arrived[0]
        keep, send = add_split(keep, arrived, 0)
        arrived = swap(send, *steps[at])
    return keep[0].astype(F32) + arrived[0].astype(F32)


def norm_back(inputs, gain, upstream):
    scale = rms_of(inputs)
    weighted = gain * upstream
    middle = jnp.mean(inputs * weighted, axis=1, keepdims=True)
    grad = scale * weighted - inputs * (scale * scale * scale) * middle
    return grad, jnp.sum(upstream * inputs * scale, axis=0, keepdims=True)


def back_body(terms, *refs):
    refs = list(refs)
    parts = [refs.pop(0) for _ in range(terms)]
    (
        residual_ref, cot_ref, gain, gates_ref, router, message_ref, wo,
        d_res_ref, d_branch_ref, d_mix_ref, small_ref, total,
    ) = refs
    rows = residual_ref.shape[0]
    experts = gates_ref.shape[0]

    @pl.when(pl.program_id(0) == 0)
    def _():
        value = parts[0][...].astype(F32)
        for part in parts[1:]:
            value = value + part[...].astype(F32)
        total[...] = value
        slopes = total[rows:, :rows] + total[rows:, rows : 2 * rows]
        gates = gates_ref[...]
        mean = jnp.sum(gates * slopes, axis=0, keepdims=True)
        d_logits = (gates * (slopes - mean)).astype(BF16)
        d_routed = total[:rows, :] + dot_tn(d_logits, router[...])
        grad, d_gain = norm_back(residual_ref[...], gain[...], d_routed)
        d_residual = cot_ref[...].astype(F32) + grad
        d_res_ref[...] = d_residual
        d_branch_ref[...] = d_residual.astype(BF16)
        small_ref[:experts, :] = dot(d_logits, message_ref[:rows, :])
        small_ref[experts:, :] = jnp.broadcast_to(d_gain, (8, d_gain.shape[1]))

    d_mix_ref[...] = dot_nt(d_branch_ref[...], wo[...]).astype(BF16)


def back_through_branch(terms, residual, cot, gain, gates_t, router_t, message, wo, after=()):
    rows, width = residual.shape
    experts = gates_t.shape[0]
    tile = 256
    outs = (
        shaped((rows, width), F32),
        shaped((rows, width), BF16),
        shaped((experts + 8, width), F32),
    )
    d_mix = shaped((rows, wo.shape[0]), BF16)
    d_residual, d_branch, d_mix, small = kernel_call(
        13.8,
        functools.partial(back_body, len(terms)),
        (wo.shape[0] // tile,),
        [(a, whole(a)) for a in terms]
        + [(a, whole(a)) for a in (residual, cot, gain, gates_t, router_t, message)]
        + [(wo, pl.BlockSpec((tile, width), lambda i: (i, 0)))],
        [(s, whole(s)) for s in outs[:2]]
        + [(d_mix, pl.BlockSpec((rows, tile), lambda i: (0, i))), (outs[2], whole(outs[2]))],
        scratch=[pltpu.VMEM((rows + experts, width), F32)],
        after=after,
    )
    return d_residual, d_branch, d_mix, small


def output_body(residual_ref, *refs):
    total = residual_ref[...]
    for part in refs[:-1]:
        total = total + part[...].astype(F32)
    refs[-1][...] = total.astype(BF16)


def layer_output(residual, terms):
    out = shaped(residual.shape, BF16)
    return kernel_call(
        5,
        output_body, (1,), [(a, whole(a)) for a in [residual, *terms]], [(out, whole(out))]
    )[0]


def key_value_back_body(members, held_ref, arrived_ref, cos_ref, sin_ref, own_ref, joined_ref):
    total = held_ref[...].astype(F32) + arrived_ref[...].astype(F32)
    kd = total.shape[1] // 2
    keys = [
        turn(total[:, h * HD : (h + 1) * HD], cos_ref[...], -sin_ref[...])
        for h in range(kd // HD)
    ]
    keys, values = jnp.concatenate(keys, axis=1), total[:, kd:]
    own_ref[:, :kd] = keys.astype(BF16)
    own_ref[:, kd:] = values.astype(BF16)
    part = kd // members
    joined = []
    for c in range(members):
        cols = slice(c * part, (c + 1) * part)
        joined += [keys[:, cols], values[:, cols]]
    joined_ref[...] = jnp.concatenate(joined, axis=1).astype(BF16)


def key_value_back(held, arrived, cos_wide, sin_wide, members):
    return kernel_call(
        2.6,
        functools.partial(key_value_back_body, members),
        (1,),
        [(a, whole(a)) for a in (held, arrived, cos_wide, sin_wide)],
        [(s, whole(s)) for s in [shaped(held.shape, BF16)] * 2],
    )


def finish_body(steps, dq_ref, dkv_ref, wq, wk, wv, x_ref, d_res_ref, gain, small_ref,
                d_hidden_ref, sums_ref, total):
    i = pl.program_id(0)
    kd = wk.shape[1]
    part = dot_nt(dq_ref[...], wq[...])
    part = part + dot_nt(dkv_ref[:, :kd], wk[...]) + dot_nt(dkv_ref[:, kd:], wv[...])
    total[:, column(i, part.shape[1])] = part

    @pl.when(i == steps - 1)
    def _():
        x = x_ref[...].astype(F32)
        grad, d_gain = norm_back(x, gain[...], total[...])
        d_hidden_ref[...] = d_res_ref[...] + grad
        lead = small_ref.shape[0] - 8
        sums_ref[:lead, :] = small_ref[:lead, :]
        row = lax.broadcasted_iota(jnp.int32, (8, 1), 0)
        sums_ref[lead:, :] = jnp.where(row == 1, d_gain, small_ref[lead:, :])


def finish(dq, dkv, wq, wk, wv, x, d_residual, gain, small, after=()):
    rows, width = x.shape
    tile = 256
    by_rows = lambda w: (w, pl.BlockSpec((tile, w.shape[1]), lambda i: (i, 0)))
    outs = (shaped((rows, width), F32), shaped(small.shape, F32))
    return kernel_call(
        13,
        functools.partial(finish_body, width // tile),
        (width // tile,),
        [(dq, whole(dq)), (dkv, whole(dkv)), by_rows(wq), by_rows(wk), by_rows(wv)]
        + [(a, whole(a)) for a in (x, d_residual, gain, small)],
        [(s, whole(s)) for s in outs],
        scratch=[pltpu.VMEM((rows, width), F32)],
        after=after,
    )


def per_device(
    hidden_in, cotangent, norm_attn, w_query, w_key, w_value, w_out, norm_ffn, w_router,
    w_gate, w_up, w_down, expert_ids, priority, prefix,
):
    group_count, span_len, width = hidden_in.shape
    row_count = group_count * span_len
    q_width, kv_width = w_query.shape[1], w_key.shape[1]
    kv_heads = kv_width // HD
    members, n_dp = lax.axis_size("expert"), lax.axis_size("dp")
    expert_count = w_router.shape[1]
    local_count = w_gate.shape[0]
    team_count = local_count // 2
    top_count = expert_ids.shape[3]
    slot_count = row_count * top_count * 5 // (expert_count * 4)
    capacity = 9 * row_count * members * top_count // (8 * expert_count)
    e_index, d_index = lax.axis_index("expert"), lax.axis_index("dp")
    parity = (d_index // TEAM_BIT) % 2
    first_local = parity * team_count
    first_expert = (e_index * local_count + first_local).reshape(1).astype(jnp.int32)
    e_steps = [("expert", bit) for bit in bits_of(members)]
    team = ("dp", TEAM_BIT)
    gain_one, gain_two = norm_attn.reshape(1, width), norm_ffn.reshape(1, width)
    router_t = w_router.T

    expert_range = jnp.arange(expert_count, dtype=jnp.int32)
    routes_t = expert_ids.reshape(row_count, top_count).T
    hit_t = jnp.any(routes_t[:, None, :] == expert_range[None, :, None], axis=0)
    tables = jnp.concatenate([routes_t, priority.reshape(1, row_count)], axis=0)[None]
    for axis_name, bit in [team] + e_steps:
        tables = jnp.concatenate([tables, swap(tables, axis_name, bit)], axis=0)

    offset = e_index * span_len
    positions = (offset + jnp.arange(span_len, dtype=jnp.int32)).astype(F32)
    frequency = ROPE_BASE ** (-(jnp.arange(HD // 2, dtype=F32) * 2.0 / HD))
    angles = positions[:, None] * frequency[None, :]
    cos_table, sin_table = jnp.cos(angles), jnp.sin(angles)
    cos_span = jnp.concatenate([cos_table, cos_table], axis=1)
    sin_span = jnp.concatenate([-sin_table, sin_table], axis=1)
    cos_wide, sin_wide = jnp.tile(cos_span, (group_count, 1)), jnp.tile(sin_span, (group_count, 1))
    x = hidden_in.reshape(row_count, width)
    cot = cotangent.reshape(row_count, width)
    normed, kv_own, queries, cot_later = project_inputs(
        x, gain_one, w_query, w_key, w_value, cos_wide, sin_wide, cot
    )
    kv = gather_pieces(kv_own.reshape(group_count, span_len, 2 * kv_width), e_steps)
    q = queries([tables])
    source = e_index ^ sum(
        ((jnp.arange(members) >> at) & 1) * bit for at, (_, bit) in enumerate(e_steps)
    )
    source = jnp.concatenate([source, offset.reshape(1)]).astype(jnp.int32)

    cut = row_count // 2

    far, near = ("expert", 2), ("expert", 1)

    def corner_of(over_z, over_y):
        return swap(over_z[:cut], *far), swap(over_y[cut:], *team)

    def over_near(piece):
        return tuple(swap(s, *near) for s in piece)

    def scatter_team(make):
        if members != 4:
            pieces = [make(at, [], 0)[0] for at in range(2 * members)]
            return [scatter_pieces(pieces, [team] + e_steps)]
        sent = {at: swap(make(at + 4, [], 0)[0], "expert", 1) for at in (3, 1, 2, 0)}
        low, high = make(3, [(sent[3], 0)], cut)
        from_y, from_z = swap(low, *far), swap(high, *team)
        own = make(0, [(sent[0], 0)], 0)[0]
        over_z = swap(make(1, [(sent[1], 0), (from_y, 0)], 0)[0], *team)
        over_y = swap(make(2, [(sent[2], 0), (from_z, cut)], 0)[0], *far)
        return [own, over_z, over_y]

    split = members == 4
    if split:
        over_z, over_y = swap(cot, *team), swap(cot_later, *far)
        cots = [(cot,), (over_z,), (over_y,)]
    else:
        cots = [(piece,) for piece in gather_pieces(cot, [team] + e_steps)]

    q = q.reshape(group_count, span_len, q_width)
    mix, lse = attend(q, kv, prefix, source)
    mix = mix.reshape(row_count, q_width)
    residual, message, gates_t = branch(x, mix, w_out, gain_two, router_t, hit_t.astype(F32))

    u_rows, gate_rows = {}, {}

    def send_rows(at, piece, after):
        u_rows[at], gate_rows[at] = dispatch(
            piece, at, places, first_expert, slot_count, True, after
        )

    if split:
        over_z, over_y = swap(message, *team), swap(message, *far)
    else:
        pieces = gather_pieces(message, [team] + e_steps)
    places = find_places(tables, first_expert, team_count, capacity, [message])
    if split:
        cots.append(corner_of(hold(cots[1][0], [places]), hold(cots[2][0], [places])))
        cots += [over_near(piece) for piece in cots]
    dz_rows = []
    for at, piece in enumerate(cots):
        dz_rows.append(
            dispatch(piece, at, places, first_expert, slot_count, False, dz_rows[-1:])[0]
        )
    if split:
        send_rows(0, (message,), dz_rows[-1:])
        send_rows(4, over_near((message,)), [u_rows[0]])
        over_z, over_y = hold(over_z, [u_rows[4]]), hold(over_y, [u_rows[4]])
        corner = corner_of(over_z, over_y)
        for at, piece in ((1, (over_z,)), (2, (over_y,))):
            send_rows(at, piece, [])
            send_rows(4 + at, over_near(piece), [])
        last = [u_rows[5], u_rows[6]]
        corner = tuple(hold(part, last) for part in corner)
        send_rows(3, corner, [])
        send_rows(7, over_near(corner), [])
    else:
        for at, piece in enumerate(pieces):
            send_rows(at, (piece,), dz_rows[-1:])
    u_rows, gate_rows = ([rows[at] for at in range(2 * members)] for rows in (u_rows, gate_rows))
    d_order = [bit for bit in reversed(bits_of(n_dp)) if bit != TEAM_BIT] + [TEAM_BIT]
    me = d_index.reshape(1).astype(jnp.int32)
    outs, backs, slopes, chains = [], [], [], []
    chunk = 8
    for e in range(team_count):
        expert = (first_local + e).reshape(1).astype(jnp.int32)
        parts = []
        for start in range(0, len(u_rows), chunk):
            span = slice(start, start + chunk)
            parts.append(
                expert_pass(
                    e, expert, me, u_rows[span], dz_rows[span], gate_rows[span],
                    w_gate, w_up, w_down, n_dp, d_order, False, slopes[-1:],
                )
            )
        if len(parts) == 1:
            out, back, slope, *grads = parts[0]
        else:
            out, back, slope = (jnp.concatenate([p[i] for p in parts], axis=0) for i in range(3))
            grads = [
                sum(p[i].astype(F32) for p in parts).astype(BF16) for i in range(3, len(parts[0]))
            ]
        outs.append(out)
        backs.append(back)
        slopes.append(slope)
        chains.append((grads[0], swap(grads[1], "dp", d_order[0])))
    done = [0] * team_count
    ppermuted = team_count

    def advance(e, after):
        if e >= ppermuted or done[e] >= len(d_order) - 1:
            return list(after)
        done[e] += 1
        step = done[e]
        keep, arrived = chains[e]
        keep, send = add_split(keep, arrived, 1, step == len(d_order) - 1, after)
        if step == len(d_order) - 1:
            chains[e] = (keep[:, 0], swap(send[:, 0], "dp", d_order[step]))
        else:
            chains[e] = (keep, swap(send, "dp", d_order[step]))
        return [keep]

    extra = expert_count

    first_marks = advance(0, slopes[-1:])

    def make_back(at, added, cut_at):
        return combine(
            backs, at, places, slopes, first_expert, added, cut_at, extra,
            first_marks if at >= members else (),
        )

    back_terms = scatter_team(make_back)
    marks = advance(0, advance(1, back_terms[:1]))
    d_residual, d_branch, d_mix, small = back_through_branch(
        back_terms, residual, cot, gain_two, gates_t, router_t, message, w_out, marks
    )

    member_order = [bit for _, bit in reversed(e_steps)]
    member_places = [
        sum(((q >> (len(member_order) - 1 - at)) & 1) * bit for at, bit in enumerate(member_order))
        for q in range(members)
    ]
    grad_places = jnp.concatenate(
        [e_index ^ jnp.array(member_places, jnp.int32), d_index.reshape(1)]
    ).astype(jnp.int32)
    w_order = list(reversed(bits_of(n_dp)))
    w_steps = [("expert", bit) for bit in member_order] + [("dp", bit) for bit in w_order]
    q_part, kv_part = q_width // members, kv_width // members
    w_parts = []

    def add_weight(left, right, start, after):
        buffers = w_parts[-1] if w_parts else []
        w_parts.append(
            weight_grad(
                left, right, grad_places, n_dp, members, w_order,
                2 * q_part + 2 * kv_part, start, buffers, after,
            )
        )

    dq, d_kv = attend_back(
        q, d_mix.reshape(group_count, span_len, q_width), lse, kv, prefix, source,
        cos_span, sin_span,
    )
    dq = dq.reshape(row_count, q_width)
    add_weight(mix, d_branch, 0, [dq])
    add_weight(normed, dq, q_part, [])
    last_step = e_steps[0]
    halves = [scatter_pieces(d_kv[at::2], e_steps[1:]) for at in range(2)]
    held, sent = (h.reshape(row_count, 2 * kv_width) for h in halves)
    arrived = hold(swap(sent, *last_step), w_parts[-1][:1])
    d_kv_own, joined = key_value_back(held, arrived, cos_wide, sin_wide, members)
    add_weight(normed, joined, 2 * q_part, [])
    d_hidden, sums = finish(
        dq, d_kv_own, w_query, w_key, w_value, x, d_residual, gain_one, small, w_parts[-1][:1]
    )
    if q_part % 128 == 0 and kv_part % 64 == 0:
        w_keep, w_send = w_parts[-1]
    else:
        w_keep, w_send = (jnp.concatenate([p[i] for p in w_parts], axis=3) for i in range(2))
    marks = advance(1, advance(2, [d_hidden]))

    def make_out(at, added, cut_at):
        return combine(outs, at, places, None, first_expert, added, cut_at, 0, marks)

    output = layer_output(residual, scatter_team(make_out))
    sums = all_sum(sums, ("expert", "dp"))
    w_total = reduce_grad(w_keep, w_send, w_steps)

    totals = []
    for e in range(team_count):
        while e < ppermuted and done[e] < len(d_order) - 1:
            advance(e, [output])
        own, other = chains[e]
        slots = jnp.stack([first_local + e, team_count - first_local + e]).astype(jnp.int32)
        totals = settle(own, other, slots, local_count, totals, [output])
    grad_gate, grad_up, grad_down = totals
    return (
        output.reshape(group_count, span_len, width),
        d_hidden.reshape(group_count, span_len, width),
        sums[expert_count + 1],
        w_total[:, q_part : 2 * q_part],
        w_total[:, 2 * q_part : 2 * q_part + kv_part],
        w_total[:, 2 * q_part + kv_part :],
        w_total[:, :q_part],
        sums[expert_count],
        sums[:expert_count].T,
        grad_gate,
        grad_up,
        grad_down,
    )


def solution(mesh):
    in_specs = (
        P("dp", "expert", None),
        P("dp", "expert", None),
        P(),
        P(),
        P(),
        P(),
        P(),
        P(),
        P(),
        P("expert", None, None),
        P("expert", None, None),
        P("expert", None, None),
        P(("dp", "expert"), None, None, None),
        P(("dp", "expert"), None, None),
        P("dp"),
    )
    out_specs = (
        P("dp", "expert", None),
        P("dp", "expert", None),
        P(),
        P("dp", "expert"),
        P("dp", "expert"),
        P("dp", "expert"),
        P("dp", "expert"),
        P(),
        P(),
        P("expert", "dp", None),
        P("expert", "dp", None),
        P("expert", "dp", None),
    )
    return jax.shard_map(
        per_device, mesh=mesh, in_specs=in_specs, out_specs=out_specs, check_vma=False
    )
```

time: 2420 us -> 999 us (0.41)
  waiting for transfers between devices: 1500 us -> 483 us
  Pallas kernels: 0 us -> 417 us
  matrix products: 288 us -> 0 us
  blocking collectives: 238 us -> 0 us
  local copies, waits for them, and re-layouts: 195 us -> 36.1 us
  other arithmetic: 164 us -> 10.8 us
  starting transfers between devices: 12.8 us -> 40.4 us
    reduce_scatter x9 -> x0, waiting for transfers between devices: 1100 us -> none  [the longest x1 315 us: per_device(): lax.psum_scatter(grad_down.astype(jnp.bfloat16), 'dp', scatter_dimension=...]
    ppermute x0 -> x65, waiting for transfers between devices: none -> 483 us  [swap(): return lax.ppermute(values, axis_name, [(i, i ^ bit) for i in range(count)])]
    pallas_call x0 -> x72, Pallas kernels: none -> 417 us  [kernel_call(): pl.pallas_call(run, grid_spec=grid_spec, out_shape=[shape for shape, _ in...]
    dot_general x31 -> x0, matrix products: 288 us -> none  [the longest x1 30.7 us: per_device(): jnp.einsum('aecd,edf->aecf', arrived, w_up, preferred_element_type=jnp.fl...]
    all_to_all x2 -> x0, blocking collectives: 186 us -> none  [the longest x1 94.9 us: per_device(): lax.all_to_all(grad_send.reshape(members, local_count, slot_count, model_...]
    all_to_all x2 -> x0, waiting for transfers between devices: 153 us -> none  [the longest x1 87.4 us: per_device(): lax.all_to_all(d_arrived, 'expert', split_axis=0, concat_axis=0, tiled=True)]
    psum x1 -> x0, waiting for transfers between devices: 124 us -> none  [per_device(): lax.psum((grad_router, grad_norm_attn, grad_norm_ffn), ('dp', 'expert'))]
    unnamed x20 -> x0, waiting for transfers between devices: 117 us -> none
  transfers between devices with their start and end apart: 18 -> 65, of which waited for: 13 -> 22; matrix products, arithmetic and copies ran while one was open for 10% -> 2% of each run, Pallas kernels for 0% -> 38%
where the time goes in v1:
time: 999 us; the launch traced here: 989 us
  waiting for transfers between devices  483 us (48%)
  Pallas kernels  417 us (42%)
  starting transfers between devices  40.4 us (4%)
  local copies, waits for them, and re-layouts  36.1 us (4%)
  other arithmetic  10.8 us (1%)
    ppermute x65, waiting for transfers between devices, swap(): return lax.ppermute(values, axis_name, [(i, i ^ bit) for i in range(count)])  483 us
    pallas_call x72, Pallas kernels, kernel_call(): pl.pallas_call(run, grid_spec=grid_spec, out_shape=[shape for shape, _ in...  417 us
    ppermute x65, starting transfers between devices, swap(): return lax.ppermute(values, axis_name, [(i, i ^ bit) for i in range(count)])  40.4 us
    unnamed x76, local copies, waits for them, and re-layouts  24.1 us
  transfers between devices with their start and end apart: 65, of which 22 were waited for; matrix products, arithmetic and copies ran while one was open for 2% of the time, Pallas kernels for 38%

profile of v1, /device:TPU:0, one launch (start us, length us, event | category | flops | bytes accessed | tf_op | source)
XLA Modules:
  0.0 988.6 jit_solution(17702550192922529281)
XLA Ops:
  6.7 4.2 shard_map.247
  16.3 35.0 %collective-permute-done = s32[1,5,512]{2,1,0:T(8,128)S(1)} collective-permute-done((s32[1,5,512]{2,1,0:T(8,128)S(1)}, s32[1,5,512]{2,1,0:T(8,128)S(1)}, u32[]{:S(2)}, u32[]{:S(2)}) %collective-permute-start) | collective-permute-done | bytes 10272 | tf_op jit(solution)/shard_map/ppermute | solution.py:40
  58.3 7.7 shard_map.248
  69.5 15.7 %shard_map.249 = (bf16[2,256,1536]{2,1,0:T(8,128)(2,1)}, f32[2,256,12]{2,1,0:T(8,128)}) custom-call(s32[2]{0:T(128)} %refs_0_.3, s32[5]{0:T(128)} %pad_add_fusion.3.refs_1_, bf16[2,256,1536]{2,1,0:T(8,128)(2,1)} %bitcast.78, bf16[2,256,512]{2,1,0:T(8,128)(2,1)} %bitcast.71, bf16[2,256,512]{2,1,0:T(8,128)(2,1)} %collective-permute-done.3.refs_4_.refs_8_, ...), custom_call_target="tpu_custom_call" | custom-call | flops 15699999744 | bytes 51810000 | tf_op jit(solution)/shard_map/pallas_call | solution.py:91
  85.2 8.9 collective-permute-done.9.refs_0_.refs_1_
  94.6 10.6 %shard_map.250 = (f32[512,1536]{1,0:T(8,128)}, bf16[544,1536]{1,0:T(8,128)(2,1)}, f32[32,512]{1,0:T(8,128)}) custom-call(bf16[512,1536]{1,0:T(8,128)(2,1)} %bitcast.65, bf16[512,1536]{1,0:T(8,128)(2,1)} %bitcast.76, bf16[1536,1536]{1,0:T(8,128)(2,1)} %refs_9_.1, f32[1,1536]{1,0:T(1,128)} %reshape.123.refs_3_.refs_5_, bf16[32,1536]{1,0:T(8,128)(2,1)} %bitcast.73, ...), custom_call_target="tpu_custom_call" | custom-call | flops 10000000000 | bytes 33000000 | tf_op jit(solution)/shard_map/pallas_call | solution.py:91
  105.2 7.6 shard_map.251.refs_1_.refs_2_.refs_3_.refs_4_.refs_5_
  128.6 15.2 %collective-permute-done.10.refs_2_ = bf16[256,1536]{1,0:T(8,128)(2,1)} collective-permute-done((bf16[256,1536]{1,0:T(8,128)(2,1)S(1)}, bf16[256,1536]{1,0:T(8,128)(2,1)}, u32[]{:S(2)}, u32[]{:S(2)}) %collective-permute-start.10) | collective-permute-done | bytes 786464 | tf_op jit(solution)/shard_map/ppermute | solution.py:40
  169.1 12.0 %collective-permute-done.17.refs_0_ = bf16[544,1536]{1,0:T(8,128)(2,1)S(1)} collective-permute-done((bf16[544,1536]{1,0:T(8,128)(2,1)}, bf16[544,1536]{1,0:T(8,128)(2,1)S(1)}, u32[]{:S(2)}, u32[]{:S(2)}) %collective-permute-start.17) | collective-permute-done | bytes 1671200 | tf_op jit(solution)/shard_map/ppermute | solution.py:40
  193.8 12.9 %collective-permute-done.21.refs_0_ = bf16[288,1536]{1,0:T(8,128)(2,1)S(1)} collective-permute-done((bf16[288,1536]{1,0:T(8,128)(2,1)}, bf16[288,1536]{1,0:T(8,128)(2,1)S(1)}, u32[]{:S(2)}, u32[]{:S(2)}) %collective-permute-start.21) | collective-permute-done | bytes 884768 | tf_op jit(solution)/shard_map/ppermute | solution.py:40
  223.5 26.8 %shard_map.274 = (bf16[8,80,1536]{2,1,0:T(8,128)(2,1)}, bf16[8,80,1536]{2,1,0:T(8,128)(2,1)}, f32[8,80,128]{2,1,0:T(8,128)}, bf16[3,4,192,768]{3,2,1,0:T(8,128)(2,1)}, bf16[3,4,192,768]{3,2,1,0:T(8,128)(2,1)}) custom-call(s32[1]{0:T(128)} %bitcast.14.refs_0_, s32[1]{0:T(128)} %bitcast.15.refs_1_, bf16[4,80,1536]{2,1,0:T(8,128)(2,1)} %get-tuple-element.121.refs_4_.refs_2_, ...), custom_call_target="tpu_custom_call" | custom-call | flops 26499999744 | bytes 87450000 | tf_op jit(solution)/shard_map/pallas_call | solution.py:91
  251.8 26.3 %shard_map.275 = (bf16[8,80,1536]{2,1,0:T(8,128)(2,1)}, bf16[8,80,1536]{2,1,0:T(8,128)(2,1)}, f32[8,80,128]{2,1,0:T(8,128)}, bf16[3,4,192,768]{3,2,1,0:T(8,128)(2,1)}, bf16[3,4,192,768]{3,2,1,0:T(8,128)(2,1)}) custom-call(s32[1]{0:T(128)} %bitcast.16.refs_0_, s32[1]{0:T(128)} %bitcast.15.refs_1_, bf16[4,80,1536]{2,1,0:T(8,128)(2,1)} %get-tuple-element.121.refs_4_.refs_2_, ...), custom_call_target="tpu_custom_call" | custom-call | flops 26499999744 | bytes 87450000 | tf_op jit(solution)/shard_map/pallas_call | solution.py:91
  278.1 26.5 %shard_map.276 = (bf16[8,80,1536]{2,1,0:T(8,128)(2,1)}, bf16[8,80,1536]{2,1,0:T(8,128)(2,1)}, f32[8,80,128]{2,1,0:T(8,128)}, bf16[3,4,192,768]{3,2,1,0:T(8,128)(2,1)}, bf16[3,4,192,768]{3,2,1,0:T(8,128)(2,1)}) custom-call(s32[1]{0:T(128)} %bitcast.17.refs_0_, s32[1]{0:T(128)} %bitcast.15.refs_1_, bf16[4,80,1536]{2,1,0:T(8,128)(2,1)} %get-tuple-element.121.refs_4_.refs_2_, ...), custom_call_target="tpu_custom_call" | custom-call | flops 26499999744 | bytes 87450000 | tf_op jit(solution)/shard_map/pallas_call | solution.py:91
  304.6 26.6 %shard_map.277 = (bf16[8,80,1536]{2,1,0:T(8,128)(2,1)}, bf16[8,80,1536]{2,1,0:T(8,128)(2,1)}, f32[8,80,128]{2,1,0:T(8,128)}, bf16[3,4,192,768]{3,2,1,0:T(8,128)(2,1)}, bf16[3,4,192,768]{3,2,1,0:T(8,128)(2,1)}) custom-call(s32[1]{0:T(128)} %bitcast.18.refs_0_, s32[1]{0:T(128)} %bitcast.15.refs_1_, bf16[4,80,1536]{2,1,0:T(8,128)(2,1)} %get-tuple-element.121.refs_4_.refs_2_, ...), custom_call_target="tpu_custom_call" | custom-call | flops 26499999744 | bytes 87450000 | tf_op jit(solution)/shard_map/pallas_call | solution.py:91
  333.1 4.7 shard_map.278
  359.0 15.5 %collective-permute-done.31.refs_11_ = bf16[256,1536]{1,0:T(8,128)(2,1)S(1)} collective-permute-done((bf16[256,1536]{1,0:T(8,128)(2,1)}, bf16[256,1536]{1,0:T(8,128)(2,1)S(1)}, u32[]{:S(2)}, u32[]{:S(2)}) %collective-permute-start.31) | collective-permute-done | bytes 786464 | tf_op jit(solution)/shard_map/ppermute | solution.py:40
  377.1 4.4 shard_map.285
  382.7 4.5 shard_map.287
  390.9 4.2 shard_map.280.refs_4_.refs_0_
  395.1 25.7 %collective-permute-done.24.refs_1_.refs_3_ = bf16[3,4,192,768]{3,2,1,0:T(8,128)(2,1)} collective-permute-done((bf16[3,4,192,768]{3,2,1,0:T(8,128)(2,1)}, bf16[3,4,192,768]{3,2,1,0:T(8,128)(2,1)}, u32[]{:S(2)}, u32[]{:S(2)}) %collective-permute-start.24) | collective-permute-done | bytes 3538976 | tf_op jit(solution)/shard_map/ppermute | solution.py:40
  420.9 4.7 shard_map.281
  425.5 28.2 %collective-permute-done.36.refs_1_.refs_3_ = bf16[3,2,192,768]{3,2,1,0:T(8,128)(2,1)} collective-permute-done((bf16[3,2,192,768]{3,2,1,0:T(8,128)(2,1)}, bf16[3,2,192,768]{3,2,1,0:T(8,128)(2,1)}, u32[]{:S(2)}, u32[]{:S(2)}) %collective-permute-start.36) | collective-permute-done | bytes 1769504 | tf_op jit(solution)/shard_map/ppermute | solution.py:40
  457.5 13.8 %shard_map.289 = (f32[512,1536]{1,0:T(8,128)}, bf16[512,1536]{1,0:T(8,128)(2,1)}, bf16[512,1536]{1,0:T(8,128)(2,1)}, f32[40,1536]{1,0:T(8,128)}) custom-call(bf16[544,1536]{1,0:T(8,128)(2,1)} %shard_map.280.refs_4_.refs_0_, bf16[544,1536]{1,0:T(8,128)(2,1)} %collective-permute-done.32.refs_1_, bf16[544,1536]{1,0:T(8,128)(2,1)} %collective-permute-done.35.refs_2_, ...), custom_call_target="tpu_custom_call" | custom-call | flops 13799999488 | bytes 45540000 | tf_op jit(solution)/shard_map/pallas_call | solution.py:91
  471.3 28.3 %shard_map.290 = (bf16[2,256,1536]{2,1,0:T(8,128)(2,1)}, bf16[2,256,512]{2,1,0:T(8,128)(2,1)}, bf16[2,256,512]{2,1,0:T(8,128)(2,1)}, bf16[2,256,512]{2,1,0:T(8,128)(2,1)}, bf16[2,256,512]{2,1,0:T(8,128)(2,1)}) custom-call(s32[2]{0:T(128)} %refs_0_.3, s32[5]{0:T(128)} %pad_add_fusion.3.refs_1_, bf16[2,256,1536]{2,1,0:T(8,128)(2,1)} %bitcast.79, ...), custom_call_target="tpu_custom_call" | custom-call | flops 28600000512 | bytes 94380000 | tf_op jit(solution)/shard_map/pallas_call | solution.py:91
  500.2 8.7 shard_map.291
  511.4 8.3 shard_map.292
  527.7 6.1 shard_map.295
  533.8 12.4 %shard_map.296 = (f32[512,1536]{1,0:T(8,128)}, f32[40,1536]{1,0:T(8,128)}) custom-call(bf16[512,1536]{1,0:T(8,128)(2,1)} %bitcast.82, bf16[512,512]{1,0:T(8,128)(2,1)} %get-tuple-element.174.refs_1_, bf16[1536,1536]{1,0:T(8,128)(2,1)} %refs_2_.5, bf16[1536,256]{1,0:T(8,128)(2,1)} %refs_3_.3, bf16[1536,256]{1,0:T(8,128)(2,1)} %refs_4_.1, ...), custom_call_target="tpu_custom_call" | custom-call | flops 12999999488 | bytes 42900000 | tf_op jit(solution)/shard_map/pallas_call | solution.py:91
  548.0 4.9 shard_map.297
  552.9 61.0 %collective-permute-done.27.refs_1_.refs_3_ = bf16[3,2,192,768]{3,2,1,0:T(8,128)(2,1)} collective-permute-done((bf16[3,2,192,768]{3,2,1,0:T(8,128)(2,1)}, bf16[3,2,192,768]{3,2,1,0:T(8,128)(2,1)}, u32[]{:S(2)}, u32[]{:S(2)}) %collective-permute-start.27) | collective-permute-done | bytes 1769504 | tf_op jit(solution)/shard_map/ppermute | solution.py:40
  629.4 4.2 collective-permute-done.49
  635.1 6.0 collective-permute-done.50
  649.9 7.3 shard_map.308
  663.8 7.9 collective-permute-done.46.refs_7_
  671.8 4.3 shard_map.306
  676.6 4.3 shard_map.304
  690.4 69.1 %collective-permute-done.47.refs_3_ = bf16[512,1536]{1,0:T(8,128)(2,1)} collective-permute-done((bf16[512,1536]{1,0:T(8,128)(2,1)}, bf16[512,1536]{1,0:T(8,128)(2,1)}, u32[]{:S(2)}, u32[]{:S(2)}) %collective-permute-start.47) | collective-permute-done | bytes 1572896 | tf_op jit(solution)/shard_map/ppermute | solution.py:40
  761.4 5.1 shard_map.307.refs_4_.refs_3_.refs_6_
  766.5 4.7 shard_map.312
  773.7 4.8 shard_map.309
  780.4 99.2 %collective-permute-done.61.refs_1_.refs_3_ = bf16[3,2,192,768]{3,2,1,0:T(8,128)(2,1)} collective-permute-done((bf16[3,2,192,768]{3,2,1,0:T(8,128)(2,1)}, bf16[3,2,192,768]{3,2,1,0:T(8,128)(2,1)}, u32[]{:S(2)}, u32[]{:S(2)}) %collective-permute-start.61) | collective-permute-done | bytes 1769504 | tf_op jit(solution)/shard_map/ppermute | solution.py:40
  883.4 4.3 shard_map.315
  887.7 25.0 %collective-permute-done.59.refs_1_.refs_3_ = bf16[3,2,192,768]{3,2,1,0:T(8,128)(2,1)} collective-permute-done((bf16[3,2,192,768]{3,2,1,0:T(8,128)(2,1)}, bf16[3,2,192,768]{3,2,1,0:T(8,128)(2,1)}, u32[]{:S(2)}, u32[]{:S(2)}) %collective-permute-start.59) | collective-permute-done | bytes 1769504 | tf_op jit(solution)/shard_map/ppermute | solution.py:40
  923.2 4.3 shard_map.316
  932.5 4.3 shard_map.317
  936.9 28.4 %collective-permute-done.56.refs_1_.refs_3_ = bf16[2,192,896]{2,1,0:T(8,128)(2,1)S(1)} collective-permute-done((bf16[2,192,896]{2,1,0:T(8,128)(2,1)}, bf16[2,192,896]{2,1,0:T(8,128)(2,1)S(1)}, u32[]{:S(2)}, u32[]{:S(2)}) %collective-permute-start.56) | collective-permute-done | bytes 688160 | tf_op jit(solution)/shard_map/ppermute | solution.py:40
  969.3 4.5 shard_map.318
  973.8 12.1 %collective-permute-done.57 = bf16[1,192,896]{2,1,0:T(8,128)(2,1)S(1)} collective-permute-done((bf16[1,192,896]{2,1,0:T(8,128)(2,1)}, bf16[1,192,896]{2,1,0:T(8,128)(2,1)S(1)}, u32[]{:S(2)}, u32[]{:S(2)}) %collective-permute-start.57) | collective-permute-done | bytes 344096 | tf_op jit(solution)/shard_map/ppermute | solution.py:40
  (270 shorter events, 216.1 us)
Async XLA Ops:
  10.9 47.2 %collective-permute-start.3 = (bf16[2,256,512]{2,1,0:T(8,128)(2,1)}, bf16[2,256,512]{2,1,0:T(8,128)(2,1)}, u32[]{:S(2)}, u32[]{:S(2)}) collective-permute-start(bf16[2,256,512]{2,1,0:T(8,128)(2,1)} %bitcast.69), channel_id=1, source_target_pairs={{0,2},{1,3},{2,0},{3,1},{4,6},{5,7},{6,4},{7,5},{8,10},{9,11},{10,... | collective-permute-start | bytes 1572872 | tf_op jit(solution)/shard_map/ppermute | solution.py:40
  13.9 54.8 %collective-permute-start.4 = (bf16[2,256,512]{2,1,0:T(8,128)(2,1)}, bf16[2,256,512]{2,1,0:T(8,128)(2,1)}, u32[]{:S(2)}, u32[]{:S(2)}) collective-permute-start(bf16[2,256,512]{2,1,0:T(8,128)(2,1)} %bitcast.70), channel_id=1, source_target_pairs={{0,1},{1,0},{2,3},{3,2},{4,5},{5,4},{6,7},{7,6},{8,9},{9,8},{10,11... | collective-permute-start | bytes 1572872 | tf_op jit(solution)/shard_map/ppermute | solution.py:40
  13.9 80.2 %collective-permute-start.6 = (bf16[512,1536]{1,0:T(8,128)(2,1)}, bf16[512,1536]{1,0:T(8,128)(2,1)S(1)}, u32[]{:S(2)}, u32[]{:S(2)}) collective-permute-start(bf16[512,1536]{1,0:T(8,128)(2,1)} %bitcast.4.refs_1_.refs_4_), channel_id=1, source_target_pairs={{0,8},{4,12},{8,0},{12,4},{16,24},{20,28},{24,16},{28,20},{1,9},{5... | collective-permute-start | bytes 4718600 | tf_op jit(solution)/shard_map/ppermute | solution.py:40
  15.5 112.7 %collective-permute-start.14 = (bf16[512,1536]{1,0:T(8,128)(2,1)}, bf16[512,1536]{1,0:T(8,128)(2,1)}, u32[]{:S(2)}, u32[]{:S(2)}) collective-permute-start(bf16[512,1536]{1,0:T(8,128)(2,1)} %bitcast.4.refs_1_.refs_4_), channel_id=1, source_target_pairs={{0,1},{1,0},{2,3},{3,2},{4,5},{5,4},{6,7},{7,6},{8,9},{9,8},{10,11... | collective-permute-start | bytes 4718600 | tf_op jit(solution)/shard_map/ppermute | solution.py:40
  15.7 35.5 %collective-permute-start = (s32[1,5,512]{2,1,0:T(8,128)S(1)}, s32[1,5,512]{2,1,0:T(8,128)S(1)}, u32[]{:S(2)}, u32[]{:S(2)}) collective-permute-start(s32[1,5,512]{2,1,0:T(8,128)S(1)} %add_bitcast_fusion.1), channel_id=1, source_target_pairs={{0,8},{4,12},{8,0},{12,4},{16,24},{20,28},{24,16},{28,20},{1,9},{5... | collective-permute-start | bytes 30728 | tf_op jit(solution)/shard_map/ppermute | solution.py:40
  57.1 37.0 %collective-permute-start.9 = (bf16[512,1536]{1,0:T(8,128)(2,1)}, bf16[512,1536]{1,0:T(8,128)(2,1)S(1)}, u32[]{:S(2)}, u32[]{:S(2)}) collective-permute-start(bf16[512,1536]{1,0:T(8,128)(2,1)} %get-tuple-element.120), channel_id=1, source_target_pairs={{0,2},{1,3},{2,0},{3,1},{4,6},{5,7},{6,4},{7,5},{8,10},{9,11},{10,... | collective-permute-start | bytes 4718600 | tf_op jit(solution)/shard_map/ppermute | solution.py:40
  94.1 27.9 %collective-permute-start.12 = (bf16[512,1536]{1,0:T(8,128)(2,1)S(1)}, bf16[512,1536]{1,0:T(8,128)(2,1)}, u32[]{:S(2)}, u32[]{:S(2)}) collective-permute-start(bf16[512,1536]{1,0:T(8,128)(2,1)S(1)} %collective-permute-done.9.refs_0_.refs_1_), channel_id=1, source_target_pairs={{0,1},{1,0},{2,3},{3,2},{4,5},{5,4},{6,7},{7,6},{8,9},{9,8},{10,11... | collective-permute-start | bytes 4718600 | tf_op jit(solution)/shard_map/ppermute | solution.py:40
  94.1 30.7 %collective-permute-start.13 = (bf16[512,1536]{1,0:T(8,128)(2,1)S(1)}, bf16[512,1536]{1,0:T(8,128)(2,1)}, u32[]{:S(2)}, u32[]{:S(2)}) collective-permute-start(bf16[512,1536]{1,0:T(8,128)(2,1)S(1)} %collective-permute-done.6.refs_0_.refs_1_), channel_id=1, source_target_pairs={{0,1},{1,0},{2,3},{3,2},{4,5},{5,4},{6,7},{7,6},{8,9},{9,8},{10,11... | collective-permute-start | bytes 4718600 | tf_op jit(solution)/shard_map/ppermute | solution.py:40
  123.2 20.6 %collective-permute-start.10 = (bf16[256,1536]{1,0:T(8,128)(2,1)S(1)}, bf16[256,1536]{1,0:T(8,128)(2,1)}, u32[]{:S(2)}, u32[]{:S(2)}) collective-permute-start(bf16[256,1536]{1,0:T(8,128)(2,1)S(1)} %slice.50), channel_id=1, source_target_pairs={{0,8},{4,12},{8,0},{12,4},{16,24},{20,28},{24,16},{28,20},{1,9},{5... | collective-permute-start | bytes 2359304 | tf_op jit(solution)/shard_map/ppermute | solution.py:40
  126.0 20.6 %collective-permute-start.7 = (bf16[256,1536]{1,0:T(8,128)(2,1)S(1)}, bf16[256,1536]{1,0:T(8,128)(2,1)}, u32[]{:S(2)}, u32[]{:S(2)}) collective-permute-start(bf16[256,1536]{1,0:T(8,128)(2,1)S(1)} %slice.49), channel_id=1, source_target_pairs={{0,2},{1,3},{2,0},{3,1},{4,6},{5,7},{6,4},{7,5},{8,10},{9,11},{10,... | collective-permute-start | bytes 2359304 | tf_op jit(solution)/shard_map/ppermute | solution.py:40
  126.6 39.2 %collective-permute-start.16 = (bf16[544,1536]{1,0:T(8,128)(2,1)}, bf16[544,1536]{1,0:T(8,128)(2,1)}, u32[]{:S(2)}, u32[]{:S(2)}) collective-permute-start(bf16[544,1536]{1,0:T(8,128)(2,1)} %get-tuple-element.119.refs_3_.refs_1_.refs_2_.refs_8_), channel_id=1, source_target_pairs={{0,1},{1,0},{2,3},{3,2},{4,5},{5,4},{6,7},{7,6},{8,9},{9,8},{10,11... | collective-permute-start | bytes 5013512 | tf_op jit(solution)/shard_map/ppermute | solution.py:40
  126.6 54.5 %collective-permute-start.17 = (bf16[544,1536]{1,0:T(8,128)(2,1)}, bf16[544,1536]{1,0:T(8,128)(2,1)S(1)}, u32[]{:S(2)}, u32[]{:S(2)}) collective-permute-start(bf16[544,1536]{1,0:T(8,128)(2,1)} %get-tuple-element.119.refs_3_.refs_1_.refs_2_.refs_8_), channel_id=1, source_target_pairs={{0,2},{1,3},{2,0},{3,1},{4,6},{5,7},{6,4},{7,5},{8,10},{9,11},{10,... | collective-permute-start | bytes 5013512 | tf_op jit(solution)/shard_map/ppermute | solution.py:40
  128.1 54.1 %collective-permute-start.15 = (bf16[544,1536]{1,0:T(8,128)(2,1)}, bf16[544,1536]{1,0:T(8,128)(2,1)S(1)}, u32[]{:S(2)}, u32[]{:S(2)}) collective-permute-start(bf16[544,1536]{1,0:T(8,128)(2,1)} %get-tuple-element.119.refs_3_.refs_1_.refs_2_.refs_8_), channel_id=1, source_target_pairs={{0,8},{4,12},{8,0},{12,4},{16,24},{20,28},{24,16},{28,20},{1,9},{5... | collective-permute-start | bytes 5013512 | tf_op jit(solution)/shard_map/ppermute | solution.py:40
  143.8 15.0 %collective-permute-start.11 = (bf16[256,1536]{1,0:T(8,128)(2,1)}, bf16[256,1536]{1,0:T(8,128)(2,1)S(1)}, u32[]{:S(2)}, u32[]{:S(2)}) collective-permute-start(bf16[256,1536]{1,0:T(8,128)(2,1)} %collective-permute-done.10.refs_2_), channel_id=1, source_target_pairs={{0,1},{1,0},{2,3},{3,2},{4,5},{5,4},{6,7},{7,6},{8,9},{9,8},{10,11... | collective-permute-start | bytes 2359304 | tf_op jit(solution)/shard_map/ppermute | solution.py:40
  185.3 21.4 %collective-permute-start.21 = (bf16[288,1536]{1,0:T(8,128)(2,1)}, bf16[288,1536]{1,0:T(8,128)(2,1)S(1)}, u32[]{:S(2)}, u32[]{:S(2)}) collective-permute-start(bf16[288,1536]{1,0:T(8,128)(2,1)} %slice.52), channel_id=1, source_target_pairs={{0,8},{4,12},{8,0},{12,4},{16,24},{20,28},{24,16},{28,20},{1,9},{5... | collective-permute-start | bytes 2654216 | tf_op jit(solution)/shard_map/ppermute | solution.py:40
  186.9 20.7 %collective-permute-start.18 = (bf16[256,1536]{1,0:T(8,128)(2,1)S(1)}, bf16[256,1536]{1,0:T(8,128)(2,1)S(1)}, u32[]{:S(2)}, u32[]{:S(2)}) collective-permute-start(bf16[256,1536]{1,0:T(8,128)(2,1)S(1)} %slice.51), channel_id=1, source_target_pairs={{0,2},{1,3},{2,0},{3,1},{4,6},{5,7},{6,4},{7,5},{8,10},{9,11},{10,... | collective-permute-start | bytes 2359304 | tf_op jit(solution)/shard_map/ppermute | solution.py:40
  250.2 81.0 %collective-permute-start.25 = (bf16[3,4,192,768]{3,2,1,0:T(8,128)(2,1)}, bf16[3,4,192,768]{3,2,1,0:T(8,128)(2,1)S(1)}, u32[]{:S(2)}, u32[]{:S(2)}) collective-permute-start(bf16[3,4,192,768]{3,2,1,0:T(8,128)(2,1)} %get-tuple-element.152), channel_id=1, source_target_pairs={{0,4},{4,0},{8,12},{12,8},{16,20},{20,16},{24,28},{28,24},{1,5},{5... | collective-permute-start | bytes 10616840 | tf_op jit(solution)/shard_map/ppermute | solution.py:40
  341.2 79.6 %collective-permute-start.24 = (bf16[3,4,192,768]{3,2,1,0:T(8,128)(2,1)}, bf16[3,4,192,768]{3,2,1,0:T(8,128)(2,1)}, u32[]{:S(2)}, u32[]{:S(2)}) collective-permute-start(bf16[3,4,192,768]{3,2,1,0:T(8,128)(2,1)} %get-tuple-element.145), channel_id=1, source_target_pairs={{0,4},{4,0},{8,12},{12,8},{16,20},{20,16},{24,28},{28,24},{1,5},{5... | collective-permute-start | bytes 10616840 | tf_op jit(solution)/shard_map/ppermute | solution.py:40
  349.1 32.5 %collective-permute-start.33 = (bf16[544,1536]{1,0:T(8,128)(2,1)}, bf16[544,1536]{1,0:T(8,128)(2,1)S(1)}, u32[]{:S(2)}, u32[]{:S(2)}) collective-permute-start(bf16[544,1536]{1,0:T(8,128)(2,1)} %shard_map.286), channel_id=1, source_target_pairs={{0,1},{1,0},{2,3},{3,2},{4,5},{5,4},{6,7},{7,6},{8,9},{9,8},{10,11... | collective-permute-start | bytes 5013512 | tf_op jit(solution)/shard_map/ppermute | solution.py:40
  354.6 19.9 %collective-permute-start.31 = (bf16[256,1536]{1,0:T(8,128)(2,1)}, bf16[256,1536]{1,0:T(8,128)(2,1)S(1)}, u32[]{:S(2)}, u32[]{:S(2)}) collective-permute-start(bf16[256,1536]{1,0:T(8,128)(2,1)} %get-tuple-element.158), channel_id=1, source_target_pairs={{0,2},{1,3},{2,0},{3,1},{4,6},{5,7},{6,4},{7,5},{8,10},{9,11},{10,... | collective-permute-start | bytes 2359304 | tf_op jit(solution)/shard_map/ppermute | solution.py:40
  355.1 26.9 %collective-permute-start.34 = (bf16[288,1536]{1,0:T(8,128)(2,1)}, bf16[288,1536]{1,0:T(8,128)(2,1)}, u32[]{:S(2)}, u32[]{:S(2)}) collective-permute-start(bf16[288,1536]{1,0:T(8,128)(2,1)} %get-tuple-element.159), channel_id=1, source_target_pairs={{0,8},{4,12},{8,0},{12,4},{16,24},{20,28},{24,16},{28,20},{1,9},{5... | collective-permute-start | bytes 2654216 | tf_op jit(solution)/shard_map/ppermute | solution.py:40
  359.0 29.3 %collective-permute-start.26 = (bf16[544,1536]{1,0:T(8,128)(2,1)}, bf16[544,1536]{1,0:T(8,128)(2,1)S(1)}, u32[]{:S(2)}, u32[]{:S(2)}) collective-permute-start(bf16[544,1536]{1,0:T(8,128)(2,1)} %shard_map.279), channel_id=1, source_target_pairs={{0,1},{1,0},{2,3},{3,2},{4,5},{5,4},{6,7},{7,6},{8,9},{9,8},{10,11... | collective-permute-start | bytes 5013512 | tf_op jit(solution)/shard_map/ppermute | solution.py:40
  374.5 79.3 %collective-permute-start.36 = (bf16[3,2,192,768]{3,2,1,0:T(8,128)(2,1)}, bf16[3,2,192,768]{3,2,1,0:T(8,128)(2,1)}, u32[]{:S(2)}, u32[]{:S(2)}) collective-permute-start(bf16[3,2,192,768]{3,2,1,0:T(8,128)(2,1)} %get-tuple-element.161), channel_id=1, source_target_pairs={{0,16},{4,20},{8,24},{12,28},{16,0},{20,4},{24,8},{28,12},{1,17},{... | collective-permute-start | bytes 5308424 | tf_op jit(solution)/shard_map/ppermute | solution.py:40
  381.5 76.0 %collective-permute-start.32 = (bf16[544,1536]{1,0:T(8,128)(2,1)}, bf16[544,1536]{1,0:T(8,128)(2,1)}, u32[]{:S(2)}, u32[]{:S(2)}) collective-permute-start(bf16[544,1536]{1,0:T(8,128)(2,1)} %shard_map.285), channel_id=1, source_target_pairs={{0,8},{4,12},{8,0},{12,4},{16,24},{20,28},{24,16},{28,20},{1,9},{5... | collective-permute-start | bytes 5013512 | tf_op jit(solution)/shard_map/ppermute | solution.py:40
  387.2 70.4 %collective-permute-start.35 = (bf16[544,1536]{1,0:T(8,128)(2,1)}, bf16[544,1536]{1,0:T(8,128)(2,1)}, u32[]{:S(2)}, u32[]{:S(2)}) collective-permute-start(bf16[544,1536]{1,0:T(8,128)(2,1)} %shard_map.287), channel_id=1, source_target_pairs={{0,2},{1,3},{2,0},{3,1},{4,6},{5,7},{6,4},{7,5},{8,10},{9,11},{10,... | collective-permute-start | bytes 5013512 | tf_op jit(solution)/shard_map/ppermute | solution.py:40
  389.4 156.7 %collective-permute-start.28 = (bf16[3,4,192,768]{3,2,1,0:T(8,128)(2,1)}, bf16[3,4,192,768]{3,2,1,0:T(8,128)(2,1)S(1)}, u32[]{:S(2)}, u32[]{:S(2)}) collective-permute-start(bf16[3,4,192,768]{3,2,1,0:T(8,128)(2,1)} %get-tuple-element.157), channel_id=1, source_target_pairs={{0,4},{4,0},{8,12},{12,8},{16,20},{20,16},{24,28},{28,24},{1,5},{5... | collective-permute-start | bytes 10616840 | tf_op jit(solution)/shard_map/ppermute | solution.py:40
  499.7 20.0 %collective-permute-start.37 = (bf16[2,256,512]{2,1,0:T(8,128)(2,1)}, bf16[2,256,512]{2,1,0:T(8,128)(2,1)}, u32[]{:S(2)}, u32[]{:S(2)}) collective-permute-start(bf16[2,256,512]{2,1,0:T(8,128)(2,1)} %get-tuple-element.167), channel_id=1, source_target_pairs={{0,1},{1,0},{2,3},{3,2},{4,5},{5,4},{6,7},{7,6},{8,9},{9,8},{10,11... | collective-permute-start | bytes 1572872 | tf_op jit(solution)/shard_map/ppermute | solution.py:40
  533.8 115.6 %collective-permute-start.53 = (bf16[2,8,192,896]{3,2,1,0:T(8,128)(2,1)}, bf16[2,8,192,896]{3,2,1,0:T(8,128)(2,1)}, u32[]{:S(2)}, u32[]{:S(2)}) collective-permute-start(bf16[2,8,192,896]{3,2,1,0:T(8,128)(2,1)} %get-tuple-element.186), channel_id=1, source_target_pairs={{0,1},{1,0},{2,3},{3,2},{4,5},{5,4},{6,7},{7,6},{8,9},{9,8},{10,11... | collective-permute-start | bytes 16515080 | tf_op jit(solution)/shard_map/ppermute | solution.py:40
  533.8 80.0 %collective-permute-start.27 = (bf16[3,2,192,768]{3,2,1,0:T(8,128)(2,1)}, bf16[3,2,192,768]{3,2,1,0:T(8,128)(2,1)}, u32[]{:S(2)}, u32[]{:S(2)}) collective-permute-start(bf16[3,2,192,768]{3,2,1,0:T(8,128)(2,1)} %get-tuple-element.155), channel_id=1, source_target_pairs={{0,16},{4,20},{8,24},{12,28},{16,0},{20,4},{24,8},{28,12},{1,17},{... | collective-permute-start | bytes 5308424 | tf_op jit(solution)/shard_map/ppermute | solution.py:40
  621.1 21.6 %collective-permute-start.42 = (bf16[512,1536]{1,0:T(8,128)(2,1)}, bf16[512,1536]{1,0:T(8,128)(2,1)}, u32[]{:S(2)}, u32[]{:S(2)}) collective-permute-start(bf16[512,1536]{1,0:T(8,128)(2,1)} %shard_map.302), channel_id=1, source_target_pairs={{0,1},{1,0},{2,3},{3,2},{4,5},{5,4},{6,7},{7,6},{8,9},{9,8},{10,11... | collective-permute-start | bytes 4718600 | tf_op jit(solution)/shard_map/ppermute | solution.py:40
  625.1 32.1 %collective-permute-start.45 = (bf16[512,1536]{1,0:T(8,128)(2,1)}, bf16[512,1536]{1,0:T(8,128)(2,1)S(1)}, u32[]{:S(2)}, u32[]{:S(2)}) collective-permute-start(bf16[512,1536]{1,0:T(8,128)(2,1)} %shard_map.305), channel_id=1, source_target_pairs={{0,1},{1,0},{2,3},{3,2},{4,5},{5,4},{6,7},{7,6},{8,9},{9,8},{10,11... | collective-permute-start | bytes 4718600 | tf_op jit(solution)/shard_map/ppermute | solution.py:40
  629.2 29.6 %collective-permute-start.41 = (bf16[512,1536]{1,0:T(8,128)(2,1)}, bf16[512,1536]{1,0:T(8,128)(2,1)S(1)}, u32[]{:S(2)}, u32[]{:S(2)}) collective-permute-start(bf16[512,1536]{1,0:T(8,128)(2,1)} %shard_map.301), channel_id=1, source_target_pairs={{0,1},{1,0},{2,3},{3,2},{4,5},{5,4},{6,7},{7,6},{8,9},{9,8},{10,11... | collective-permute-start | bytes 4718600 | tf_op jit(solution)/shard_map/ppermute | solution.py:40
  641.2 125.3 %collective-permute-start.58 = (bf16[3,4,192,768]{3,2,1,0:T(8,128)(2,1)}, bf16[3,4,192,768]{3,2,1,0:T(8,128)(2,1)}, u32[]{:S(2)}, u32[]{:S(2)}) collective-permute-start(bf16[3,4,192,768]{3,2,1,0:T(8,128)(2,1)} %get-tuple-element.196), channel_id=1, source_target_pairs={{0,4},{4,0},{8,12},{12,8},{16,20},{20,16},{24,28},{28,24},{1,5},{5... | collective-permute-start | bytes 10616840 | tf_op jit(solution)/shard_map/ppermute | solution.py:40
  649.1 22.7 %collective-permute-start.46 = (bf16[256,1536]{1,0:T(8,128)(2,1)}, bf16[256,1536]{1,0:T(8,128)(2,1)}, u32[]{:S(2)}, u32[]{:S(2)}) collective-permute-start(bf16[256,1536]{1,0:T(8,128)(2,1)} %get-tuple-element.184), channel_id=1, source_target_pairs={{0,8},{4,12},{8,0},{12,4},{16,24},{20,28},{24,16},{28,20},{1,9},{5... | collective-permute-start | bytes 2359304 | tf_op jit(solution)/shard_map/ppermute | solution.py:40
  649.4 26.7 %collective-permute-start.43 = (bf16[256,1536]{1,0:T(8,128)(2,1)}, bf16[256,1536]{1,0:T(8,128)(2,1)}, u32[]{:S(2)}, u32[]{:S(2)}) collective-permute-start(bf16[256,1536]{1,0:T(8,128)(2,1)} %get-tuple-element.183), channel_id=1, source_target_pairs={{0,2},{1,3},{2,0},{3,1},{4,6},{5,7},{6,4},{7,5},{8,10},{9,11},{10,... | collective-permute-start | bytes 2359304 | tf_op jit(solution)/shard_map/ppermute | solution.py:40
  657.2 23.6 %collective-permute-start.52 = (f32[40,1536]{1,0:T(8,128)S(1)}, f32[40,1536]{1,0:T(8,128)}, u32[]{:S(2)}, u32[]{:S(2)}) collective-permute-start(f32[40,1536]{1,0:T(8,128)S(1)} %add.85), channel_id=1, source_target_pairs={{0,16},{4,20},{8,24},{12,28},{16,0},{20,4},{24,8},{28,12},{1,17},{... | collective-permute-start | bytes 737288 | tf_op jit(solution)/shard_map/ppermute | solution.py:40
  658.9 114.8 %collective-permute-start.54 = (bf16[1,8,192,896]{3,2,1,0:T(8,128)(2,1)}, bf16[1,8,192,896]{3,2,1,0:T(8,128)(2,1)}, u32[]{:S(2)}, u32[]{:S(2)}) collective-permute-start(bf16[1,8,192,896]{3,2,1,0:T(8,128)(2,1)} %get-tuple-element.188), channel_id=1, source_target_pairs={{0,2},{1,3},{2,0},{3,1},{4,6},{5,7},{6,4},{7,5},{8,10},{9,11},{10,... | collective-permute-start | bytes 8257544 | tf_op jit(solution)/shard_map/ppermute | solution.py:40
  676.0 83.5 %collective-permute-start.47 = (bf16[512,1536]{1,0:T(8,128)(2,1)}, bf16[512,1536]{1,0:T(8,128)(2,1)}, u32[]{:S(2)}, u32[]{:S(2)}) collective-permute-start(bf16[512,1536]{1,0:T(8,128)(2,1)} %shard_map.306), channel_id=1, source_target_pairs={{0,2},{1,3},{2,0},{3,1},{4,6},{5,7},{6,4},{7,5},{8,10},{9,11},{10,... | collective-permute-start | bytes 4718600 | tf_op jit(solution)/shard_map/ppermute | solution.py:40
  680.8 80.1 %collective-permute-start.44 = (bf16[512,1536]{1,0:T(8,128)(2,1)}, bf16[512,1536]{1,0:T(8,128)(2,1)}, u32[]{:S(2)}, u32[]{:S(2)}) collective-permute-start(bf16[512,1536]{1,0:T(8,128)(2,1)} %shard_map.304), channel_id=1, source_target_pairs={{0,8},{4,12},{8,0},{12,4},{16,24},{20,28},{24,16},{28,20},{1,9},{5... | collective-permute-start | bytes 4718600 | tf_op jit(solution)/shard_map/ppermute | solution.py:40
  684.2 199.1 %collective-permute-start.64 = (bf16[3,192,768]{2,1,0:T(8,128)(2,1)}, bf16[3,192,768]{2,1,0:T(8,128)(2,1)}, u32[]{:S(2)}, u32[]{:S(2)}) collective-permute-start(bf16[3,192,768]{2,1,0:T(8,128)(2,1)} %bitcast.40), channel_id=1, source_target_pairs={{0,8},{4,12},{8,0},{12,4},{16,24},{20,28},{24,16},{28,20},{1,9},{5... | collective-permute-start | bytes 2654216 | tf_op jit(solution)/shard_map/ppermute | solution.py:40
  759.5 162.7 %collective-permute-start.63 = (bf16[3,192,768]{2,1,0:T(8,128)(2,1)}, bf16[3,192,768]{2,1,0:T(8,128)(2,1)S(1)}, u32[]{:S(2)}, u32[]{:S(2)}) collective-permute-start(bf16[3,192,768]{2,1,0:T(8,128)(2,1)} %bitcast.37), channel_id=1, source_target_pairs={{0,8},{4,12},{8,0},{12,4},{16,24},{20,28},{24,16},{28,20},{1,9},{5... | collective-permute-start | bytes 2654216 | tf_op jit(solution)/shard_map/ppermute | solution.py:40
  761.0 118.7 %collective-permute-start.61 = (bf16[3,2,192,768]{3,2,1,0:T(8,128)(2,1)}, bf16[3,2,192,768]{3,2,1,0:T(8,128)(2,1)}, u32[]{:S(2)}, u32[]{:S(2)}) collective-permute-start(bf16[3,2,192,768]{3,2,1,0:T(8,128)(2,1)} %get-tuple-element.201), channel_id=1, source_target_pairs={{0,16},{4,20},{8,24},{12,28},{16,0},{20,4},{24,8},{28,12},{1,17},{... | collective-permute-start | bytes 5308424 | tf_op jit(solution)/shard_map/ppermute | solution.py:40
  771.2 141.6 %collective-permute-start.59 = (bf16[3,2,192,768]{3,2,1,0:T(8,128)(2,1)}, bf16[3,2,192,768]{3,2,1,0:T(8,128)(2,1)}, u32[]{:S(2)}, u32[]{:S(2)}) collective-permute-start(bf16[3,2,192,768]{3,2,1,0:T(8,128)(2,1)} %get-tuple-element.198), channel_id=1, source_target_pairs={{0,16},{4,20},{8,24},{12,28},{16,0},{20,4},{24,8},{28,12},{1,17},{... | collective-permute-start | bytes 5308424 | tf_op jit(solution)/shard_map/ppermute | solution.py:40
  778.5 137.9 %collective-permute-start.55 = (bf16[4,192,896]{2,1,0:T(8,128)(2,1)}, bf16[4,192,896]{2,1,0:T(8,128)(2,1)S(1)}, u32[]{:S(2)}, u32[]{:S(2)}) collective-permute-start(bf16[4,192,896]{2,1,0:T(8,128)(2,1)} %get-tuple-element.190), channel_id=1, source_target_pairs={{0,4},{4,0},{8,12},{12,8},{16,20},{20,16},{24,28},{28,24},{1,5},{5... | collective-permute-start | bytes 4128776 | tf_op jit(solution)/shard_map/ppermute | solution.py:40
  883.4 48.2 %collective-permute-start.62 = (bf16[3,192,768]{2,1,0:T(8,128)(2,1)}, bf16[3,192,768]{2,1,0:T(8,128)(2,1)S(1)}, u32[]{:S(2)}, u32[]{:S(2)}) collective-permute-start(bf16[3,192,768]{2,1,0:T(8,128)(2,1)} %bitcast.68), channel_id=1, source_target_pairs={{0,8},{4,12},{8,0},{12,4},{16,24},{20,28},{24,16},{28,20},{1,9},{5... | collective-permute-start | bytes 2654216 | tf_op jit(solution)/shard_map/ppermute | solution.py:40
  916.4 51.9 %collective-permute-start.60 = (bf16[3,192,768]{2,1,0:T(8,128)(2,1)}, bf16[3,192,768]{2,1,0:T(8,128)(2,1)S(1)}, u32[]{:S(2)}, u32[]{:S(2)}) collective-permute-start(bf16[3,192,768]{2,1,0:T(8,128)(2,1)} %bitcast.67), channel_id=1, source_target_pairs={{0,8},{4,12},{8,0},{12,4},{16,24},{20,28},{24,16},{28,20},{1,9},{5... | collective-permute-start | bytes 2654216 | tf_op jit(solution)/shard_map/ppermute | solution.py:40
  920.2 45.0 %collective-permute-start.56 = (bf16[2,192,896]{2,1,0:T(8,128)(2,1)}, bf16[2,192,896]{2,1,0:T(8,128)(2,1)S(1)}, u32[]{:S(2)}, u32[]{:S(2)}) collective-permute-start(bf16[2,192,896]{2,1,0:T(8,128)(2,1)} %get-tuple-element.192), channel_id=1, source_target_pairs={{0,8},{4,12},{8,0},{12,4},{16,24},{20,28},{24,16},{28,20},{1,9},{5... | collective-permute-start | bytes 2064392 | tf_op jit(solution)/shard_map/ppermute | solution.py:40
  968.4 17.6 %collective-permute-start.57 = (bf16[1,192,896]{2,1,0:T(8,128)(2,1)}, bf16[1,192,896]{2,1,0:T(8,128)(2,1)S(1)}, u32[]{:S(2)}, u32[]{:S(2)}) collective-permute-start(bf16[1,192,896]{2,1,0:T(8,128)(2,1)} %get-tuple-element.194), channel_id=1, source_target_pairs={{0,16},{4,20},{8,24},{12,28},{16,0},{20,4},{24,8},{28,12},{1,17},{... | collective-permute-start | bytes 1032200 | tf_op jit(solution)/shard_map/ppermute | solution.py:40
  (53 other events, 321.8 us)

commit v2 on v1

--- a/solution.py
+++ b/solution.py
@@ -71,7 +71,7 @@
 ANYWHERE = pl.BlockSpec(memory_space=pl.ANY)
 
 
-TIME_SCALE = 1.0
+TIME_SCALE = 0.01
 
 
 def kernel_call(us, body, grid, ins, outs, scalars=(), scratch=(), after=(), aliases=None):
@@ -330,7 +330,7 @@
             )
 
 
-def branch(x, mix, wo, gain, router_t, hit_t):
+def branch(x, mix, wo, gain, router_t, hit_t, after=()):
     rows, width = x.shape
     experts = router_t.shape[0]
     tile = 256
@@ -347,6 +347,7 @@
         + [(wo, pl.BlockSpec((wo.shape[0], tile), lambda i: (0, i)))]
         + [(a, whole(a)) for a in (gain, router_t, hit_t)],
         [(s, whole(s)) for s in outs],
+        after=after,
     )
 
 
@@ -535,7 +536,7 @@
     dz_hbm = [refs.pop(0) for _ in range(blocks)]
     gate_hbm = [refs.pop(0) for _ in range(blocks)]
     wg_hbm, wu_hbm, wd_hbm, yg_hbm, du_hbm, slope_ref = refs[:6]
-    grads_hbm, refs = (refs[6:7], refs[7:]) if joint else (refs[6:8], refs[8:])
+    grads_hbm, refs = refs[6 : 8 - joint], refs[8 - joint :]
     (
         u_ref, dz_ref, gate_ref, wg, wu, wd, ha, side_gate, side_up, dy, dga, dua, yg, du, stage,
         row_sems, sems,
@@ -608,10 +609,7 @@
     flat = ff // n_dp
 
     def spot(block):
-        if not joint:
-            return place_of(block ^ me, order, n_dp)
-        rank = block % TEAM_BIT + (block // (2 * TEAM_BIT)) * TEAM_BIT
-        return 2 * rank + (block // TEAM_BIT + me // TEAM_BIT) % 2
+        return place_of(block ^ me, order, n_dp)
 
     @pl.loop(0, width // wide)
     def _(t):
@@ -621,7 +619,7 @@
             d_weight = dot_tn(ut, grad[...]).astype(BF16)
             for i in range(wide // deep):
                 at = spot(t * (wide // deep) + i)
-                stage[which, at] = d_weight[i * deep : (i + 1) * deep]
+                stage[at, which] = d_weight[i * deep : (i + 1) * deep]
 
     @pl.loop(0, ff // wide)
     def _(t):
@@ -630,21 +628,14 @@
         for i in range(wide // flat):
             at = spot(t * (wide // flat) + i)
             part = d_weight[i * flat : (i + 1) * flat]
-            stage[2, at, :flat] = part[:, :ff]
-            stage[2, at, flat:] = part[:, ff:]
-
-    if joint:
-        out_grads = [
-            pltpu.make_async_copy(stage.at[m], grads_hbm[0].at[:, m], sems.at[5 + m])
-            for m in range(3)
-        ]
-    else:
-        out_grads = [
-            pltpu.make_async_copy(
-                stage.at[:, pl.ds(side * (n_dp // 2), n_dp // 2)], grads_hbm[side], sems.at[5 + side]
-            )
-            for side in range(2)
-        ]
+            stage[at, 2, :flat] = part[:, :ff]
+            stage[at, 2, flat:] = part[:, ff:]
+
+    part = n_dp // len(grads_hbm)
+    out_grads = [
+        pltpu.make_async_copy(stage.at[pl.ds(side * part, part)], target, sems.at[5 + side])
+        for side, target in enumerate(grads_hbm)
+    ]
     for copy in out_grads:
         copy.start()
 
@@ -675,10 +666,7 @@
     ff = wg.shape[2]
     rows = blocks * slot_count
     deep = width // n_dp
-    if joint:
-        packed = [shaped((n_dp, 3, deep, ff), BF16)]
-    else:
-        packed = [shaped((3, n_dp // 2, deep, ff), BF16)] * 2
+    packed = [shaped((n_dp // (2 - joint), 3, deep, ff), BF16)] * (2 - joint)
     row_shape = shaped((blocks, slot_count, width), BF16)
     slope_shape = shaped((blocks, slot_count, 128), F32)
     return kernel_call(
@@ -708,7 +696,7 @@
             pltpu.VMEM((rows, ff), BF16),
             pltpu.VMEM((blocks, slot_count, width), BF16),
             pltpu.VMEM((blocks, slot_count, width), BF16),
-            pltpu.VMEM((3, n_dp, width // n_dp, ff), BF16),
+            pltpu.VMEM((n_dp, 3, width // n_dp, ff), BF16),
             pltpu.SemaphoreType.DMA((3, blocks)),
             pltpu.SemaphoreType.DMA((8,)),
         ],
@@ -736,6 +724,18 @@
         [(shaped(shape, F32 if last else BF16), low), (shaped(shape, BF16), low)],
         after=after,
     )
+
+
+def add_body(a_ref, b_ref, out_ref):
+    out_ref[...] = (a_ref[...].astype(F32) + b_ref[...].astype(F32)).astype(BF16)
+
+
+def add_blocks(held, arrived, after):
+    block = pl.BlockSpec((1, *held.shape[1:]), lambda i: (i, 0, 0, 0))
+    return kernel_call(
+        4.5, add_body, held.shape[:1], [(held, block), (arrived, block)],
+        [(shaped(held.shape, BF16), block)], after=after,
+    )[0]
 
 
 def settle_body(slots, own_ref, other_ref, *refs):
@@ -832,13 +832,15 @@
     )
 
 
-def reduce_grad(keep, send, steps):
+def reduce_grad(keep, send, steps, after=(), marks=None):
     outer = keep.shape[0].bit_length()
     arrived = swap(send, *steps[0])
     for at in range(1, len(steps)):
         if at == outer:
             keep, arrived = keep[0], arrived[0]
-        keep, send = add_split(keep, arrived, 0)
+        keep, send = add_split(keep, arrived, 0, False, after if at == 1 else ())
+        if marks is not None:
+            marks.append(keep)
         arrived = swap(send, *steps[at])
     return keep[0].astype(F32) + arrived[0].astype(F32)
 
@@ -907,18 +909,25 @@
     return d_residual, d_branch, d_mix, small
 
 
-def output_body(residual_ref, *refs):
-    total = residual_ref[...]
-    for part in refs[:-1]:
-        total = total + part[...].astype(F32)
-    refs[-1][...] = total.astype(BF16)
+def output_body(starts, residual_ref, *refs):
+    parts, out_ref = refs[:-1], refs[-1]
+    cuts = sorted({0, residual_ref.shape[0], *starts})
+    for low, high in zip(cuts[:-1], cuts[1:], strict=True):
+        total = residual_ref[low:high, :]
+        for part, start in zip(parts, starts, strict=True):
+            if start <= low and high <= start + part.shape[0]:
+                total = total + part[low - start : high - start, :].astype(F32)
+        out_ref[low:high, :] = total.astype(BF16)
 
 
 def layer_output(residual, terms):
     out = shaped(residual.shape, BF16)
     return kernel_call(
         5,
-        output_body, (1,), [(a, whole(a)) for a in [residual, *terms]], [(out, whole(out))]
+        functools.partial(output_body, tuple(start for _, start in terms)),
+        (1,),
+        [(a, whole(a)) for a in [residual] + [t for t, _ in terms]],
+        [(out, whole(out))],
     )[0]
 
 
@@ -1030,8 +1039,11 @@
     normed, kv_own, queries, cot_later = project_inputs(
         x, gain_one, w_query, w_key, w_value, cos_wide, sin_wide, cot
     )
-    kv = gather_pieces(kv_own.reshape(group_count, span_len, 2 * kv_width), e_steps)
+    kv = [kv_own.reshape(group_count, span_len, 2 * kv_width)]
     q = queries([tables])
+    for number, (axis_name, bit) in enumerate(e_steps):
+        arrived = [swap(piece, axis_name, bit) for piece in kv]
+        kv = kv + arrived
     source = e_index ^ sum(
         ((jnp.arange(members) >> at) & 1) * bit for at, (_, bit) in enumerate(e_steps)
     )
@@ -1050,18 +1062,21 @@
     def scatter_team(make):
         if members != 4:
             pieces = [make(at, [], 0)[0] for at in range(2 * members)]
-            return [scatter_pieces(pieces, [team] + e_steps)]
+            return [(scatter_pieces(pieces, [team] + e_steps), 0)]
         sent = {at: swap(make(at + 4, [], 0)[0], "expert", 1) for at in (3, 1, 2, 0)}
         low, high = make(3, [(sent[3], 0)], cut)
         from_y, from_z = swap(low, *far), swap(high, *team)
         own = make(0, [(sent[0], 0)], 0)[0]
         over_z = swap(make(1, [(sent[1], 0), (from_y, 0)], 0)[0], *team)
         over_y = swap(make(2, [(sent[2], 0), (from_z, cut)], 0)[0], *far)
-        return [own, over_z, over_y]
+        return [(own, 0), (over_z, 0), (over_y, 0)]
 
     split = members == 4
     if split:
-        over_z, over_y = swap(cot, *team), swap(cot_later, *far)
+        over_z = swap(hold(cot, [tables]), *team)
+        cot_later = hold(cot_later, [tables, kv[1]])
+        over_y = swap(cot_later, *far)
+        near_own = over_near((cot,))
         cots = [(cot,), (over_z,), (over_y,)]
     else:
         cots = [(piece,) for piece in gather_pieces(cot, [team] + e_steps)]
@@ -1069,7 +1084,10 @@
     q = q.reshape(group_count, span_len, q_width)
     mix, lse = attend(q, kv, prefix, source)
     mix = mix.reshape(row_count, q_width)
-    residual, message, gates_t = branch(x, mix, w_out, gain_two, router_t, hit_t.astype(F32))
+    places = find_places(tables, first_expert, team_count, capacity, [mix])
+    residual, message, gates_t = branch(
+        x, mix, w_out, gain_two, router_t, hit_t.astype(F32), [over_z, over_y, places] if split else [places]
+    )
 
     u_rows, gate_rows = {}, {}
 
@@ -1080,46 +1098,66 @@
 
     if split:
         over_z, over_y = swap(message, *team), swap(message, *far)
+        near_rows = over_near((message,))
     else:
         pieces = gather_pieces(message, [team] + e_steps)
-    places = find_places(tables, first_expert, team_count, capacity, [message])
+    dz_rows = {}
+
+    def own_rows(at, piece, after):
+        dz_rows[at] = dispatch(piece, at, places, first_expert, slot_count, False, after)[0]
+        return [dz_rows[at]]
+
     if split:
-        cots.append(corner_of(hold(cots[1][0], [places]), hold(cots[2][0], [places])))
-        cots += [over_near(piece) for piece in cots]
-    dz_rows = []
-    for at, piece in enumerate(cots):
-        dz_rows.append(
-            dispatch(piece, at, places, first_expert, slot_count, False, dz_rows[-1:])[0]
-        )
-    if split:
-        send_rows(0, (message,), dz_rows[-1:])
-        send_rows(4, over_near((message,)), [u_rows[0]])
+        over_cot_z, over_cot_y = (hold(cots[n][0], [places]) for n in (1, 2))
+        corner = corner_of(over_cot_z, over_cot_y)
+        near_z, near_y = over_near((over_cot_z,)), over_near((over_cot_y,))
+        last = own_rows(0, cots[0], [places])
+        last = own_rows(4, near_own, last)
+        last = own_rows(1, (over_cot_z,), last)
+        last = own_rows(2, (over_cot_y,), last)
+        last = own_rows(5, near_z, last)
+        last = own_rows(6, near_y, last)
+        send_rows(0, (message,), last)
+        send_rows(4, near_rows, [u_rows[0]])
         over_z, over_y = hold(over_z, [u_rows[4]]), hold(over_y, [u_rows[4]])
-        corner = corner_of(over_z, over_y)
-        for at, piece in ((1, (over_z,)), (2, (over_y,))):
-            send_rows(at, piece, [])
-            send_rows(4 + at, over_near(piece), [])
-        last = [u_rows[5], u_rows[6]]
-        corner = tuple(hold(part, last) for part in corner)
-        send_rows(3, corner, [])
-        send_rows(7, over_near(corner), [])
+        corner_rows = corner_of(over_z, over_y)
+        near_rows_z, near_rows_y = over_near((over_z,)), over_near((over_y,))
+        send_rows(1, (over_z,), [])
+        send_rows(2, (over_y,), [u_rows[1]])
+        send_rows(5, near_rows_z, [u_rows[2]])
+        send_rows(6, near_rows_y, [u_rows[5]])
+        corner = tuple(hold(part, [u_rows[6]]) for part in corner)
+        near_corner = over_near(corner)
+        last = own_rows(3, corner, [u_rows[6]])
+        corner_rows = tuple(hold(part, last) for part in corner_rows)
+        near_corner_rows = over_near(corner_rows)
+        last = own_rows(7, near_corner, last)
+        send_rows(3, corner_rows, last)
+        send_rows(7, near_corner_rows, [u_rows[3]])
     else:
+        last = []
+        for at, piece in enumerate(cots):
+            last = own_rows(at, piece, last)
         for at, piece in enumerate(pieces):
-            send_rows(at, (piece,), dz_rows[-1:])
+            send_rows(at, (piece,), last)
+    dz_rows = [dz_rows[at] for at in range(2 * members)]
     u_rows, gate_rows = ([rows[at] for at in range(2 * members)] for rows in (u_rows, gate_rows))
     d_order = [bit for bit in reversed(bits_of(n_dp)) if bit != TEAM_BIT] + [TEAM_BIT]
-    me = d_index.reshape(1).astype(jnp.int32)
+    kept_bits = sum(d_order[1:-1])
+    me = (d_index - (d_index & kept_bits)).reshape(1).astype(jnp.int32)
+    team_place = (d_index & TEAM_BIT).reshape(1).astype(jnp.int32)
     outs, backs, slopes, chains = [], [], [], []
     chunk = 8
     for e in range(team_count):
         expert = (first_local + e).reshape(1).astype(jnp.int32)
+        joint = int(e == 3)
         parts = []
         for start in range(0, len(u_rows), chunk):
             span = slice(start, start + chunk)
             parts.append(
                 expert_pass(
-                    e, expert, me, u_rows[span], dz_rows[span], gate_rows[span],
-                    w_gate, w_up, w_down, n_dp, d_order, False, slopes[-1:],
+                    e, expert, team_place if joint else me, u_rows[span], dz_rows[span], gate_rows[span],
+                    w_gate, w_up, w_down, n_dp, d_order, joint, slopes[-1:],
                 )
             )
         if len(parts) == 1:
@@ -1132,35 +1170,47 @@
         outs.append(out)
         backs.append(back)
         slopes.append(slope)
-        chains.append((grads[0], swap(grads[1], "dp", d_order[0])))
-    done = [0] * team_count
-    ppermuted = team_count
+        chains.append(grads[0] if joint else (grads[0], swap(grads[1], "dp", d_order[0])))
+    pairs = {
+        bit: [[d, d + bit] for d in range(n_dp) if (d // bit) % 2 == 0] for bit in d_order[1:-1]
+    }
 
     def advance(e, after):
-        if e >= ppermuted or done[e] >= len(d_order) - 1:
+        if e >= team_count:
             return list(after)
-        done[e] += 1
-        step = done[e]
-        keep, arrived = chains[e]
-        keep, send = add_split(keep, arrived, 1, step == len(d_order) - 1, after)
-        if step == len(d_order) - 1:
-            chains[e] = (keep[:, 0], swap(send[:, 0], "dp", d_order[step]))
-        else:
-            chains[e] = (keep, swap(send, "dp", d_order[step]))
-        return [keep]
+        if e == 3:
+            ranks = [
+                sum(bit for at, bit in enumerate(d_order[:-1]) if (n_dp // 4 >> at) & r)
+                for r in range(n_dp // 2)
+            ]
+            groups = [[side * TEAM_BIT + r for r in ranks] for side in range(2)]
+            chains[e] = lax.psum_scatter(
+                hold(chains[e], after), "dp", scatter_dimension=0, tiled=True,
+                axis_index_groups=groups,
+            )
+            return list(after)
+        total = mark = add_blocks(*chains[e], after)
+        for bit in d_order[1:-1]:
+            total = lax.psum_scatter(
+                total, "dp", scatter_dimension=0, tiled=True, axis_index_groups=pairs[bit]
+            )
+        chains[e] = total
+        return [mark]
 
     extra = expert_count
 
-    first_marks = advance(0, slopes[-1:])
+    first_marks, marked = advance(0, slopes[-1:]), []
 
     def make_back(at, added, cut_at):
-        return combine(
+        parts = combine(
             backs, at, places, slopes, first_expert, added, cut_at, extra,
             first_marks if at >= members else (),
         )
-
-    back_terms = scatter_team(make_back)
-    marks = advance(0, advance(1, back_terms[:1]))
+        marked.append(parts[0])
+        return parts
+
+    back_terms = [term for term, _ in scatter_team(make_back)]
+    marks = advance(1, marked[-3:])
     d_residual, d_branch, d_mix, small = back_through_branch(
         back_terms, residual, cot, gain_two, gates_t, router_t, message, w_out, marks
     )
@@ -1178,60 +1228,86 @@
     q_part, kv_part = q_width // members, kv_width // members
     w_parts = []
 
-    def add_weight(left, right, start, after):
-        buffers = w_parts[-1] if w_parts else []
+    def add_weight(left, right, total_cols, start, after):
+        buffers = w_parts[-1] if start else []
         w_parts.append(
             weight_grad(
                 left, right, grad_places, n_dp, members, w_order,
-                2 * q_part + 2 * kv_part, start, buffers, after,
+                total_cols, start, buffers, after,
             )
         )
 
+    marks = advance(3, advance(2, [d_mix]))
+
+    def out_rows(at, added, cut_at, after):
+        return combine(outs, at, places, None, first_expert, added, cut_at, 0, after)
+
+    if split:
+        nears = {at: out_rows(at + 4, [], 0, marks)[0] for at in (3, 1, 2, 0)}
+        sent = {at: swap(rows, *near) for at, rows in nears.items()}
+        marks = list(nears.values())
     dq, d_kv = attend_back(
         q, d_mix.reshape(group_count, span_len, q_width), lse, kv, prefix, source,
-        cos_span, sin_span,
+        cos_span, sin_span, marks,
     )
     dq = dq.reshape(row_count, q_width)
-    add_weight(mix, d_branch, 0, [dq])
-    add_weight(normed, dq, q_part, [])
+    settled = []
+
+    def settle_expert(e, held, after):
+        result = hold(chains[e], held)
+        slots = jnp.stack([first_local + e, team_count - first_local + e]).astype(jnp.int32)
+        totals = settled[-1] if settled else []
+        other = swap(result[1], *team)
+        settled.append(settle(result[0], other, slots, local_count, totals, after))
+
+    marks = [dq]
+    if split:
+        low, high = out_rows(3, [(sent[3], 0)], cut, marks)
+        from_y, from_z = swap(low, *far), swap(high, *team)
+        marks = [low]
+    add_weight(mix, d_branch, 2 * q_part, 0, marks)
+    add_weight(normed, dq, 2 * q_part, q_part, [])
+    marks = w_parts[-1][:1]
+    if split:
+        own = out_rows(0, [(sent[0], 0)], 0, marks)[0]
+        over_z = out_rows(1, [(sent[1], 0), (from_y, 0)], 0, marks)[0]
+        over_y = out_rows(2, [(sent[2], 0), (from_z, cut)], 0, marks)[0]
+        out_terms = [(own, 0), (swap(over_z, *team), 0), (swap(over_y, *far), 0)]
+        marks = [own, over_z, over_y]
+    else:
+        out_terms = scatter_team(lambda at, added, cut_at: out_rows(at, added, cut_at, marks))
     last_step = e_steps[0]
     halves = [scatter_pieces(d_kv[at::2], e_steps[1:]) for at in range(2)]
-    held, sent = (h.reshape(row_count, 2 * kv_width) for h in halves)
-    arrived = hold(swap(sent, *last_step), w_parts[-1][:1])
+    held, far_half = (h.reshape(row_count, 2 * kv_width) for h in halves)
+    arrived = hold(swap(far_half, *last_step), marks)
     d_kv_own, joined = key_value_back(held, arrived, cos_wide, sin_wide, members)
-    add_weight(normed, joined, 2 * q_part, [])
-    d_hidden, sums = finish(
-        dq, d_kv_own, w_query, w_key, w_value, x, d_residual, gain_one, small, w_parts[-1][:1]
-    )
-    if q_part % 128 == 0 and kv_part % 64 == 0:
-        w_keep, w_send = w_parts[-1]
+    if q_part % 128 == 0:
+        w_keep, w_send = w_parts[1]
     else:
         w_keep, w_send = (jnp.concatenate([p[i] for p in w_parts], axis=3) for i in range(2))
-    marks = advance(1, advance(2, [d_hidden]))
-
-    def make_out(at, added, cut_at):
-        return combine(outs, at, places, None, first_expert, added, cut_at, 0, marks)
-
-    output = layer_output(residual, scatter_team(make_out))
-    sums = all_sum(sums, ("expert", "dp"))
-    w_total = reduce_grad(w_keep, w_send, w_steps)
-
-    totals = []
-    for e in range(team_count):
-        while e < ppermuted and done[e] < len(d_order) - 1:
-            advance(e, [output])
-        own, other = chains[e]
-        slots = jnp.stack([first_local + e, team_count - first_local + e]).astype(jnp.int32)
-        totals = settle(own, other, slots, local_count, totals, [output])
-    grad_gate, grad_up, grad_down = totals
+    w_marks = []
+    grads = reduce_grad(w_keep, w_send, w_steps, [d_kv_own], w_marks)
+    add_weight(normed, joined, 2 * kv_part, 0, w_marks[:1])
+    d_hidden, sums = finish(
+        dq, d_kv_own, w_query, w_key, w_value, x, d_residual, gain_one, small, [w_parts[-1][0]]
+    )
+    later = [d_hidden]
+    output = layer_output(residual, out_terms)
+    kv_keep, kv_send = w_parts[2]
+    kv_grads = reduce_grad(kv_keep, hold(kv_send, later), w_steps)
+    sums = all_sum(hold(sums, later), ("expert", "dp"))
+
+    for e in range(len(settled), team_count):
+        settle_expert(e, [dq] if e < 2 else [output], [output])
+    grad_gate, grad_up, grad_down = settled[-1]
     return (
         output.reshape(group_count, span_len, width),
         d_hidden.reshape(group_count, span_len, width),
         sums[expert_count + 1],
-        w_total[:, q_part : 2 * q_part],
-        w_total[:, 2 * q_part : 2 * q_part + kv_part],
-        w_total[:, 2 * q_part + kv_part :],
-        w_total[:, :q_part],
+        grads[:, q_part:],
+        kv_grads[:, :kv_part],
+        kv_grads[:, kv_part:],
+        grads[:, :q_part],
         sums[expert_count],
         sums[:expert_count].T,
         grad_gate,

time: 999 us -> 845 us (0.85)
  waiting for transfers between devices: 483 us -> 297 us
  local copies, waits for them, and re-layouts: 36.1 us -> 55.4 us
  between operations: 1.34 us -> 14.5 us
  Pallas kernels: 417 us -> 407 us
    ppermute x65, waiting for transfers between devices: 483 us -> 297 us  [swap(): return lax.ppermute(values, axis_name, [(i, i ^ bit) for i in range(count)])]
    pallas_call x72 -> x82, Pallas kernels: 417 us -> 407 us  [kernel_call(): pl.pallas_call(run, grid_spec=grid_spec, out_shape=[shape for shape, _ in...]
    unnamed x76 -> x99, local copies, waits for them, and re-layouts: 24.1 us -> 30.9 us
  transfers between devices with their start and end apart: 65 -> 69, of which waited for: 22 -> 21; matrix products, arithmetic and copies ran while one was open for 2% -> 4% of each run, Pallas kernels for 38% -> 44%
where the time goes in v2:
time: 845 us; the launch traced here: 833 us
  Pallas kernels  407 us (48%)
  waiting for transfers between devices  297 us (35%)
  local copies, waits for them, and re-layouts  55.4 us (7%)
  starting transfers between devices  48.2 us (6%)
  between operations  14.5 us (2%)
  other arithmetic  10.9 us (1%)
    pallas_call x82, Pallas kernels, kernel_call(): pl.pallas_call(run, grid_spec=grid_spec, out_shape=[shape for shape, _ in...  407 us
    ppermute x65, waiting for transfers between devices, swap(): return lax.ppermute(values, axis_name, [(i, i ^ bit) for i in range(count)])  297 us
    ppermute x65, starting transfers between devices, swap(): return lax.ppermute(values, axis_name, [(i, i ^ bit) for i in range(count)])  48.1 us
    unnamed x99, local copies, waits for them, and re-layouts  30.9 us
  transfers between devices with their start and end apart: 69, of which 21 were waited for; matrix products, arithmetic and copies ran while one was open for 4% of the time, Pallas kernels for 44%

profile of v2, /device:TPU:0, one launch (start us, length us, event | category | flops | bytes accessed | tf_op | source)
XLA Modules:
  0.0 833.1 jit_solution(9319731877267504969)
XLA Ops:
  13.4 4.3 shard_map.247
  24.6 8.9 %collective-permute-done.1 = s32[2,5,512]{2,1,0:T(8,128)S(1)} collective-permute-done((s32[2,5,512]{2,1,0:T(8,128)S(1)}, s32[2,5,512]{2,1,0:T(8,128)S(1)}, u32[]{:S(2)}, u32[]{:S(2)}) %collective-permute-start.1) | collective-permute-done | bytes 20512 | tf_op jit(solution)/shard_map/ppermute | solution.py:40
  44.6 7.7 shard_map.248
  52.3 15.7 %shard_map.249 = (bf16[2,256,1536]{2,1,0:T(8,128)(2,1)}, f32[2,256,12]{2,1,0:T(8,128)}) custom-call(s32[2]{0:T(128)} %refs_0_.3, s32[5]{0:T(128)} %pad_add_fusion.3.refs_1_, bf16[2,256,1536]{2,1,0:T(8,128)(2,1)} %bitcast.73, bf16[2,256,512]{2,1,0:T(8,128)(2,1)} %bitcast.94, bf16[2,256,512]{2,1,0:T(8,128)(2,1)} %copy-done.14, ...), custom_call_target="tpu_custom_call" | custom-call | flops 157000000 | bytes 518100 | tf_op jit(solution)/shard_map/pallas_call | solution.py:91
  68.0 7.4 shard_map.252.refs_8_.refs_1_.refs_2_.refs_3_.refs_4_.refs_5_
  76.5 10.2 %shard_map.253 = (f32[512,1536]{1,0:T(8,128)}, bf16[544,1536]{1,0:T(8,128)(2,1)}, f32[32,512]{1,0:T(8,128)}) custom-call(bf16[512,1536]{1,0:T(8,128)(2,1)} %bitcast.76, bf16[512,1536]{1,0:T(8,128)(2,1)} %bitcast.79, bf16[1536,1536]{1,0:T(8,128)(2,1)} %refs_9_.1, f32[1,1536]{1,0:T(1,128)} %reshape.131.refs_3_.refs_5_, bf16[32,1536]{1,0:T(8,128)(2,1)} %bitcast.100, ...), custom_call_target="tpu_custom_call" | custom-call | flops 100000000 | bytes 330000 | tf_op jit(solution)/shard_map/pallas_call | solution.py:91
  113.4 12.7 %collective-permute-done.11.refs_0_ = bf16[544,1536]{1,0:T(8,128)(2,1)S(1)} collective-permute-done((bf16[544,1536]{1,0:T(8,128)(2,1)}, bf16[544,1536]{1,0:T(8,128)(2,1)S(1)}, u32[]{:S(2)}, u32[]{:S(2)}) %collective-permute-start.11) | collective-permute-done | bytes 1671200 | tf_op jit(solution)/shard_map/ppermute | solution.py:40
  153.2 16.7 %collective-permute-done.18.refs_0_ = bf16[256,1536]{1,0:T(8,128)(2,1)} collective-permute-done((bf16[256,1536]{1,0:T(8,128)(2,1)}, bf16[256,1536]{1,0:T(8,128)(2,1)}, u32[]{:S(2)}, u32[]{:S(2)}) %collective-permute-start.18) | collective-permute-done | bytes 786464 | tf_op jit(solution)/shard_map/ppermute | solution.py:40
  190.0 26.9 %shard_map.278 = (bf16[8,80,1536]{2,1,0:T(8,128)(2,1)}, bf16[8,80,1536]{2,1,0:T(8,128)(2,1)}, f32[8,80,128]{2,1,0:T(8,128)}, bf16[4,3,192,768]{3,2,1,0:T(8,128)(2,1)}, bf16[4,3,192,768]{3,2,1,0:T(8,128)(2,1)}) custom-call(s32[1]{0:T(128)} %bitcast.14.refs_0_, s32[1]{0:T(128)} %bitcast.15.refs_1_, bf16[4,80,1536]{2,1,0:T(8,128)(2,1)} %get-tuple-element.112.refs_4_.refs_2_, ...), custom_call_target="tpu_custom_call" | custom-call | flops 265000000 | bytes 874500 | tf_op jit(solution)/shard_map/pallas_call | solution.py:91
  218.4 26.3 %shard_map.279 = (bf16[8,80,1536]{2,1,0:T(8,128)(2,1)}, bf16[8,80,1536]{2,1,0:T(8,128)(2,1)}, f32[8,80,128]{2,1,0:T(8,128)}, bf16[4,3,192,768]{3,2,1,0:T(8,128)(2,1)}, bf16[4,3,192,768]{3,2,1,0:T(8,128)(2,1)}) custom-call(s32[1]{0:T(128)} %bitcast.16.refs_0_, s32[1]{0:T(128)} %bitcast.15.refs_1_, bf16[4,80,1536]{2,1,0:T(8,128)(2,1)} %get-tuple-element.112.refs_4_.refs_2_, ...), custom_call_target="tpu_custom_call" | custom-call | flops 265000000 | bytes 874500 | tf_op jit(solution)/shard_map/pallas_call | solution.py:91
  244.8 26.4 %shard_map.280 = (bf16[8,80,1536]{2,1,0:T(8,128)(2,1)}, bf16[8,80,1536]{2,1,0:T(8,128)(2,1)}, f32[8,80,128]{2,1,0:T(8,128)}, bf16[4,3,192,768]{3,2,1,0:T(8,128)(2,1)}, bf16[4,3,192,768]{3,2,1,0:T(8,128)(2,1)}) custom-call(s32[1]{0:T(128)} %bitcast.17.refs_0_, s32[1]{0:T(128)} %bitcast.15.refs_1_, bf16[4,80,1536]{2,1,0:T(8,128)(2,1)} %get-tuple-element.112.refs_4_.refs_2_, ...), custom_call_target="tpu_custom_call" | custom-call | flops 265000000 | bytes 874500 | tf_op jit(solution)/shard_map/pallas_call | solution.py:91
  271.2 26.6 %shard_map.281 = (bf16[8,80,1536]{2,1,0:T(8,128)(2,1)}, bf16[8,80,1536]{2,1,0:T(8,128)(2,1)}, f32[8,80,128]{2,1,0:T(8,128)}, bf16[8,3,192,768]{3,2,1,0:T(8,128)(2,1)}) custom-call(s32[1]{0:T(128)} %bitcast.18.refs_0_, s32[1]{0:T(128)} %bitcast.19.refs_1_, bf16[4,80,1536]{2,1,0:T(8,128)(2,1)} %get-tuple-element.112.refs_4_.refs_2_, ...), custom_call_target="tpu_custom_call" | custom-call | flops 265000000 | bytes 874500 | tf_op jit(solution)/shard_map/pallas_call | solution.py:91
  299.6 5.4 shard_map.282.refs_10_
  309.3 3.9 shard_map.283
  321.3 4.1 shard_map.287
  326.7 4.2 shard_map.284.refs_2_.refs_0_
  330.9 15.0 %collective-permute-done.29.refs_11_ = bf16[256,1536]{1,0:T(8,128)(2,1)} collective-permute-done((bf16[256,1536]{1,0:T(8,128)(2,1)}, bf16[256,1536]{1,0:T(8,128)(2,1)}, u32[]{:S(2)}, u32[]{:S(2)}) %collective-permute-start.29) | collective-permute-done | bytes 786464 | tf_op jit(solution)/shard_map/ppermute | solution.py:40
  345.9 4.4 shard_map.288.refs_3_
  350.3 15.0 %collective-permute-done.32.refs_11_ = bf16[288,1536]{1,0:T(8,128)(2,1)} collective-permute-done((bf16[288,1536]{1,0:T(8,128)(2,1)}, bf16[288,1536]{1,0:T(8,128)(2,1)}, u32[]{:S(2)}, u32[]{:S(2)}) %collective-permute-start.32) | collective-permute-done | bytes 884768 | tf_op jit(solution)/shard_map/ppermute | solution.py:40
  365.3 4.5 shard_map.290.refs_4_
  369.8 14.0 %collective-permute-done.34.refs_1_ = bf16[4,3,192,768]{3,2,1,0:T(8,128)(2,1)S(1)} collective-permute-done((bf16[4,3,192,768]{3,2,1,0:T(8,128)(2,1)}, bf16[4,3,192,768]{3,2,1,0:T(8,128)(2,1)S(1)}, u32[]{:S(2)}, u32[]{:S(2)}) %collective-permute-start.34) | collective-permute-done | bytes 3538976 | tf_op jit(solution)/shard_map/ppermute | solution.py:40
  385.5 5.4 shard_map.291.refs_10_
  394.0 67.0 %collective-permute-done.30.refs_1_ = bf16[544,1536]{1,0:T(8,128)(2,1)S(1)} collective-permute-done((bf16[544,1536]{1,0:T(8,128)(2,1)S(1)}, bf16[544,1536]{1,0:T(8,128)(2,1)S(1)}, u32[]{:S(2)}, u32[]{:S(2)}) %collective-permute-start.30) | collective-permute-done | bytes 1671200 | tf_op jit(solution)/shard_map/ppermute | solution.py:40
  463.4 13.9 %shard_map.292 = (f32[512,1536]{1,0:T(8,128)}, bf16[512,1536]{1,0:T(8,128)(2,1)}, bf16[512,1536]{1,0:T(8,128)(2,1)}, f32[40,1536]{1,0:T(8,128)}) custom-call(bf16[544,1536]{1,0:T(8,128)(2,1)} %shard_map.284.refs_2_.refs_0_, bf16[544,1536]{1,0:T(8,128)(2,1)} %copy-done.22, bf16[544,1536]{1,0:T(8,128)(2,1)} %copy-done.23, ...), custom_call_target="tpu_custom_call" | custom-call | flops 138000000 | bytes 455400 | tf_op jit(solution)/shard_map/pallas_call | solution.py:91
  477.2 5.5 shard_map.293.refs_6_.refs_1_
  498.4 28.7 %shard_map.298 = (bf16[2,256,1536]{2,1,0:T(8,128)(2,1)}, bf16[2,256,512]{2,1,0:T(8,128)(2,1)}, bf16[2,256,512]{2,1,0:T(8,128)(2,1)}, bf16[2,256,512]{2,1,0:T(8,128)(2,1)}, bf16[2,256,512]{2,1,0:T(8,128)(2,1)}) custom-call(s32[2]{0:T(128)} %refs_0_.3, s32[5]{0:T(128)} %pad_add_fusion.3.refs_1_, bf16[2,256,1536]{2,1,0:T(8,128)(2,1)} %bitcast.74, ...), custom_call_target="tpu_custom_call" | custom-call | flops 286000000 | bytes 943800 | tf_op jit(solution)/shard_map/pallas_call | solution.py:91
  528.2 4.0 shard_map.299
  532.2 8.1 shard_map.300
  540.3 8.5 %shard_map.301 = (bf16[2,8,192,768]{3,2,1,0:T(8,128)(2,1)}, bf16[2,8,192,768]{3,2,1,0:T(8,128)(2,1)}) custom-call(s32[5]{0:T(128)} %pad_add_fusion.4.refs_0_, bf16[512,1536]{1,0:T(8,128)(2,1)} %get-tuple-element.106.refs_0_.refs_1_, bf16[512,1536]{1,0:T(8,128)(2,1)} %bitcast.62, ...), custom_call_target="tpu_custom_call", output_to_operand_aliasing={{0}: (3, {}), {1}: (4, {})} | custom-call | flops 70000000 | bytes 231000 | tf_op jit(solution)/shard_map/pallas_call | solution.py:91
  550.3 10.9 %collective-permute-done.43 = bf16[2,256,512]{2,1,0:T(8,128)(2,1)S(1)} collective-permute-done((bf16[2,256,512]{2,1,0:T(8,128)(2,1)}, bf16[2,256,512]{2,1,0:T(8,128)(2,1)S(1)}, u32[]{:S(2)}, u32[]{:S(2)}) %collective-permute-start.43) | collective-permute-done | bytes 524320 | tf_op jit(solution)/shard_map/ppermute | solution.py:40
  573.7 4.1 shard_map.302.refs_1_
  577.8 15.8 %collective-permute-done.41.refs_7_ = bf16[256,1536]{1,0:T(8,128)(2,1)} collective-permute-done((bf16[256,1536]{1,0:T(8,128)(2,1)}, bf16[256,1536]{1,0:T(8,128)(2,1)}, u32[]{:S(2)}, u32[]{:S(2)}) %collective-permute-start.41) | collective-permute-done | bytes 786464 | tf_op jit(solution)/shard_map/ppermute | solution.py:40
  593.6 4.2 shard_map.304.refs_3_
  598.8 4.2 shard_map.303.refs_2_
  606.4 6.5 shard_map.308
  615.5 6.0 shard_map.309
  621.5 12.8 %shard_map.310 = (f32[512,1536]{1,0:T(8,128)}, f32[40,1536]{1,0:T(8,128)}) custom-call(bf16[512,1536]{1,0:T(8,128)(2,1)} %bitcast.63, bf16[512,512]{1,0:T(8,128)(2,1)} %get-tuple-element.162.refs_4_.refs_1_, bf16[1536,1536]{1,0:T(8,128)(2,1)} %refs_2_.5, bf16[1536,256]{1,0:T(8,128)(2,1)} %refs_3_.3, bf16[1536,256]{1,0:T(8,128)(2,1)} %refs_4_.1, ...), custom_call_target="tpu_custom_call" | custom-call | flops 130000000 | bytes 429000 | tf_op jit(solution)/shard_map/pallas_call | solution.py:91
  640.9 62.9 %collective-permute-done.48 = f32[40,1536]{1,0:T(8,128)} collective-permute-done((f32[40,1536]{1,0:T(8,128)S(1)}, f32[40,1536]{1,0:T(8,128)}, u32[]{:S(2)}, u32[]{:S(2)}) %collective-permute-start.48) | collective-permute-done | bytes 245792 | tf_op jit(solution)/shard_map/ppermute | solution.py:40
  706.2 4.3 shard_map.312
  723.7 5.1 shard_map.305.refs_1_.refs_3_.refs_6_
  728.8 4.1 shard_map.325
  732.9 5.2 collective-permute-done.63.refs_2_
  738.0 4.1 shard_map.326
  764.0 23.2 %collective-permute-done.59.refs_1_.refs_3_ = bf16[2,192,128]{2,1,0:T(8,128)(2,1)S(1)} collective-permute-done((bf16[2,192,128]{2,1,0:T(8,128)(2,1)}, bf16[2,192,128]{2,1,0:T(8,128)(2,1)S(1)}, u32[]{:S(2)}, u32[]{:S(2)}) %collective-permute-start.59) | collective-permute-done | bytes 98336 | tf_op jit(solution)/shard_map/ppermute | solution.py:40
  799.8 4.2 shard_map.327
  804.0 4.7 collective-permute-done.55
  809.5 11.8 %collective-permute-done.61.refs_2_ = bf16[3,192,768]{2,1,0:T(8,128)(2,1)S(1)} collective-permute-done((bf16[3,192,768]{2,1,0:T(8,128)(2,1)S(1)}, bf16[3,192,768]{2,1,0:T(8,128)(2,1)S(1)}, u32[]{:S(2)}, u32[]{:S(2)}) %collective-permute-start.61) | collective-permute-done | bytes 884768 | tf_op jit(solution)/shard_map/ppermute | solution.py:40
  822.3 4.1 shard_map.328
  (320 shorter events, 219.0 us)
Async XLA Ops:
  7.2 629.2 %reduce-scatter.11.cloned.1.call-start = ((), (), s32[]{:S(2)}) async-start(), calls=%async_computation.7 | async-start | bytes 5308416 | tf_op jit(solution)/shard_map/reduce_scatter | solution.py:1194
  17.7 19.5 %collective-permute-start.3 = (bf16[2,256,512]{2,1,0:T(8,128)(2,1)}, bf16[2,256,512]{2,1,0:T(8,128)(2,1)S(1)}, u32[]{:S(2)}, u32[]{:S(2)}) collective-permute-start(bf16[2,256,512]{2,1,0:T(8,128)(2,1)} %bitcast.92), channel_id=1, source_target_pairs={{0,2},{1,3},{2,0},{3,1},{4,6},{5,7},{6,4},{7,5},{8,10},{9,11},{10,... | collective-permute-start | bytes 1572872 | tf_op jit(solution)/shard_map/ppermute | solution.py:40
  35.4 39.9 %collective-permute-start.6 = (bf16[512,1536]{1,0:T(8,128)(2,1)}, bf16[512,1536]{1,0:T(8,128)(2,1)S(1)}, u32[]{:S(2)}, u32[]{:S(2)}) collective-permute-start(bf16[512,1536]{1,0:T(8,128)(2,1)} %shard_map.250), channel_id=1, source_target_pairs={{0,8},{4,12},{8,0},{12,4},{16,24},{20,28},{24,16},{28,20},{1,9},{5... | collective-permute-start | bytes 4718600 | tf_op jit(solution)/shard_map/ppermute | solution.py:40
  38.0 37.4 %collective-permute-start.7 = (bf16[512,1536]{1,0:T(8,128)(2,1)}, bf16[512,1536]{1,0:T(8,128)(2,1)}, u32[]{:S(2)}, u32[]{:S(2)}) collective-permute-start(bf16[512,1536]{1,0:T(8,128)(2,1)} %shard_map.251), channel_id=1, source_target_pairs={{0,2},{1,3},{2,0},{3,1},{4,6},{5,7},{6,4},{7,5},{8,10},{9,11},{10,... | collective-permute-start | bytes 4718600 | tf_op jit(solution)/shard_map/ppermute | solution.py:40
  39.6 48.7 %collective-permute-start.10 = (bf16[512,1536]{1,0:T(8,128)(2,1)S(1)}, bf16[512,1536]{1,0:T(8,128)(2,1)}, u32[]{:S(2)}, u32[]{:S(2)}) collective-permute-start(bf16[512,1536]{1,0:T(8,128)(2,1)S(1)} %bitcast.70), channel_id=1, source_target_pairs={{0,1},{1,0},{2,3},{3,2},{4,5},{5,4},{6,7},{7,6},{8,9},{9,8},{10,11... | collective-permute-start | bytes 4718600 | tf_op jit(solution)/shard_map/ppermute | solution.py:40
  86.8 23.4 %collective-permute-start.12 = (bf16[544,1536]{1,0:T(8,128)(2,1)}, bf16[544,1536]{1,0:T(8,128)(2,1)}, u32[]{:S(2)}, u32[]{:S(2)}) collective-permute-start(bf16[544,1536]{1,0:T(8,128)(2,1)} %get-tuple-element.111.refs_1_.refs_2_.refs_8_), channel_id=1, source_target_pairs={{0,1},{1,0},{2,3},{3,2},{4,5},{5,4},{6,7},{7,6},{8,9},{9,8},{10,11... | collective-permute-start | bytes 5013512 | tf_op jit(solution)/shard_map/ppermute | solution.py:40
  87.3 38.7 %collective-permute-start.11 = (bf16[544,1536]{1,0:T(8,128)(2,1)}, bf16[544,1536]{1,0:T(8,128)(2,1)S(1)}, u32[]{:S(2)}, u32[]{:S(2)}) collective-permute-start(bf16[544,1536]{1,0:T(8,128)(2,1)} %get-tuple-element.111.refs_1_.refs_2_.refs_8_), channel_id=1, source_target_pairs={{0,8},{4,12},{8,0},{12,4},{16,24},{20,28},{24,16},{28,20},{1,9},{5... | collective-permute-start | bytes 5013512 | tf_op jit(solution)/shard_map/ppermute | solution.py:40
  87.8 16.1 %collective-permute-start.8 = (bf16[512,1536]{1,0:T(8,128)(2,1)}, bf16[512,1536]{1,0:T(8,128)(2,1)}, u32[]{:S(2)}, u32[]{:S(2)}) collective-permute-start(bf16[512,1536]{1,0:T(8,128)(2,1)} %shard_map.254.refs_1_), channel_id=1, source_target_pairs={{0,1},{1,0},{2,3},{3,2},{4,5},{5,4},{6,7},{7,6},{8,9},{9,8},{10,11... | collective-permute-start | bytes 4718600 | tf_op jit(solution)/shard_map/ppermute | solution.py:40
  88.3 38.9 %collective-permute-start.13 = (bf16[544,1536]{1,0:T(8,128)(2,1)}, bf16[544,1536]{1,0:T(8,128)(2,1)S(1)}, u32[]{:S(2)}, u32[]{:S(2)}) collective-permute-start(bf16[544,1536]{1,0:T(8,128)(2,1)} %get-tuple-element.111.refs_1_.refs_2_.refs_8_), channel_id=1, source_target_pairs={{0,2},{1,3},{2,0},{3,1},{4,6},{5,7},{6,4},{7,5},{8,10},{9,11},{10,... | collective-permute-start | bytes 5013512 | tf_op jit(solution)/shard_map/ppermute | solution.py:40
  128.4 21.5 %collective-permute-start.16 = (bf16[544,1536]{1,0:T(8,128)(2,1)}, bf16[544,1536]{1,0:T(8,128)(2,1)}, u32[]{:S(2)}, u32[]{:S(2)}) collective-permute-start(bf16[544,1536]{1,0:T(8,128)(2,1)} %shard_map.266.refs_1_.refs_2_), channel_id=1, source_target_pairs={{0,1},{1,0},{2,3},{3,2},{4,5},{5,4},{6,7},{7,6},{8,9},{9,8},{10,11... | collective-permute-start | bytes 5013512 | tf_op jit(solution)/shard_map/ppermute | solution.py:40
  131.0 41.9 %collective-permute-start.19 = (bf16[288,1536]{1,0:T(8,128)(2,1)}, bf16[288,1536]{1,0:T(8,128)(2,1)S(1)}, u32[]{:S(2)}, u32[]{:S(2)}) collective-permute-start(bf16[288,1536]{1,0:T(8,128)(2,1)} %slice.84), channel_id=1, source_target_pairs={{0,8},{4,12},{8,0},{12,4},{16,24},{20,28},{24,16},{28,20},{1,9},{5... | collective-permute-start | bytes 2654216 | tf_op jit(solution)/shard_map/ppermute | solution.py:40
  134.0 35.8 %collective-permute-start.18 = (bf16[256,1536]{1,0:T(8,128)(2,1)}, bf16[256,1536]{1,0:T(8,128)(2,1)}, u32[]{:S(2)}, u32[]{:S(2)}) collective-permute-start(bf16[256,1536]{1,0:T(8,128)(2,1)} %slice.83), channel_id=1, source_target_pairs={{0,8},{4,12},{8,0},{12,4},{16,24},{20,28},{24,16},{28,20},{1,9},{5... | collective-permute-start | bytes 2359304 | tf_op jit(solution)/shard_map/ppermute | solution.py:40
  136.1 33.8 %collective-permute-start.15 = (bf16[256,1536]{1,0:T(8,128)(2,1)}, bf16[256,1536]{1,0:T(8,128)(2,1)}, u32[]{:S(2)}, u32[]{:S(2)}) collective-permute-start(bf16[256,1536]{1,0:T(8,128)(2,1)} %slice.82), channel_id=1, source_target_pairs={{0,2},{1,3},{2,0},{3,1},{4,6},{5,7},{6,4},{7,5},{8,10},{9,11},{10,... | collective-permute-start | bytes 2359304 | tf_op jit(solution)/shard_map/ppermute | solution.py:40
  138.7 35.7 %collective-permute-start.14 = (bf16[256,1536]{1,0:T(8,128)(2,1)}, bf16[256,1536]{1,0:T(8,128)(2,1)S(1)}, u32[]{:S(2)}, u32[]{:S(2)}) collective-permute-start(bf16[256,1536]{1,0:T(8,128)(2,1)} %slice.81), channel_id=1, source_target_pairs={{0,2},{1,3},{2,0},{3,1},{4,6},{5,7},{6,4},{7,5},{8,10},{9,11},{10,... | collective-permute-start | bytes 2359304 | tf_op jit(solution)/shard_map/ppermute | solution.py:40
  216.9 81.0 %collective-permute-start.25 = (bf16[4,3,192,768]{3,2,1,0:T(8,128)(2,1)}, bf16[4,3,192,768]{3,2,1,0:T(8,128)(2,1)S(1)}, u32[]{:S(2)}, u32[]{:S(2)}) collective-permute-start(bf16[4,3,192,768]{3,2,1,0:T(8,128)(2,1)} %get-tuple-element.143), channel_id=1, source_target_pairs={{0,4},{4,0},{8,12},{12,8},{16,20},{20,16},{24,28},{28,24},{1,5},{5... | collective-permute-start | bytes 10616840 | tf_op jit(solution)/shard_map/ppermute | solution.py:40
  305.1 335.8 %reduce-scatter.9.cloned.1.call-start = ((), (), s32[]{:S(2)}) async-start(), calls=%async_computation.6 | async-start | bytes 5308416 | tf_op jit(solution)/shard_map/reduce_scatter | solution.py:1194
  305.1 78.6 %collective-permute-start.34 = (bf16[4,3,192,768]{3,2,1,0:T(8,128)(2,1)}, bf16[4,3,192,768]{3,2,1,0:T(8,128)(2,1)S(1)}, u32[]{:S(2)}, u32[]{:S(2)}) collective-permute-start(bf16[4,3,192,768]{3,2,1,0:T(8,128)(2,1)} %get-tuple-element.148), channel_id=1, source_target_pairs={{0,4},{4,0},{8,12},{12,8},{16,20},{20,16},{24,28},{28,24},{1,5},{5... | collective-permute-start | bytes 10616840 | tf_op jit(solution)/shard_map/ppermute | solution.py:40
  320.8 29.5 %collective-permute-start.31 = (bf16[544,1536]{1,0:T(8,128)(2,1)}, bf16[544,1536]{1,0:T(8,128)(2,1)}, u32[]{:S(2)}, u32[]{:S(2)}) collective-permute-start(bf16[544,1536]{1,0:T(8,128)(2,1)} %shard_map.289), channel_id=1, source_target_pairs={{0,1},{1,0},{2,3},{3,2},{4,5},{5,4},{6,7},{7,6},{8,9},{9,8},{10,11... | collective-permute-start | bytes 5013512 | tf_op jit(solution)/shard_map/ppermute | solution.py:40
  325.4 39.9 %collective-permute-start.32 = (bf16[288,1536]{1,0:T(8,128)(2,1)}, bf16[288,1536]{1,0:T(8,128)(2,1)}, u32[]{:S(2)}, u32[]{:S(2)}) collective-permute-start(bf16[288,1536]{1,0:T(8,128)(2,1)} %get-tuple-element.145), channel_id=1, source_target_pairs={{0,8},{4,12},{8,0},{12,4},{16,24},{20,28},{24,16},{28,20},{1,9},{5... | collective-permute-start | bytes 2654216 | tf_op jit(solution)/shard_map/ppermute | solution.py:40
  326.4 19.5 %collective-permute-start.29 = (bf16[256,1536]{1,0:T(8,128)(2,1)}, bf16[256,1536]{1,0:T(8,128)(2,1)}, u32[]{:S(2)}, u32[]{:S(2)}) collective-permute-start(bf16[256,1536]{1,0:T(8,128)(2,1)} %get-tuple-element.144), channel_id=1, source_target_pairs={{0,2},{1,3},{2,0},{3,1},{4,6},{5,7},{6,4},{7,5},{8,10},{9,11},{10,... | collective-permute-start | bytes 2359304 | tf_op jit(solution)/shard_map/ppermute | solution.py:40
  391.0 351.1 %reduce-scatter.7.cloned.1.call-start = ((), (), s32[]{:S(2)}) async-start(), calls=%async_computation.5 | async-start | bytes 5308416 | tf_op jit(solution)/shard_map/reduce_scatter | solution.py:1194
  391.0 86.2 %collective-permute-start.24 = (bf16[4,3,192,768]{3,2,1,0:T(8,128)(2,1)}, bf16[4,3,192,768]{3,2,1,0:T(8,128)(2,1)}, u32[]{:S(2)}, u32[]{:S(2)}) collective-permute-start(bf16[4,3,192,768]{3,2,1,0:T(8,128)(2,1)} %get-tuple-element.136), channel_id=1, source_target_pairs={{0,4},{4,0},{8,12},{12,8},{16,20},{20,16},{24,28},{28,24},{1,5},{5... | collective-permute-start | bytes 10616840 | tf_op jit(solution)/shard_map/ppermute | solution.py:40
  392.4 68.6 %collective-permute-start.30 = (bf16[544,1536]{1,0:T(8,128)(2,1)S(1)}, bf16[544,1536]{1,0:T(8,128)(2,1)S(1)}, u32[]{:S(2)}, u32[]{:S(2)}) collective-permute-start(bf16[544,1536]{1,0:T(8,128)(2,1)S(1)} %copy-done.9), channel_id=1, source_target_pairs={{0,8},{4,12},{8,0},{12,4},{16,24},{20,28},{24,16},{28,20},{1,9},{5... | collective-permute-start | bytes 5013512 | tf_op jit(solution)/shard_map/ppermute | solution.py:40
  393.6 67.5 %collective-permute-start.33 = (bf16[544,1536]{1,0:T(8,128)(2,1)S(1)}, bf16[544,1536]{1,0:T(8,128)(2,1)S(1)}, u32[]{:S(2)}, u32[]{:S(2)}) collective-permute-start(bf16[544,1536]{1,0:T(8,128)(2,1)S(1)} %copy-done.10), channel_id=1, source_target_pairs={{0,2},{1,3},{2,0},{3,1},{4,6},{5,7},{6,4},{7,5},{8,10},{9,11},{10,... | collective-permute-start | bytes 5013512 | tf_op jit(solution)/shard_map/ppermute | solution.py:40
  482.8 312.4 %reduce-scatter.5.cloned.1.call-start = ((), (), s32[]{:S(2)}) async-start(), calls=%async_computation.4 | async-start | bytes 8847360 | tf_op jit(solution)/shard_map/reduce_scatter | solution.py:1187
  486.9 40.2 %collective-permute-start.36 = (bf16[512,1536]{1,0:T(8,128)(2,1)}, bf16[512,1536]{1,0:T(8,128)(2,1)S(1)}, u32[]{:S(2)}, u32[]{:S(2)}) collective-permute-start(bf16[512,1536]{1,0:T(8,128)(2,1)} %shard_map.295.refs_11_), channel_id=1, source_target_pairs={{0,1},{1,0},{2,3},{3,2},{4,5},{5,4},{6,7},{7,6},{8,9},{9,8},{10,11... | collective-permute-start | bytes 4718600 | tf_op jit(solution)/shard_map/ppermute | solution.py:40
  548.8 57.6 %collective-permute-start.46 = (bf16[2,8,192,768]{3,2,1,0:T(8,128)(2,1)}, bf16[2,8,192,768]{3,2,1,0:T(8,128)(2,1)}, u32[]{:S(2)}, u32[]{:S(2)}) collective-permute-start(bf16[2,8,192,768]{3,2,1,0:T(8,128)(2,1)} %get-tuple-element.166), channel_id=1, source_target_pairs={{0,1},{1,0},{2,3},{3,2},{4,5},{5,4},{6,7},{7,6},{8,9},{9,8},{10,11... | collective-permute-start | bytes 14155784 | tf_op jit(solution)/shard_map/ppermute | solution.py:40
  549.2 18.3 %collective-permute-start.35 = (bf16[512,1536]{1,0:T(8,128)(2,1)}, bf16[512,1536]{1,0:T(8,128)(2,1)}, u32[]{:S(2)}, u32[]{:S(2)}) collective-permute-start(bf16[512,1536]{1,0:T(8,128)(2,1)} %shard_map.294.refs_14_), channel_id=1, source_target_pairs={{0,1},{1,0},{2,3},{3,2},{4,5},{5,4},{6,7},{7,6},{8,9},{9,8},{10,11... | collective-permute-start | bytes 4718600 | tf_op jit(solution)/shard_map/ppermute | solution.py:40
  549.3 20.3 %collective-permute-start.40 = (bf16[512,1536]{1,0:T(8,128)(2,1)S(1)}, bf16[512,1536]{1,0:T(8,128)(2,1)S(1)}, u32[]{:S(2)}, u32[]{:S(2)}) collective-permute-start(bf16[512,1536]{1,0:T(8,128)(2,1)S(1)} %copy-done.12), channel_id=1, source_target_pairs={{0,1},{1,0},{2,3},{3,2},{4,5},{5,4},{6,7},{7,6},{8,9},{9,8},{10,11... | collective-permute-start | bytes 4718600 | tf_op jit(solution)/shard_map/ppermute | solution.py:40
  549.8 48.0 %collective-permute-start.37 = (bf16[512,1536]{1,0:T(8,128)(2,1)S(1)}, bf16[512,1536]{1,0:T(8,128)(2,1)}, u32[]{:S(2)}, u32[]{:S(2)}) collective-permute-start(bf16[512,1536]{1,0:T(8,128)(2,1)S(1)} %copy-done.11), channel_id=1, source_target_pairs={{0,1},{1,0},{2,3},{3,2},{4,5},{5,4},{6,7},{7,6},{8,9},{9,8},{10,11... | collective-permute-start | bytes 4718600 | tf_op jit(solution)/shard_map/ppermute | solution.py:40
  565.0 28.6 %collective-permute-start.41 = (bf16[256,1536]{1,0:T(8,128)(2,1)}, bf16[256,1536]{1,0:T(8,128)(2,1)}, u32[]{:S(2)}, u32[]{:S(2)}) collective-permute-start(bf16[256,1536]{1,0:T(8,128)(2,1)} %get-tuple-element.157), channel_id=1, source_target_pairs={{0,8},{4,12},{8,0},{12,4},{16,24},{20,28},{24,16},{28,20},{1,9},{5... | collective-permute-start | bytes 2359304 | tf_op jit(solution)/shard_map/ppermute | solution.py:40
  567.5 30.3 %collective-permute-start.38 = (bf16[256,1536]{1,0:T(8,128)(2,1)}, bf16[256,1536]{1,0:T(8,128)(2,1)S(1)}, u32[]{:S(2)}, u32[]{:S(2)}) collective-permute-start(bf16[256,1536]{1,0:T(8,128)(2,1)} %get-tuple-element.153.refs_3_), channel_id=1, source_target_pairs={{0,2},{1,3},{2,0},{3,1},{4,6},{5,7},{6,4},{7,5},{8,10},{9,11},{10,... | collective-permute-start | bytes 2359304 | tf_op jit(solution)/shard_map/ppermute | solution.py:40
  570.8 32.3 %collective-permute-start.45 = (bf16[512,512]{1,0:T(8,128)(2,1)}, bf16[512,512]{1,0:T(8,128)(2,1)S(1)}, u32[]{:S(2)}, u32[]{:S(2)}) collective-permute-start(bf16[512,512]{1,0:T(8,128)(2,1)} %bitcast.25), channel_id=1, source_target_pairs={{0,2},{1,3},{2,0},{3,1},{4,6},{5,7},{6,4},{7,5},{8,10},{9,11},{10,... | collective-permute-start | bytes 1572872 | tf_op jit(solution)/shard_map/ppermute | solution.py:40
  612.9 91.9 %collective-permute-start.52 = (bf16[1,8,192,768]{3,2,1,0:T(8,128)(2,1)}, bf16[1,8,192,768]{3,2,1,0:T(8,128)(2,1)S(1)}, u32[]{:S(2)}, u32[]{:S(2)}) collective-permute-start(bf16[1,8,192,768]{3,2,1,0:T(8,128)(2,1)} %get-tuple-element.171), channel_id=1, source_target_pairs={{0,2},{1,3},{2,0},{3,1},{4,6},{5,7},{6,4},{7,5},{8,10},{9,11},{10,... | collective-permute-start | bytes 7077896 | tf_op jit(solution)/shard_map/ppermute | solution.py:40
  613.0 97.6 %collective-permute-start.39 = (bf16[512,1536]{1,0:T(8,128)(2,1)}, bf16[512,1536]{1,0:T(8,128)(2,1)}, u32[]{:S(2)}, u32[]{:S(2)}) collective-permute-start(bf16[512,1536]{1,0:T(8,128)(2,1)} %shard_map.303.refs_2_), channel_id=1, source_target_pairs={{0,8},{4,12},{8,0},{12,4},{16,24},{20,28},{24,16},{28,20},{1,9},{5... | collective-permute-start | bytes 4718600 | tf_op jit(solution)/shard_map/ppermute | solution.py:40
  634.4 88.4 %collective-permute-start.42 = (bf16[512,1536]{1,0:T(8,128)(2,1)}, bf16[512,1536]{1,0:T(8,128)(2,1)}, u32[]{:S(2)}, u32[]{:S(2)}) collective-permute-start(bf16[512,1536]{1,0:T(8,128)(2,1)} %shard_map.304.refs_3_), channel_id=1, source_target_pairs={{0,2},{1,3},{2,0},{3,1},{4,6},{5,7},{6,4},{7,5},{8,10},{9,11},{10,... | collective-permute-start | bytes 4718600 | tf_op jit(solution)/shard_map/ppermute | solution.py:40
  636.4 67.4 %collective-permute-start.48 = (f32[40,1536]{1,0:T(8,128)S(1)}, f32[40,1536]{1,0:T(8,128)}, u32[]{:S(2)}, u32[]{:S(2)}) collective-permute-start(f32[40,1536]{1,0:T(8,128)S(1)} %add.96), channel_id=1, source_target_pairs={{0,2},{1,3},{2,0},{3,1},{4,6},{5,7},{6,4},{7,5},{8,10},{9,11},{10,... | collective-permute-start | bytes 737288 | tf_op jit(solution)/shard_map/ppermute | solution.py:40
  640.8 88.0 %collective-permute-start.64 = (bf16[3,192,768]{2,1,0:T(8,128)(2,1)}, bf16[3,192,768]{2,1,0:T(8,128)(2,1)}, u32[]{:S(2)}, u32[]{:S(2)}) collective-permute-start(bf16[3,192,768]{2,1,0:T(8,128)(2,1)} %get-tuple-element.238), channel_id=1, source_target_pairs={{0,8},{4,12},{8,0},{12,4},{16,24},{20,28},{24,16},{28,20},{1,9},{5... | collective-permute-start | bytes 2654216 | tf_op jit(solution)/shard_map/ppermute | solution.py:40
  703.8 15.2 %collective-permute-start.56 = (bf16[2,8,192,128]{3,2,1,0:T(8,128)(2,1)}, bf16[2,8,192,128]{3,2,1,0:T(8,128)(2,1)S(1)}, u32[]{:S(2)}, u32[]{:S(2)}) collective-permute-start(bf16[2,8,192,128]{3,2,1,0:T(8,128)(2,1)} %shard_map.315), channel_id=1, source_target_pairs={{0,1},{1,0},{2,3},{3,2},{4,5},{5,4},{6,7},{7,6},{8,9},{9,8},{10,11... | collective-permute-start | bytes 2359304 | tf_op jit(solution)/shard_map/ppermute | solution.py:40
  710.6 33.3 %collective-permute-start.53 = (bf16[4,192,768]{2,1,0:T(8,128)(2,1)}, bf16[4,192,768]{2,1,0:T(8,128)(2,1)S(1)}, u32[]{:S(2)}, u32[]{:S(2)}) collective-permute-start(bf16[4,192,768]{2,1,0:T(8,128)(2,1)} %get-tuple-element.173), channel_id=1, source_target_pairs={{0,4},{4,0},{8,12},{12,8},{16,20},{20,16},{24,28},{28,24},{1,5},{5... | collective-permute-start | bytes 3538952 | tf_op jit(solution)/shard_map/ppermute | solution.py:40
  714.5 23.5 %collective-permute-start.63 = (bf16[3,192,768]{2,1,0:T(8,128)(2,1)S(1)}, bf16[3,192,768]{2,1,0:T(8,128)(2,1)}, u32[]{:S(2)}, u32[]{:S(2)}) collective-permute-start(bf16[3,192,768]{2,1,0:T(8,128)(2,1)S(1)} %get-tuple-element.240), channel_id=1, source_target_pairs={{0,8},{4,12},{8,0},{12,4},{16,24},{20,28},{24,16},{28,20},{1,9},{5... | collective-permute-start | bytes 2654216 | tf_op jit(solution)/shard_map/ppermute | solution.py:40
  719.1 23.4 %collective-permute-start.50 = (f32[40,1536]{1,0:T(8,128)S(1)}, f32[40,1536]{1,0:T(8,128)S(1)}, u32[]{:S(2)}, u32[]{:S(2)}) collective-permute-start(f32[40,1536]{1,0:T(8,128)S(1)} %add.98), channel_id=1, source_target_pairs={{0,8},{4,12},{8,0},{12,4},{16,24},{20,28},{24,16},{28,20},{1,9},{5... | collective-permute-start | bytes 737288 | tf_op jit(solution)/shard_map/ppermute | solution.py:40
  722.8 28.1 %collective-permute-start.57 = (bf16[1,8,192,128]{3,2,1,0:T(8,128)(2,1)}, bf16[1,8,192,128]{3,2,1,0:T(8,128)(2,1)S(1)}, u32[]{:S(2)}, u32[]{:S(2)}) collective-permute-start(bf16[1,8,192,128]{3,2,1,0:T(8,128)(2,1)} %get-tuple-element.180), channel_id=1, source_target_pairs={{0,2},{1,3},{2,0},{3,1},{4,6},{5,7},{6,4},{7,5},{8,10},{9,11},{10,... | collective-permute-start | bytes 1179656 | tf_op jit(solution)/shard_map/ppermute | solution.py:40
  747.5 42.9 %collective-permute-start.54 = (bf16[2,192,768]{2,1,0:T(8,128)(2,1)}, bf16[2,192,768]{2,1,0:T(8,128)(2,1)S(1)}, u32[]{:S(2)}, u32[]{:S(2)}) collective-permute-start(bf16[2,192,768]{2,1,0:T(8,128)(2,1)} %get-tuple-element.175), channel_id=1, source_target_pairs={{0,8},{4,12},{8,0},{12,4},{16,24},{20,28},{24,16},{28,20},{1,9},{5... | collective-permute-start | bytes 1769480 | tf_op jit(solution)/shard_map/ppermute | solution.py:40
  749.3 50.4 %collective-permute-start.62 = (bf16[3,192,768]{2,1,0:T(8,128)(2,1)}, bf16[3,192,768]{2,1,0:T(8,128)(2,1)}, u32[]{:S(2)}, u32[]{:S(2)}) collective-permute-start(bf16[3,192,768]{2,1,0:T(8,128)(2,1)} %get-tuple-element.242), channel_id=1, source_target_pairs={{0,8},{4,12},{8,0},{12,4},{16,24},{20,28},{24,16},{28,20},{1,9},{5... | collective-permute-start | bytes 2654216 | tf_op jit(solution)/shard_map/ppermute | solution.py:40
  762.9 24.3 %collective-permute-start.59 = (bf16[2,192,128]{2,1,0:T(8,128)(2,1)}, bf16[2,192,128]{2,1,0:T(8,128)(2,1)S(1)}, u32[]{:S(2)}, u32[]{:S(2)}) collective-permute-start(bf16[2,192,128]{2,1,0:T(8,128)(2,1)} %get-tuple-element.184), channel_id=1, source_target_pairs={{0,8},{4,12},{8,0},{12,4},{16,24},{20,28},{24,16},{28,20},{1,9},{5... | collective-permute-start | bytes 294920 | tf_op jit(solution)/shard_map/ppermute | solution.py:40
  793.3 15.3 %collective-permute-start.55 = (bf16[1,192,768]{2,1,0:T(8,128)(2,1)}, bf16[1,192,768]{2,1,0:T(8,128)(2,1)S(1)}, u32[]{:S(2)}, u32[]{:S(2)}) collective-permute-start(bf16[1,192,768]{2,1,0:T(8,128)(2,1)} %get-tuple-element.177), channel_id=1, source_target_pairs={{0,16},{4,20},{8,24},{12,28},{16,0},{20,4},{24,8},{28,12},{1,17},{... | collective-permute-start | bytes 884744 | tf_op jit(solution)/shard_map/ppermute | solution.py:40
  797.7 23.7 %collective-permute-start.61 = (bf16[3,192,768]{2,1,0:T(8,128)(2,1)S(1)}, bf16[3,192,768]{2,1,0:T(8,128)(2,1)S(1)}, u32[]{:S(2)}, u32[]{:S(2)}) collective-permute-start(bf16[3,192,768]{2,1,0:T(8,128)(2,1)S(1)} %get-tuple-element.244), channel_id=1, source_target_pairs={{0,8},{4,12},{8,0},{12,4},{16,24},{20,28},{24,16},{28,20},{1,9},{5... | collective-permute-start | bytes 2654216 | tf_op jit(solution)/shard_map/ppermute | solution.py:40
  (68 other events, 426.2 us)
Sparse Core Ops, SparseCore 0:
  305.2 85.4 reduce-scatter.10
  393.0 85.5 reduce-scatter.8
  482.9 85.4 reduce-scatter.6
  571.6 133.5 reduce-scatter.4

commit v3 on v2

--- a/solution.py
+++ b/solution.py
@@ -832,7 +832,7 @@
     )
 
 
-def reduce_grad(keep, send, steps, after=(), marks=None):
+def reduce_grad(keep, send, steps, after=(), marks=None, late=None):
     outer = keep.shape[0].bit_length()
     arrived = swap(send, *steps[0])
     for at in range(1, len(steps)):
@@ -841,6 +841,8 @@
         keep, send = add_split(keep, arrived, 0, False, after if at == 1 else ())
         if marks is not None:
             marks.append(keep)
+        if late is not None and steps[at] == ("dp", TEAM_BIT):
+            send = hold(send, late(keep))
         arrived = swap(send, *steps[at])
     return keep[0].astype(F32) + arrived[0].astype(F32)
 
@@ -920,7 +922,7 @@
         out_ref[low:high, :] = total.astype(BF16)
 
 
-def layer_output(residual, terms):
+def layer_output(residual, terms, after=()):
     out = shaped(residual.shape, BF16)
     return kernel_call(
         5,
@@ -928,6 +930,7 @@
         (1,),
         [(a, whole(a)) for a in [residual] + [t for t, _ in terms]],
         [(out, whole(out))],
+        after=after,
     )[0]
 
 
@@ -1150,7 +1153,7 @@
     chunk = 8
     for e in range(team_count):
         expert = (first_local + e).reshape(1).astype(jnp.int32)
-        joint = int(e == 3)
+        joint = 0
         parts = []
         for start in range(0, len(u_rows), chunk):
             span = slice(start, start + chunk)
@@ -1178,7 +1181,7 @@
     def advance(e, after):
         if e >= team_count:
             return list(after)
-        if e == 3:
+        if joint:
             ranks = [
                 sum(bit for at, bit in enumerate(d_order[:-1]) if (n_dp // 4 >> at) & r)
                 for r in range(n_dp // 2)
@@ -1237,7 +1240,7 @@
             )
         )
 
-    marks = advance(3, advance(2, [d_mix]))
+    marks = advance(2, [d_mix])
 
     def out_rows(at, added, cut_at, after):
         return combine(outs, at, places, None, first_expert, added, cut_at, 0, after)
@@ -1260,14 +1263,26 @@
         other = swap(result[1], *team)
         settled.append(settle(result[0], other, slots, local_count, totals, after))
 
-    marks = [dq]
+    marks, corners = [dq], []
     if split:
         low, high = out_rows(3, [(sent[3], 0)], cut, marks)
-        from_y, from_z = swap(low, *far), swap(high, *team)
+        from_y, from_z = corners = swap(low, *far), swap(high, *team)
         marks = [low]
     add_weight(mix, d_branch, 2 * q_part, 0, marks)
     add_weight(normed, dq, 2 * q_part, q_part, [])
-    marks = w_parts[-1][:1]
+    last_step = e_steps[0]
+    halves = [scatter_pieces(d_kv[at::2], e_steps[1:]) for at in range(2)]
+    held, far_half = (h.reshape(row_count, 2 * kv_width) for h in halves)
+    arrived = hold(swap(far_half, *last_step), [w_parts[-1][0], *corners])
+    d_kv_own, joined = key_value_back(held, arrived, cos_wide, sin_wide, members)
+    marks = advance(3, [d_kv_own])
+    if q_part % 128 == 0:
+        w_keep, w_send = w_parts[1]
+    else:
+        w_keep, w_send = (jnp.concatenate([p[i] for p in w_parts], axis=3) for i in range(2))
+    w_marks = []
+    grads = reduce_grad(w_keep, w_send, w_steps, marks, w_marks)
+    marks = w_marks[:1]
     if split:
         own = out_rows(0, [(sent[0], 0)], 0, marks)[0]
         over_z = out_rows(1, [(sent[1], 0), (from_y, 0)], 0, marks)[0]
@@ -1276,29 +1291,29 @@
         marks = [own, over_z, over_y]
     else:
         out_terms = scatter_team(lambda at, added, cut_at: out_rows(at, added, cut_at, marks))
-    last_step = e_steps[0]
-    halves = [scatter_pieces(d_kv[at::2], e_steps[1:]) for at in range(2)]
-    held, far_half = (h.reshape(row_count, 2 * kv_width) for h in halves)
-    arrived = hold(swap(far_half, *last_step), marks)
-    d_kv_own, joined = key_value_back(held, arrived, cos_wide, sin_wide, members)
-    if q_part % 128 == 0:
-        w_keep, w_send = w_parts[1]
-    else:
-        w_keep, w_send = (jnp.concatenate([p[i] for p in w_parts], axis=3) for i in range(2))
-    w_marks = []
-    grads = reduce_grad(w_keep, w_send, w_steps, [d_kv_own], w_marks)
-    add_weight(normed, joined, 2 * kv_part, 0, w_marks[:1])
+    add_weight(normed, joined, 2 * kv_part, 0, [])
     d_hidden, sums = finish(
         dq, d_kv_own, w_query, w_key, w_value, x, d_residual, gain_one, small, [w_parts[-1][0]]
     )
-    later = [d_hidden]
-    output = layer_output(residual, out_terms)
+    output = layer_output(residual, out_terms, [d_hidden, *w_marks[1:2]])
+    sums = all_sum(hold(sums, [output]), ("expert",))
+    sums = sums + swap(sums, "dp", w_order[0])
+    early = max(1, team_count - 1)
+
+    def late(mark):
+        if not settled:
+            for e in range(early):
+                settle_expert(e, [d_hidden], [sums, mark])
+        return settled[-1][:1]
+
     kv_keep, kv_send = w_parts[2]
-    kv_grads = reduce_grad(kv_keep, hold(kv_send, later), w_steps)
-    sums = all_sum(hold(sums, later), ("expert", "dp"))
-
-    for e in range(len(settled), team_count):
-        settle_expert(e, [dq] if e < 2 else [output], [output])
+    kv_grads = reduce_grad(kv_keep, hold(kv_send, [output]), w_steps, late=late)
+    sums = hold(sums, late(output))
+    for bit in w_order[1:]:
+        sums = sums + swap(sums, "dp", bit)
+
+    for e in range(early, team_count):
+        settle_expert(e, [output], [])
     grad_gate, grad_up, grad_down = settled[-1]
     return (
         output.reshape(group_count, span_len, width),

time: 845 us -> 840 us (level)
    ppermute x65 -> x66, waiting for transfers between devices: 297 us -> 291 us  [swap(): return lax.ppermute(values, axis_name, [(i, i ^ bit) for i in range(count)])]
    pallas_call x82 -> x84, Pallas kernels: 407 us -> 412 us  [kernel_call(): pl.pallas_call(run, grid_spec=grid_spec, out_shape=[shape for shape, _ in...]
    unnamed x99 -> x87, local copies, waits for them, and re-layouts: 30.9 us -> 29.2 us
    ppermute x65 -> x66, starting transfers between devices: 48.1 us -> 46.4 us  [swap(): return lax.ppermute(values, axis_name, [(i, i ^ bit) for i in range(count)])]
  transfers between devices with their start and end apart: 69 -> 70, of which waited for: 21 -> 26; matrix products, arithmetic and copies ran while one was open for 4% -> 4% of each run, Pallas kernels for 44% -> 45%
where the time goes in v3:
time: 840 us; the launch traced here: 829 us
  Pallas kernels  412 us (49%)
  waiting for transfers between devices  291 us (35%)
  local copies, waits for them, and re-layouts  52.7 us (6%)
  starting transfers between devices  46.5 us (6%)
  between operations  14.5 us (2%)
  other arithmetic  12.3 us (1%)
    pallas_call x84, Pallas kernels, kernel_call(): pl.pallas_call(run, grid_spec=grid_spec, out_shape=[shape for shape, _ in...  412 us
    ppermute x66, waiting for transfers between devices, swap(): return lax.ppermute(values, axis_name, [(i, i ^ bit) for i in range(count)])  291 us
    ppermute x66, starting transfers between devices, swap(): return lax.ppermute(values, axis_name, [(i, i ^ bit) for i in range(count)])  46.4 us
    unnamed x87, local copies, waits for them, and re-layouts  29.2 us
  transfers between devices with their start and end apart: 70, of which 26 were waited for; matrix products, arithmetic and copies ran while one was open for 4% of the time, Pallas kernels for 45%

profile of v3, /device:TPU:0, one launch (start us, length us, event | category | flops | bytes accessed | tf_op | source)
XLA Modules:
  0.0 829.0 jit_solution(11376857751585394374)
XLA Ops:
  13.4 4.3 shard_map.247
  24.6 8.9 %collective-permute-done.1 = s32[2,5,512]{2,1,0:T(8,128)S(1)} collective-permute-done((s32[2,5,512]{2,1,0:T(8,128)S(1)}, s32[2,5,512]{2,1,0:T(8,128)S(1)}, u32[]{:S(2)}, u32[]{:S(2)}) %collective-permute-start.1) | collective-permute-done | bytes 20512 | tf_op jit(solution)/shard_map/ppermute | solution.py:40
  44.7 7.7 shard_map.248
  52.4 15.7 %shard_map.249 = (bf16[2,256,1536]{2,1,0:T(8,128)(2,1)}, f32[2,256,12]{2,1,0:T(8,128)}) custom-call(s32[2]{0:T(128)} %refs_0_.3, s32[5]{0:T(128)} %pad_add_fusion.3.refs_1_, bf16[2,256,1536]{2,1,0:T(8,128)(2,1)} %bitcast.68, bf16[2,256,512]{2,1,0:T(8,128)(2,1)} %bitcast.91, bf16[2,256,512]{2,1,0:T(8,128)(2,1)} %copy-done.15, ...), custom_call_target="tpu_custom_call" | custom-call | flops 157000000 | bytes 518100 | tf_op jit(solution)/shard_map/pallas_call | solution.py:91
  68.1 7.4 shard_map.252.refs_8_.refs_1_.refs_2_.refs_3_.refs_4_.refs_5_
  76.6 10.3 %shard_map.253 = (f32[512,1536]{1,0:T(8,128)}, bf16[544,1536]{1,0:T(8,128)(2,1)}, f32[32,512]{1,0:T(8,128)}) custom-call(bf16[512,1536]{1,0:T(8,128)(2,1)} %bitcast.74, bf16[512,1536]{1,0:T(8,128)(2,1)} %bitcast.77, bf16[1536,1536]{1,0:T(8,128)(2,1)} %refs_9_.1, f32[1,1536]{1,0:T(1,128)} %reshape.128.refs_3_.refs_5_, bf16[32,1536]{1,0:T(8,128)(2,1)} %bitcast.98, ...), custom_call_target="tpu_custom_call" | custom-call | flops 100000000 | bytes 330000 | tf_op jit(solution)/shard_map/pallas_call | solution.py:91
  113.6 12.6 %collective-permute-done.11.refs_0_ = bf16[544,1536]{1,0:T(8,128)(2,1)S(1)} collective-permute-done((bf16[544,1536]{1,0:T(8,128)(2,1)}, bf16[544,1536]{1,0:T(8,128)(2,1)S(1)}, u32[]{:S(2)}, u32[]{:S(2)}) %collective-permute-start.11) | collective-permute-done | bytes 1671200 | tf_op jit(solution)/shard_map/ppermute | solution.py:40
  153.4 16.7 %collective-permute-done.18.refs_0_ = bf16[256,1536]{1,0:T(8,128)(2,1)} collective-permute-done((bf16[256,1536]{1,0:T(8,128)(2,1)}, bf16[256,1536]{1,0:T(8,128)(2,1)}, u32[]{:S(2)}, u32[]{:S(2)}) %collective-permute-start.18) | collective-permute-done | bytes 786464 | tf_op jit(solution)/shard_map/ppermute | solution.py:40
  190.1 26.8 %shard_map.278 = (bf16[8,80,1536]{2,1,0:T(8,128)(2,1)}, bf16[8,80,1536]{2,1,0:T(8,128)(2,1)}, f32[8,80,128]{2,1,0:T(8,128)}, bf16[4,3,192,768]{3,2,1,0:T(8,128)(2,1)}, bf16[4,3,192,768]{3,2,1,0:T(8,128)(2,1)}) custom-call(s32[1]{0:T(128)} %bitcast.14.refs_0_, s32[1]{0:T(128)} %bitcast.15.refs_1_, bf16[4,80,1536]{2,1,0:T(8,128)(2,1)} %get-tuple-element.113.refs_4_.refs_2_, ...), custom_call_target="tpu_custom_call" | custom-call | flops 265000000 | bytes 874500 | tf_op jit(solution)/shard_map/pallas_call | solution.py:91
  218.5 26.4 %shard_map.279 = (bf16[8,80,1536]{2,1,0:T(8,128)(2,1)}, bf16[8,80,1536]{2,1,0:T(8,128)(2,1)}, f32[8,80,128]{2,1,0:T(8,128)}, bf16[4,3,192,768]{3,2,1,0:T(8,128)(2,1)}, bf16[4,3,192,768]{3,2,1,0:T(8,128)(2,1)}) custom-call(s32[1]{0:T(128)} %bitcast.16.refs_0_, s32[1]{0:T(128)} %bitcast.15.refs_1_, bf16[4,80,1536]{2,1,0:T(8,128)(2,1)} %get-tuple-element.113.refs_4_.refs_2_, ...), custom_call_target="tpu_custom_call" | custom-call | flops 265000000 | bytes 874500 | tf_op jit(solution)/shard_map/pallas_call | solution.py:91
  244.9 26.4 %shard_map.280 = (bf16[8,80,1536]{2,1,0:T(8,128)(2,1)}, bf16[8,80,1536]{2,1,0:T(8,128)(2,1)}, f32[8,80,128]{2,1,0:T(8,128)}, bf16[4,3,192,768]{3,2,1,0:T(8,128)(2,1)}, bf16[4,3,192,768]{3,2,1,0:T(8,128)(2,1)}) custom-call(s32[1]{0:T(128)} %bitcast.17.refs_0_, s32[1]{0:T(128)} %bitcast.15.refs_1_, bf16[4,80,1536]{2,1,0:T(8,128)(2,1)} %get-tuple-element.113.refs_4_.refs_2_, ...), custom_call_target="tpu_custom_call" | custom-call | flops 265000000 | bytes 874500 | tf_op jit(solution)/shard_map/pallas_call | solution.py:91
  271.3 26.6 %shard_map.281 = (bf16[8,80,1536]{2,1,0:T(8,128)(2,1)}, bf16[8,80,1536]{2,1,0:T(8,128)(2,1)}, f32[8,80,128]{2,1,0:T(8,128)}, bf16[4,3,192,768]{3,2,1,0:T(8,128)(2,1)}, bf16[4,3,192,768]{3,2,1,0:T(8,128)(2,1)}) custom-call(s32[1]{0:T(128)} %bitcast.18.refs_0_, s32[1]{0:T(128)} %bitcast.15.refs_1_, bf16[4,80,1536]{2,1,0:T(8,128)(2,1)} %get-tuple-element.113.refs_4_.refs_2_, ...), custom_call_target="tpu_custom_call" | custom-call | flops 265000000 | bytes 874500 | tf_op jit(solution)/shard_map/pallas_call | solution.py:91
  299.7 5.5 shard_map.282.refs_10_
  321.5 4.1 shard_map.287
  326.8 4.2 shard_map.284.refs_2_.refs_0_
  331.0 15.0 %collective-permute-done.29.refs_11_ = bf16[256,1536]{1,0:T(8,128)(2,1)} collective-permute-done((bf16[256,1536]{1,0:T(8,128)(2,1)}, bf16[256,1536]{1,0:T(8,128)(2,1)}, u32[]{:S(2)}, u32[]{:S(2)}) %collective-permute-start.29) | collective-permute-done | bytes 786464 | tf_op jit(solution)/shard_map/ppermute | solution.py:40
  346.0 4.5 shard_map.288.refs_3_
  350.5 15.0 %collective-permute-done.32.refs_11_ = bf16[288,1536]{1,0:T(8,128)(2,1)} collective-permute-done((bf16[288,1536]{1,0:T(8,128)(2,1)}, bf16[288,1536]{1,0:T(8,128)(2,1)}, u32[]{:S(2)}, u32[]{:S(2)}) %collective-permute-start.32) | collective-permute-done | bytes 884768 | tf_op jit(solution)/shard_map/ppermute | solution.py:40
  365.5 4.5 shard_map.290.refs_4_
  370.0 13.8 %collective-permute-done.34.refs_1_ = bf16[4,3,192,768]{3,2,1,0:T(8,128)(2,1)S(1)} collective-permute-done((bf16[4,3,192,768]{3,2,1,0:T(8,128)(2,1)}, bf16[4,3,192,768]{3,2,1,0:T(8,128)(2,1)S(1)}, u32[]{:S(2)}, u32[]{:S(2)}) %collective-permute-start.34) | collective-permute-done | bytes 3538976 | tf_op jit(solution)/shard_map/ppermute | solution.py:40
  385.6 5.4 shard_map.291.refs_10_
  394.1 66.9 %collective-permute-done.30.refs_1_ = bf16[544,1536]{1,0:T(8,128)(2,1)S(1)} collective-permute-done((bf16[544,1536]{1,0:T(8,128)(2,1)S(1)}, bf16[544,1536]{1,0:T(8,128)(2,1)S(1)}, u32[]{:S(2)}, u32[]{:S(2)}) %collective-permute-start.30) | collective-permute-done | bytes 1671200 | tf_op jit(solution)/shard_map/ppermute | solution.py:40
  463.4 13.8 %shard_map.292 = (f32[512,1536]{1,0:T(8,128)}, bf16[512,1536]{1,0:T(8,128)(2,1)}, bf16[512,1536]{1,0:T(8,128)(2,1)}, f32[40,1536]{1,0:T(8,128)}) custom-call(bf16[544,1536]{1,0:T(8,128)(2,1)} %shard_map.284.refs_2_.refs_0_, bf16[544,1536]{1,0:T(8,128)(2,1)} %copy-done.24, bf16[544,1536]{1,0:T(8,128)(2,1)} %copy-done.25, ...), custom_call_target="tpu_custom_call" | custom-call | flops 138000000 | bytes 455400 | tf_op jit(solution)/shard_map/pallas_call | solution.py:91
  477.2 5.5 shard_map.293.refs_6_
  497.8 28.6 %shard_map.298 = (bf16[2,256,1536]{2,1,0:T(8,128)(2,1)}, bf16[2,256,512]{2,1,0:T(8,128)(2,1)}, bf16[2,256,512]{2,1,0:T(8,128)(2,1)}, bf16[2,256,512]{2,1,0:T(8,128)(2,1)}, bf16[2,256,512]{2,1,0:T(8,128)(2,1)}) custom-call(s32[2]{0:T(128)} %refs_0_.3, s32[5]{0:T(128)} %pad_add_fusion.3.refs_1_, bf16[2,256,1536]{2,1,0:T(8,128)(2,1)} %bitcast.69, ...), custom_call_target="tpu_custom_call" | custom-call | flops 286000000 | bytes 943800 | tf_op jit(solution)/shard_map/pallas_call | solution.py:91
  530.4 8.2 shard_map.300
  538.7 8.3 shard_map.301
  547.9 6.4 collective-permute-done.40
  558.5 20.4 %collective-permute-done.41.refs_0_ = bf16[512,512]{1,0:T(8,128)(2,1)S(1)} collective-permute-done((bf16[512,512]{1,0:T(8,128)(2,1)S(1)}, bf16[512,512]{1,0:T(8,128)(2,1)S(1)}, u32[]{:S(2)}, u32[]{:S(2)}) %collective-permute-start.41) | collective-permute-done | bytes 524320 | tf_op jit(solution)/shard_map/ppermute | solution.py:40
  578.9 4.6 collective-permute-done.43.refs_3_.refs_7_
  587.9 5.5 shard_map.304.refs_4_
  594.0 6.6 shard_map.305
  602.3 4.2 shard_map.307
  606.5 4.2 shard_map.308
  611.1 6.0 shard_map.309
  617.1 12.5 %shard_map.310 = (f32[512,1536]{1,0:T(8,128)}, f32[40,1536]{1,0:T(8,128)}) custom-call(bf16[512,1536]{1,0:T(8,128)(2,1)} %bitcast.72, bf16[512,512]{1,0:T(8,128)(2,1)} %get-tuple-element.166.refs_2_.refs_1_, bf16[1536,1536]{1,0:T(8,128)(2,1)} %refs_2_.5, bf16[1536,256]{1,0:T(8,128)(2,1)} %refs_3_.3, bf16[1536,256]{1,0:T(8,128)(2,1)} %refs_4_.1, ...), custom_call_target="tpu_custom_call" | custom-call | flops 130000000 | bytes 429000 | tf_op jit(solution)/shard_map/pallas_call | solution.py:91
  633.7 21.2 %collective-permute-done.48 = bf16[1,8,192,768]{3,2,1,0:T(8,128)(2,1)S(1)} collective-permute-done((bf16[1,8,192,768]{3,2,1,0:T(8,128)(2,1)}, bf16[1,8,192,768]{3,2,1,0:T(8,128)(2,1)S(1)}, u32[]{:S(2)}, u32[]{:S(2)}) %collective-permute-start.48) | collective-permute-done | bytes 2359328 | tf_op jit(solution)/shard_map/ppermute | solution.py:40
  656.3 4.4 shard_map.311
  660.6 19.7 %collective-permute-done.45.refs_2_ = bf16[512,1536]{1,0:T(8,128)(2,1)} collective-permute-done((bf16[512,1536]{1,0:T(8,128)(2,1)}, bf16[512,1536]{1,0:T(8,128)(2,1)}, u32[]{:S(2)}, u32[]{:S(2)}) %collective-permute-start.45) | collective-permute-done | bytes 1572896 | tf_op jit(solution)/shard_map/ppermute | solution.py:40
  680.3 7.7 collective-permute-done.47.refs_3_
  688.0 5.1 shard_map.312.refs_1_
  713.0 6.4 collective-permute-done.56
  723.6 10.4 %collective-permute-done.51 = f32[40,1536]{1,0:T(8,128)S(1)} collective-permute-done((f32[40,1536]{1,0:T(8,128)S(1)}, f32[40,1536]{1,0:T(8,128)S(1)}, u32[]{:S(2)}, u32[]{:S(2)}) %collective-permute-start.51) | collective-permute-done | bytes 245792 | tf_op jit(solution)/shard_map/ppermute | solution.py:40
  746.0 4.1 shard_map.321
  750.1 4.1 shard_map.322
  767.1 15.6 %collective-permute-done.63.refs_1_.refs_3_ = bf16[2,192,128]{2,1,0:T(8,128)(2,1)S(1)} collective-permute-done((bf16[2,192,128]{2,1,0:T(8,128)(2,1)}, bf16[2,192,128]{2,1,0:T(8,128)(2,1)S(1)}, u32[]{:S(2)}, u32[]{:S(2)}) %collective-permute-start.63) | collective-permute-done | bytes 98336 | tf_op jit(solution)/shard_map/ppermute | solution.py:40
  788.5 5.6 collective-permute-done.64
  808.1 12.2 %collective-permute-done.62 = bf16[1,192,768]{2,1,0:T(8,128)(2,1)S(1)} collective-permute-done((bf16[1,192,768]{2,1,0:T(8,128)(2,1)}, bf16[1,192,768]{2,1,0:T(8,128)(2,1)S(1)}, u32[]{:S(2)}, u32[]{:S(2)}) %collective-permute-start.62) | collective-permute-done | bytes 294944 | tf_op jit(solution)/shard_map/ppermute | solution.py:40
  (312 shorter events, 234.6 us)
Async XLA Ops:
  7.2 685.9 %reduce-scatter.9.cloned.1.call-start = ((), (), s32[]{:S(2)}) async-start(), calls=%async_computation.6 | async-start | bytes 5308416 | tf_op jit(solution)/shard_map/reduce_scatter | solution.py:1197
  17.7 19.5 %collective-permute-start.3 = (bf16[2,256,512]{2,1,0:T(8,128)(2,1)}, bf16[2,256,512]{2,1,0:T(8,128)(2,1)S(1)}, u32[]{:S(2)}, u32[]{:S(2)}) collective-permute-start(bf16[2,256,512]{2,1,0:T(8,128)(2,1)} %bitcast.89), channel_id=1, source_target_pairs={{0,2},{1,3},{2,0},{3,1},{4,6},{5,7},{6,4},{7,5},{8,10},{9,11},{10,... | collective-permute-start | bytes 1572872 | tf_op jit(solution)/shard_map/ppermute | solution.py:40
  35.4 40.1 %collective-permute-start.6 = (bf16[512,1536]{1,0:T(8,128)(2,1)}, bf16[512,1536]{1,0:T(8,128)(2,1)S(1)}, u32[]{:S(2)}, u32[]{:S(2)}) collective-permute-start(bf16[512,1536]{1,0:T(8,128)(2,1)} %shard_map.250), channel_id=1, source_target_pairs={{0,8},{4,12},{8,0},{12,4},{16,24},{20,28},{24,16},{28,20},{1,9},{5... | collective-permute-start | bytes 4718600 | tf_op jit(solution)/shard_map/ppermute | solution.py:40
  38.0 37.5 %collective-permute-start.7 = (bf16[512,1536]{1,0:T(8,128)(2,1)}, bf16[512,1536]{1,0:T(8,128)(2,1)}, u32[]{:S(2)}, u32[]{:S(2)}) collective-permute-start(bf16[512,1536]{1,0:T(8,128)(2,1)} %shard_map.251), channel_id=1, source_target_pairs={{0,2},{1,3},{2,0},{3,1},{4,6},{5,7},{6,4},{7,5},{8,10},{9,11},{10,... | collective-permute-start | bytes 4718600 | tf_op jit(solution)/shard_map/ppermute | solution.py:40
  39.6 48.9 %collective-permute-start.10 = (bf16[512,1536]{1,0:T(8,128)(2,1)S(1)}, bf16[512,1536]{1,0:T(8,128)(2,1)}, u32[]{:S(2)}, u32[]{:S(2)}) collective-permute-start(bf16[512,1536]{1,0:T(8,128)(2,1)S(1)} %bitcast.66), channel_id=1, source_target_pairs={{0,1},{1,0},{2,3},{3,2},{4,5},{5,4},{6,7},{7,6},{8,9},{9,8},{10,11... | collective-permute-start | bytes 4718600 | tf_op jit(solution)/shard_map/ppermute | solution.py:40
  86.9 23.4 %collective-permute-start.12 = (bf16[544,1536]{1,0:T(8,128)(2,1)}, bf16[544,1536]{1,0:T(8,128)(2,1)}, u32[]{:S(2)}, u32[]{:S(2)}) collective-permute-start(bf16[544,1536]{1,0:T(8,128)(2,1)} %get-tuple-element.112.refs_1_.refs_2_.refs_8_), channel_id=1, source_target_pairs={{0,1},{1,0},{2,3},{3,2},{4,5},{5,4},{6,7},{7,6},{8,9},{9,8},{10,11... | collective-permute-start | bytes 5013512 | tf_op jit(solution)/shard_map/ppermute | solution.py:40
  87.5 38.7 %collective-permute-start.11 = (bf16[544,1536]{1,0:T(8,128)(2,1)}, bf16[544,1536]{1,0:T(8,128)(2,1)S(1)}, u32[]{:S(2)}, u32[]{:S(2)}) collective-permute-start(bf16[544,1536]{1,0:T(8,128)(2,1)} %get-tuple-element.112.refs_1_.refs_2_.refs_8_), channel_id=1, source_target_pairs={{0,8},{4,12},{8,0},{12,4},{16,24},{20,28},{24,16},{28,20},{1,9},{5... | collective-permute-start | bytes 5013512 | tf_op jit(solution)/shard_map/ppermute | solution.py:40
  87.9 16.0 %collective-permute-start.8 = (bf16[512,1536]{1,0:T(8,128)(2,1)}, bf16[512,1536]{1,0:T(8,128)(2,1)}, u32[]{:S(2)}, u32[]{:S(2)}) collective-permute-start(bf16[512,1536]{1,0:T(8,128)(2,1)} %shard_map.254.refs_1_), channel_id=1, source_target_pairs={{0,1},{1,0},{2,3},{3,2},{4,5},{5,4},{6,7},{7,6},{8,9},{9,8},{10,11... | collective-permute-start | bytes 4718600 | tf_op jit(solution)/shard_map/ppermute | solution.py:40
  88.5 38.9 %collective-permute-start.13 = (bf16[544,1536]{1,0:T(8,128)(2,1)}, bf16[544,1536]{1,0:T(8,128)(2,1)S(1)}, u32[]{:S(2)}, u32[]{:S(2)}) collective-permute-start(bf16[544,1536]{1,0:T(8,128)(2,1)} %get-tuple-element.112.refs_1_.refs_2_.refs_8_), channel_id=1, source_target_pairs={{0,2},{1,3},{2,0},{3,1},{4,6},{5,7},{6,4},{7,5},{8,10},{9,11},{10,... | collective-permute-start | bytes 5013512 | tf_op jit(solution)/shard_map/ppermute | solution.py:40
  128.6 21.6 %collective-permute-start.16 = (bf16[544,1536]{1,0:T(8,128)(2,1)}, bf16[544,1536]{1,0:T(8,128)(2,1)}, u32[]{:S(2)}, u32[]{:S(2)}) collective-permute-start(bf16[544,1536]{1,0:T(8,128)(2,1)} %shard_map.266.refs_1_.refs_2_), channel_id=1, source_target_pairs={{0,1},{1,0},{2,3},{3,2},{4,5},{5,4},{6,7},{7,6},{8,9},{9,8},{10,11... | collective-permute-start | bytes 5013512 | tf_op jit(solution)/shard_map/ppermute | solution.py:40
  131.2 41.9 %collective-permute-start.19 = (bf16[288,1536]{1,0:T(8,128)(2,1)}, bf16[288,1536]{1,0:T(8,128)(2,1)S(1)}, u32[]{:S(2)}, u32[]{:S(2)}) collective-permute-start(bf16[288,1536]{1,0:T(8,128)(2,1)} %slice.84), channel_id=1, source_target_pairs={{0,8},{4,12},{8,0},{12,4},{16,24},{20,28},{24,16},{28,20},{1,9},{5... | collective-permute-start | bytes 2654216 | tf_op jit(solution)/shard_map/ppermute | solution.py:40
  134.2 35.8 %collective-permute-start.18 = (bf16[256,1536]{1,0:T(8,128)(2,1)}, bf16[256,1536]{1,0:T(8,128)(2,1)}, u32[]{:S(2)}, u32[]{:S(2)}) collective-permute-start(bf16[256,1536]{1,0:T(8,128)(2,1)} %slice.83), channel_id=1, source_target_pairs={{0,8},{4,12},{8,0},{12,4},{16,24},{20,28},{24,16},{28,20},{1,9},{5... | collective-permute-start | bytes 2359304 | tf_op jit(solution)/shard_map/ppermute | solution.py:40
  136.3 33.8 %collective-permute-start.15 = (bf16[256,1536]{1,0:T(8,128)(2,1)}, bf16[256,1536]{1,0:T(8,128)(2,1)}, u32[]{:S(2)}, u32[]{:S(2)}) collective-permute-start(bf16[256,1536]{1,0:T(8,128)(2,1)} %slice.82), channel_id=1, source_target_pairs={{0,2},{1,3},{2,0},{3,1},{4,6},{5,7},{6,4},{7,5},{8,10},{9,11},{10,... | collective-permute-start | bytes 2359304 | tf_op jit(solution)/shard_map/ppermute | solution.py:40
  138.9 35.6 %collective-permute-start.14 = (bf16[256,1536]{1,0:T(8,128)(2,1)}, bf16[256,1536]{1,0:T(8,128)(2,1)S(1)}, u32[]{:S(2)}, u32[]{:S(2)}) collective-permute-start(bf16[256,1536]{1,0:T(8,128)(2,1)} %slice.81), channel_id=1, source_target_pairs={{0,2},{1,3},{2,0},{3,1},{4,6},{5,7},{6,4},{7,5},{8,10},{9,11},{10,... | collective-permute-start | bytes 2359304 | tf_op jit(solution)/shard_map/ppermute | solution.py:40
  216.9 81.0 %collective-permute-start.25 = (bf16[4,3,192,768]{3,2,1,0:T(8,128)(2,1)}, bf16[4,3,192,768]{3,2,1,0:T(8,128)(2,1)S(1)}, u32[]{:S(2)}, u32[]{:S(2)}) collective-permute-start(bf16[4,3,192,768]{3,2,1,0:T(8,128)(2,1)} %get-tuple-element.144), channel_id=1, source_target_pairs={{0,4},{4,0},{8,12},{12,8},{16,20},{20,16},{24,28},{28,24},{1,5},{5... | collective-permute-start | bytes 10616840 | tf_op jit(solution)/shard_map/ppermute | solution.py:40
  305.2 390.7 %reduce-scatter.7.cloned.1.call-start = ((), (), s32[]{:S(2)}) async-start(), calls=%async_computation.5 | async-start | bytes 5308416 | tf_op jit(solution)/shard_map/reduce_scatter | solution.py:1197
  305.2 78.6 %collective-permute-start.34 = (bf16[4,3,192,768]{3,2,1,0:T(8,128)(2,1)}, bf16[4,3,192,768]{3,2,1,0:T(8,128)(2,1)S(1)}, u32[]{:S(2)}, u32[]{:S(2)}) collective-permute-start(bf16[4,3,192,768]{3,2,1,0:T(8,128)(2,1)} %get-tuple-element.149), channel_id=1, source_target_pairs={{0,4},{4,0},{8,12},{12,8},{16,20},{20,16},{24,28},{28,24},{1,5},{5... | collective-permute-start | bytes 10616840 | tf_op jit(solution)/shard_map/ppermute | solution.py:40
  313.3 13.2 %collective-permute-start.26 = (bf16[544,1536]{1,0:T(8,128)(2,1)}, bf16[544,1536]{1,0:T(8,128)(2,1)}, u32[]{:S(2)}, u32[]{:S(2)}) collective-permute-start(bf16[544,1536]{1,0:T(8,128)(2,1)} %shard_map.283), channel_id=1, source_target_pairs={{0,1},{1,0},{2,3},{3,2},{4,5},{5,4},{6,7},{7,6},{8,9},{9,8},{10,11... | collective-permute-start | bytes 5013512 | tf_op jit(solution)/shard_map/ppermute | solution.py:40
  317.4 13.6 %collective-permute-start.27 = (bf16[544,1536]{1,0:T(8,128)(2,1)}, bf16[544,1536]{1,0:T(8,128)(2,1)}, u32[]{:S(2)}, u32[]{:S(2)}) collective-permute-start(bf16[544,1536]{1,0:T(8,128)(2,1)} %shard_map.285), channel_id=1, source_target_pairs={{0,1},{1,0},{2,3},{3,2},{4,5},{5,4},{6,7},{7,6},{8,9},{9,8},{10,11... | collective-permute-start | bytes 5013512 | tf_op jit(solution)/shard_map/ppermute | solution.py:40
  320.9 29.5 %collective-permute-start.31 = (bf16[544,1536]{1,0:T(8,128)(2,1)}, bf16[544,1536]{1,0:T(8,128)(2,1)}, u32[]{:S(2)}, u32[]{:S(2)}) collective-permute-start(bf16[544,1536]{1,0:T(8,128)(2,1)} %shard_map.289), channel_id=1, source_target_pairs={{0,1},{1,0},{2,3},{3,2},{4,5},{5,4},{6,7},{7,6},{8,9},{9,8},{10,11... | collective-permute-start | bytes 5013512 | tf_op jit(solution)/shard_map/ppermute | solution.py:40
  325.6 39.9 %collective-permute-start.32 = (bf16[288,1536]{1,0:T(8,128)(2,1)}, bf16[288,1536]{1,0:T(8,128)(2,1)}, u32[]{:S(2)}, u32[]{:S(2)}) collective-permute-start(bf16[288,1536]{1,0:T(8,128)(2,1)} %get-tuple-element.146), channel_id=1, source_target_pairs={{0,8},{4,12},{8,0},{12,4},{16,24},{20,28},{24,16},{28,20},{1,9},{5... | collective-permute-start | bytes 2654216 | tf_op jit(solution)/shard_map/ppermute | solution.py:40
  326.5 19.5 %collective-permute-start.29 = (bf16[256,1536]{1,0:T(8,128)(2,1)}, bf16[256,1536]{1,0:T(8,128)(2,1)}, u32[]{:S(2)}, u32[]{:S(2)}) collective-permute-start(bf16[256,1536]{1,0:T(8,128)(2,1)} %get-tuple-element.145), channel_id=1, source_target_pairs={{0,2},{1,3},{2,0},{3,1},{4,6},{5,7},{6,4},{7,5},{8,10},{9,11},{10,... | collective-permute-start | bytes 2359304 | tf_op jit(solution)/shard_map/ppermute | solution.py:40
  391.1 309.6 %reduce-scatter.5.cloned.1.call-start = ((), (), s32[]{:S(2)}) async-start(), calls=%async_computation.4 | async-start | bytes 5308416 | tf_op jit(solution)/shard_map/reduce_scatter | solution.py:1197
  391.1 86.1 %collective-permute-start.24 = (bf16[4,3,192,768]{3,2,1,0:T(8,128)(2,1)}, bf16[4,3,192,768]{3,2,1,0:T(8,128)(2,1)}, u32[]{:S(2)}, u32[]{:S(2)}) collective-permute-start(bf16[4,3,192,768]{3,2,1,0:T(8,128)(2,1)} %get-tuple-element.137), channel_id=1, source_target_pairs={{0,4},{4,0},{8,12},{12,8},{16,20},{20,16},{24,28},{28,24},{1,5},{5... | collective-permute-start | bytes 10616840 | tf_op jit(solution)/shard_map/ppermute | solution.py:40
  392.5 68.6 %collective-permute-start.30 = (bf16[544,1536]{1,0:T(8,128)(2,1)S(1)}, bf16[544,1536]{1,0:T(8,128)(2,1)S(1)}, u32[]{:S(2)}, u32[]{:S(2)}) collective-permute-start(bf16[544,1536]{1,0:T(8,128)(2,1)S(1)} %copy-done.11), channel_id=1, source_target_pairs={{0,8},{4,12},{8,0},{12,4},{16,24},{20,28},{24,16},{28,20},{1,9},{5... | collective-permute-start | bytes 5013512 | tf_op jit(solution)/shard_map/ppermute | solution.py:40
  393.6 67.4 %collective-permute-start.33 = (bf16[544,1536]{1,0:T(8,128)(2,1)S(1)}, bf16[544,1536]{1,0:T(8,128)(2,1)S(1)}, u32[]{:S(2)}, u32[]{:S(2)}) collective-permute-start(bf16[544,1536]{1,0:T(8,128)(2,1)S(1)} %copy-done.12), channel_id=1, source_target_pairs={{0,2},{1,3},{2,0},{3,1},{4,6},{5,7},{6,4},{7,5},{8,10},{9,11},{10,... | collective-permute-start | bytes 5013512 | tf_op jit(solution)/shard_map/ppermute | solution.py:40
  482.7 237.8 %reduce-scatter.11.cloned.1.call-start = ((), (), s32[]{:S(2)}) async-start(), calls=%async_computation.7 | async-start | bytes 5308416 | tf_op jit(solution)/shard_map/reduce_scatter | solution.py:1197
  482.8 103.4 %collective-permute-start.38 = (bf16[4,3,192,768]{3,2,1,0:T(8,128)(2,1)}, bf16[4,3,192,768]{3,2,1,0:T(8,128)(2,1)S(1)}, u32[]{:S(2)}, u32[]{:S(2)}) collective-permute-start(bf16[4,3,192,768]{3,2,1,0:T(8,128)(2,1)} %get-tuple-element.160), channel_id=1, source_target_pairs={{0,4},{4,0},{8,12},{12,8},{16,20},{20,16},{24,28},{28,24},{1,5},{5... | collective-permute-start | bytes 10616840 | tf_op jit(solution)/shard_map/ppermute | solution.py:40
  486.3 40.0 %collective-permute-start.36 = (bf16[512,1536]{1,0:T(8,128)(2,1)}, bf16[512,1536]{1,0:T(8,128)(2,1)}, u32[]{:S(2)}, u32[]{:S(2)}) collective-permute-start(bf16[512,1536]{1,0:T(8,128)(2,1)} %shard_map.295.refs_11_), channel_id=1, source_target_pairs={{0,1},{1,0},{2,3},{3,2},{4,5},{5,4},{6,7},{7,6},{8,9},{9,8},{10,11... | collective-permute-start | bytes 4718600 | tf_op jit(solution)/shard_map/ppermute | solution.py:40
  547.0 47.0 %collective-permute-start.37 = (bf16[2,8,192,768]{3,2,1,0:T(8,128)(2,1)}, bf16[2,8,192,768]{3,2,1,0:T(8,128)(2,1)}, u32[]{:S(2)}, u32[]{:S(2)}) collective-permute-start(bf16[2,8,192,768]{3,2,1,0:T(8,128)(2,1)} %get-tuple-element.158), channel_id=1, source_target_pairs={{0,1},{1,0},{2,3},{3,2},{4,5},{5,4},{6,7},{7,6},{8,9},{9,8},{10,11... | collective-permute-start | bytes 14155784 | tf_op jit(solution)/shard_map/ppermute | solution.py:40
  547.9 35.6 %collective-permute-start.42 = (bf16[256,1536]{1,0:T(8,128)(2,1)}, bf16[256,1536]{1,0:T(8,128)(2,1)}, u32[]{:S(2)}, u32[]{:S(2)}) collective-permute-start(bf16[256,1536]{1,0:T(8,128)(2,1)} %get-tuple-element.154.refs_3_), channel_id=1, source_target_pairs={{0,2},{1,3},{2,0},{3,1},{4,6},{5,7},{6,4},{7,5},{8,10},{9,11},{10,... | collective-permute-start | bytes 2359304 | tf_op jit(solution)/shard_map/ppermute | solution.py:40
  554.3 29.2 %collective-permute-start.43 = (bf16[256,1536]{1,0:T(8,128)(2,1)}, bf16[256,1536]{1,0:T(8,128)(2,1)}, u32[]{:S(2)}, u32[]{:S(2)}) collective-permute-start(bf16[256,1536]{1,0:T(8,128)(2,1)} %get-tuple-element.165), channel_id=1, source_target_pairs={{0,8},{4,12},{8,0},{12,4},{16,24},{20,28},{24,16},{28,20},{1,9},{5... | collective-permute-start | bytes 2359304 | tf_op jit(solution)/shard_map/ppermute | solution.py:40
  557.5 21.4 %collective-permute-start.41 = (bf16[512,512]{1,0:T(8,128)(2,1)S(1)}, bf16[512,512]{1,0:T(8,128)(2,1)S(1)}, u32[]{:S(2)}, u32[]{:S(2)}) collective-permute-start(bf16[512,512]{1,0:T(8,128)(2,1)S(1)} %bitcast.97), channel_id=1, source_target_pairs={{0,2},{1,3},{2,0},{3,1},{4,6},{5,7},{6,4},{7,5},{8,10},{9,11},{10,... | collective-permute-start | bytes 1572872 | tf_op jit(solution)/shard_map/ppermute | solution.py:40
  600.6 54.3 %collective-permute-start.48 = (bf16[1,8,192,768]{3,2,1,0:T(8,128)(2,1)}, bf16[1,8,192,768]{3,2,1,0:T(8,128)(2,1)S(1)}, u32[]{:S(2)}, u32[]{:S(2)}) collective-permute-start(bf16[1,8,192,768]{3,2,1,0:T(8,128)(2,1)} %get-tuple-element.173), channel_id=1, source_target_pairs={{0,2},{1,3},{2,0},{3,1},{4,6},{5,7},{6,4},{7,5},{8,10},{9,11},{10,... | collective-permute-start | bytes 7077896 | tf_op jit(solution)/shard_map/ppermute | solution.py:40
  602.3 27.4 %collective-permute-start.35 = (bf16[512,1536]{1,0:T(8,128)(2,1)S(1)}, bf16[512,1536]{1,0:T(8,128)(2,1)}, u32[]{:S(2)}, u32[]{:S(2)}) collective-permute-start(bf16[512,1536]{1,0:T(8,128)(2,1)S(1)} %copy-done.13), channel_id=1, source_target_pairs={{0,1},{1,0},{2,3},{3,2},{4,5},{5,4},{6,7},{7,6},{8,9},{9,8},{10,11... | collective-permute-start | bytes 4718600 | tf_op jit(solution)/shard_map/ppermute | solution.py:40
  606.5 73.8 %collective-permute-start.45 = (bf16[512,1536]{1,0:T(8,128)(2,1)}, bf16[512,1536]{1,0:T(8,128)(2,1)}, u32[]{:S(2)}, u32[]{:S(2)}) collective-permute-start(bf16[512,1536]{1,0:T(8,128)(2,1)} %shard_map.307), channel_id=1, source_target_pairs={{0,8},{4,12},{8,0},{12,4},{16,24},{20,28},{24,16},{28,20},{1,9},{5... | collective-permute-start | bytes 4718600 | tf_op jit(solution)/shard_map/ppermute | solution.py:40
  610.7 77.2 %collective-permute-start.47 = (bf16[512,1536]{1,0:T(8,128)(2,1)}, bf16[512,1536]{1,0:T(8,128)(2,1)}, u32[]{:S(2)}, u32[]{:S(2)}) collective-permute-start(bf16[512,1536]{1,0:T(8,128)(2,1)} %shard_map.308), channel_id=1, source_target_pairs={{0,2},{1,3},{2,0},{3,1},{4,6},{5,7},{6,4},{7,5},{8,10},{9,11},{10,... | collective-permute-start | bytes 4718600 | tf_op jit(solution)/shard_map/ppermute | solution.py:40
  695.8 50.2 %collective-permute-start.54 = (bf16[3,192,768]{2,1,0:T(8,128)(2,1)}, bf16[3,192,768]{2,1,0:T(8,128)(2,1)}, u32[]{:S(2)}, u32[]{:S(2)}) collective-permute-start(bf16[3,192,768]{2,1,0:T(8,128)(2,1)} %get-tuple-element.242), channel_id=1, source_target_pairs={{0,8},{4,12},{8,0},{12,4},{16,24},{20,28},{24,16},{28,20},{1,9},{5... | collective-permute-start | bytes 2654216 | tf_op jit(solution)/shard_map/ppermute | solution.py:40
  698.7 51.4 %collective-permute-start.53 = (bf16[3,192,768]{2,1,0:T(8,128)(2,1)}, bf16[3,192,768]{2,1,0:T(8,128)(2,1)}, u32[]{:S(2)}, u32[]{:S(2)}) collective-permute-start(bf16[3,192,768]{2,1,0:T(8,128)(2,1)} %get-tuple-element.244), channel_id=1, source_target_pairs={{0,8},{4,12},{8,0},{12,4},{16,24},{20,28},{24,16},{28,20},{1,9},{5... | collective-permute-start | bytes 2654216 | tf_op jit(solution)/shard_map/ppermute | solution.py:40
  700.7 62.8 %collective-permute-start.60 = (bf16[4,192,768]{2,1,0:T(8,128)(2,1)}, bf16[4,192,768]{2,1,0:T(8,128)(2,1)S(1)}, u32[]{:S(2)}, u32[]{:S(2)}) collective-permute-start(bf16[4,192,768]{2,1,0:T(8,128)(2,1)} %get-tuple-element.189), channel_id=1, source_target_pairs={{0,4},{4,0},{8,12},{12,8},{16,20},{20,16},{24,28},{28,24},{1,5},{5... | collective-permute-start | bytes 3538952 | tf_op jit(solution)/shard_map/ppermute | solution.py:40
  711.7 44.7 %collective-permute-start.52 = (bf16[3,192,768]{2,1,0:T(8,128)(2,1)}, bf16[3,192,768]{2,1,0:T(8,128)(2,1)S(1)}, u32[]{:S(2)}, u32[]{:S(2)}) collective-permute-start(bf16[3,192,768]{2,1,0:T(8,128)(2,1)} %get-tuple-element.246), channel_id=1, source_target_pairs={{0,8},{4,12},{8,0},{12,4},{16,24},{20,28},{24,16},{28,20},{1,9},{5... | collective-permute-start | bytes 2654216 | tf_op jit(solution)/shard_map/ppermute | solution.py:40
  719.4 14.6 %collective-permute-start.51 = (f32[40,1536]{1,0:T(8,128)S(1)}, f32[40,1536]{1,0:T(8,128)S(1)}, u32[]{:S(2)}, u32[]{:S(2)}) collective-permute-start(f32[40,1536]{1,0:T(8,128)S(1)} %add.97), channel_id=1, source_target_pairs={{0,4},{4,0},{8,12},{12,8},{16,20},{20,16},{24,28},{28,24},{1,5},{5... | collective-permute-start | bytes 737288 | tf_op jit(solution)/shard_map/ppermute | solution.py:40
  740.9 55.6 %collective-permute-start.65 = (bf16[3,192,768]{2,1,0:T(8,128)(2,1)S(1)}, bf16[3,192,768]{2,1,0:T(8,128)(2,1)}, u32[]{:S(2)}, u32[]{:S(2)}) collective-permute-start(bf16[3,192,768]{2,1,0:T(8,128)(2,1)S(1)} %get-tuple-element.240), channel_id=1, source_target_pairs={{0,8},{4,12},{8,0},{12,4},{16,24},{20,28},{24,16},{28,20},{1,9},{5... | collective-permute-start | bytes 2654216 | tf_op jit(solution)/shard_map/ppermute | solution.py:40
  761.4 24.1 %collective-permute-start.58 = (f32[40,1536]{1,0:T(8,128)}, f32[40,1536]{1,0:T(8,128)S(1)}, u32[]{:S(2)}, u32[]{:S(2)}) collective-permute-start(f32[40,1536]{1,0:T(8,128)} %shard_map.324), channel_id=1, source_target_pairs={{0,8},{4,12},{8,0},{12,4},{16,24},{20,28},{24,16},{28,20},{1,9},{5... | collective-permute-start | bytes 737288 | tf_op jit(solution)/shard_map/ppermute | solution.py:40
  761.5 21.2 %collective-permute-start.63 = (bf16[2,192,128]{2,1,0:T(8,128)(2,1)}, bf16[2,192,128]{2,1,0:T(8,128)(2,1)S(1)}, u32[]{:S(2)}, u32[]{:S(2)}) collective-permute-start(bf16[2,192,128]{2,1,0:T(8,128)(2,1)} %shard_map.327), channel_id=1, source_target_pairs={{0,8},{4,12},{8,0},{12,4},{16,24},{20,28},{24,16},{28,20},{1,9},{5... | collective-permute-start | bytes 294920 | tf_op jit(solution)/shard_map/ppermute | solution.py:40
  767.1 34.3 %collective-permute-start.61 = (bf16[2,192,768]{2,1,0:T(8,128)(2,1)}, bf16[2,192,768]{2,1,0:T(8,128)(2,1)S(1)}, u32[]{:S(2)}, u32[]{:S(2)}) collective-permute-start(bf16[2,192,768]{2,1,0:T(8,128)(2,1)} %get-tuple-element.191), channel_id=1, source_target_pairs={{0,8},{4,12},{8,0},{12,4},{16,24},{20,28},{24,16},{28,20},{1,9},{5... | collective-permute-start | bytes 1769480 | tf_op jit(solution)/shard_map/ppermute | solution.py:40
  785.5 21.2 %collective-permute-start.59 = (f32[40,1536]{1,0:T(8,128)S(1)}, f32[40,1536]{1,0:T(8,128)S(1)}, u32[]{:S(2)}, u32[]{:S(2)}) collective-permute-start(f32[40,1536]{1,0:T(8,128)S(1)} %add.101), channel_id=1, source_target_pairs={{0,16},{4,20},{8,24},{12,28},{16,0},{20,4},{24,8},{28,12},{1,17},{... | collective-permute-start | bytes 737288 | tf_op jit(solution)/shard_map/ppermute | solution.py:40
  804.3 16.1 %collective-permute-start.62 = (bf16[1,192,768]{2,1,0:T(8,128)(2,1)}, bf16[1,192,768]{2,1,0:T(8,128)(2,1)S(1)}, u32[]{:S(2)}, u32[]{:S(2)}) collective-permute-start(bf16[1,192,768]{2,1,0:T(8,128)(2,1)} %get-tuple-element.193), channel_id=1, source_target_pairs={{0,16},{4,20},{8,24},{12,28},{16,0},{20,4},{24,8},{28,12},{1,17},{... | collective-permute-start | bytes 884744 | tf_op jit(solution)/shard_map/ppermute | solution.py:40
  (63 other events, 365.7 us)
Sparse Core Ops, SparseCore 0:
  305.3 85.4 reduce-scatter.8
  393.2 85.5 reduce-scatter.6
  482.9 85.5 reduce-scatter.4
  593.5 85.5 reduce-scatter.10

commit v4 on v3

--- a/solution.py
+++ b/solution.py
@@ -564,11 +564,11 @@
         load.start()
     for load in first:
         load.wait()
-    tile = 256
-
-    @pl.loop(0, ff // tile)
+    ff_tile, tile = 384, 512
+
+    @pl.loop(0, ff // ff_tile)
     def _(t):
-        cols = column(t, tile)
+        cols = column(t, ff_tile)
         u = u_ref[...].reshape(rows, width)
         a = dot(u, wg[:, cols])
         b = dot(u, wu[:, cols])
@@ -597,9 +597,9 @@
     out_yg = pltpu.make_async_copy(yg, yg_hbm, sems.at[3])
     out_yg.start()
 
-    @pl.loop(0, ff // tile)
+    @pl.loop(0, ff // ff_tile)
     def _(t):
-        cols = column(t, tile)
+        cols = column(t, ff_tile)
         dha = dot_nt(dy[...], wd[cols, :])
         dga[:, cols] = (dha * side_gate[:, cols]).astype(BF16)
         dua[:, cols] = (dha * side_up[:, cols]).astype(BF16)

time: 840 us -> 839 us (level)
  no operation moved by 1% of the time
where the time goes in v4:
time: 839 us; the launch traced here: 827 us
  Pallas kernels  410 us (49%)
  waiting for transfers between devices  291 us (35%)
  local copies, waits for them, and re-layouts  52.7 us (6%)
  starting transfers between devices  46.6 us (6%)
  between operations  14.5 us (2%)
  other arithmetic  12.3 us (1%)
    pallas_call x84, Pallas kernels, kernel_call(): pl.pallas_call(run, grid_spec=grid_spec, out_shape=[shape for shape, _ in...  410 us
    ppermute x66, waiting for transfers between devices, swap(): return lax.ppermute(values, axis_name, [(i, i ^ bit) for i in range(count)])  291 us
    ppermute x66, starting transfers between devices, swap(): return lax.ppermute(values, axis_name, [(i, i ^ bit) for i in range(count)])  46.5 us
    unnamed x87, local copies, waits for them, and re-layouts  29.2 us
  transfers between devices with their start and end apart: 70, of which 26 were waited for; matrix products, arithmetic and copies ran while one was open for 4% of the time, Pallas kernels for 45%

profile of v4, /device:TPU:0, one launch (start us, length us, event | category | flops | bytes accessed | tf_op | source)
XLA Modules:
  0.0 827.4 jit_solution(774617201428265127)
XLA Ops:
  13.4 4.3 shard_map.247
  24.6 8.9 %collective-permute-done.1 = s32[2,5,512]{2,1,0:T(8,128)S(1)} collective-permute-done((s32[2,5,512]{2,1,0:T(8,128)S(1)}, s32[2,5,512]{2,1,0:T(8,128)S(1)}, u32[]{:S(2)}, u32[]{:S(2)}) %collective-permute-start.1) | collective-permute-done | bytes 20512 | tf_op jit(solution)/shard_map/ppermute | solution.py:40
  44.7 7.7 shard_map.248
  52.4 15.7 %shard_map.249 = (bf16[2,256,1536]{2,1,0:T(8,128)(2,1)}, f32[2,256,12]{2,1,0:T(8,128)}) custom-call(s32[2]{0:T(128)} %refs_0_.3, s32[5]{0:T(128)} %pad_add_fusion.3.refs_1_, bf16[2,256,1536]{2,1,0:T(8,128)(2,1)} %bitcast.68, bf16[2,256,512]{2,1,0:T(8,128)(2,1)} %bitcast.91, bf16[2,256,512]{2,1,0:T(8,128)(2,1)} %copy-done.15, ...), custom_call_target="tpu_custom_call" | custom-call | flops 157000000 | bytes 518100 | tf_op jit(solution)/shard_map/pallas_call | solution.py:91
  68.1 7.4 shard_map.252.refs_8_.refs_1_.refs_2_.refs_3_.refs_4_.refs_5_
  76.6 10.3 %shard_map.253 = (f32[512,1536]{1,0:T(8,128)}, bf16[544,1536]{1,0:T(8,128)(2,1)}, f32[32,512]{1,0:T(8,128)}) custom-call(bf16[512,1536]{1,0:T(8,128)(2,1)} %bitcast.74, bf16[512,1536]{1,0:T(8,128)(2,1)} %bitcast.77, bf16[1536,1536]{1,0:T(8,128)(2,1)} %refs_9_.1, f32[1,1536]{1,0:T(1,128)} %reshape.128.refs_3_.refs_5_, bf16[32,1536]{1,0:T(8,128)(2,1)} %bitcast.98, ...), custom_call_target="tpu_custom_call" | custom-call | flops 100000000 | bytes 330000 | tf_op jit(solution)/shard_map/pallas_call | solution.py:91
  113.6 12.6 %collective-permute-done.11.refs_0_ = bf16[544,1536]{1,0:T(8,128)(2,1)S(1)} collective-permute-done((bf16[544,1536]{1,0:T(8,128)(2,1)}, bf16[544,1536]{1,0:T(8,128)(2,1)S(1)}, u32[]{:S(2)}, u32[]{:S(2)}) %collective-permute-start.11) | collective-permute-done | bytes 1671200 | tf_op jit(solution)/shard_map/ppermute | solution.py:40
  153.4 16.7 %collective-permute-done.18.refs_0_ = bf16[256,1536]{1,0:T(8,128)(2,1)} collective-permute-done((bf16[256,1536]{1,0:T(8,128)(2,1)}, bf16[256,1536]{1,0:T(8,128)(2,1)}, u32[]{:S(2)}, u32[]{:S(2)}) %collective-permute-start.18) | collective-permute-done | bytes 786464 | tf_op jit(solution)/shard_map/ppermute | solution.py:40
  190.1 26.4 %shard_map.278 = (bf16[8,80,1536]{2,1,0:T(8,128)(2,1)}, bf16[8,80,1536]{2,1,0:T(8,128)(2,1)}, f32[8,80,128]{2,1,0:T(8,128)}, bf16[4,3,192,768]{3,2,1,0:T(8,128)(2,1)}, bf16[4,3,192,768]{3,2,1,0:T(8,128)(2,1)}) custom-call(s32[1]{0:T(128)} %bitcast.14.refs_0_, s32[1]{0:T(128)} %bitcast.15.refs_1_, bf16[4,80,1536]{2,1,0:T(8,128)(2,1)} %get-tuple-element.113.refs_4_.refs_2_, ...), custom_call_target="tpu_custom_call" | custom-call | flops 265000000 | bytes 874500 | tf_op jit(solution)/shard_map/pallas_call | solution.py:91
  218.1 26.0 %shard_map.279 = (bf16[8,80,1536]{2,1,0:T(8,128)(2,1)}, bf16[8,80,1536]{2,1,0:T(8,128)(2,1)}, f32[8,80,128]{2,1,0:T(8,128)}, bf16[4,3,192,768]{3,2,1,0:T(8,128)(2,1)}, bf16[4,3,192,768]{3,2,1,0:T(8,128)(2,1)}) custom-call(s32[1]{0:T(128)} %bitcast.16.refs_0_, s32[1]{0:T(128)} %bitcast.15.refs_1_, bf16[4,80,1536]{2,1,0:T(8,128)(2,1)} %get-tuple-element.113.refs_4_.refs_2_, ...), custom_call_target="tpu_custom_call" | custom-call | flops 265000000 | bytes 874500 | tf_op jit(solution)/shard_map/pallas_call | solution.py:91
  244.1 26.2 %shard_map.280 = (bf16[8,80,1536]{2,1,0:T(8,128)(2,1)}, bf16[8,80,1536]{2,1,0:T(8,128)(2,1)}, f32[8,80,128]{2,1,0:T(8,128)}, bf16[4,3,192,768]{3,2,1,0:T(8,128)(2,1)}, bf16[4,3,192,768]{3,2,1,0:T(8,128)(2,1)}) custom-call(s32[1]{0:T(128)} %bitcast.17.refs_0_, s32[1]{0:T(128)} %bitcast.15.refs_1_, bf16[4,80,1536]{2,1,0:T(8,128)(2,1)} %get-tuple-element.113.refs_4_.refs_2_, ...), custom_call_target="tpu_custom_call" | custom-call | flops 265000000 | bytes 874500 | tf_op jit(solution)/shard_map/pallas_call | solution.py:91
  270.3 26.0 %shard_map.281 = (bf16[8,80,1536]{2,1,0:T(8,128)(2,1)}, bf16[8,80,1536]{2,1,0:T(8,128)(2,1)}, f32[8,80,128]{2,1,0:T(8,128)}, bf16[4,3,192,768]{3,2,1,0:T(8,128)(2,1)}, bf16[4,3,192,768]{3,2,1,0:T(8,128)(2,1)}) custom-call(s32[1]{0:T(128)} %bitcast.18.refs_0_, s32[1]{0:T(128)} %bitcast.15.refs_1_, bf16[4,80,1536]{2,1,0:T(8,128)(2,1)} %get-tuple-element.113.refs_4_.refs_2_, ...), custom_call_target="tpu_custom_call" | custom-call | flops 265000000 | bytes 874500 | tf_op jit(solution)/shard_map/pallas_call | solution.py:91
  298.2 5.5 shard_map.282.refs_10_
  319.9 4.1 shard_map.287
  325.3 4.2 shard_map.284.refs_2_.refs_0_
  329.5 15.0 %collective-permute-done.29.refs_11_ = bf16[256,1536]{1,0:T(8,128)(2,1)} collective-permute-done((bf16[256,1536]{1,0:T(8,128)(2,1)}, bf16[256,1536]{1,0:T(8,128)(2,1)}, u32[]{:S(2)}, u32[]{:S(2)}) %collective-permute-start.29) | collective-permute-done | bytes 786464 | tf_op jit(solution)/shard_map/ppermute | solution.py:40
  344.5 4.5 shard_map.288.refs_3_
  348.9 15.0 %collective-permute-done.32.refs_11_ = bf16[288,1536]{1,0:T(8,128)(2,1)} collective-permute-done((bf16[288,1536]{1,0:T(8,128)(2,1)}, bf16[288,1536]{1,0:T(8,128)(2,1)}, u32[]{:S(2)}, u32[]{:S(2)}) %collective-permute-start.32) | collective-permute-done | bytes 884768 | tf_op jit(solution)/shard_map/ppermute | solution.py:40
  363.9 4.5 shard_map.290.refs_4_
  368.4 13.8 %collective-permute-done.34.refs_1_ = bf16[4,3,192,768]{3,2,1,0:T(8,128)(2,1)S(1)} collective-permute-done((bf16[4,3,192,768]{3,2,1,0:T(8,128)(2,1)}, bf16[4,3,192,768]{3,2,1,0:T(8,128)(2,1)S(1)}, u32[]{:S(2)}, u32[]{:S(2)}) %collective-permute-start.34) | collective-permute-done | bytes 3538976 | tf_op jit(solution)/shard_map/ppermute | solution.py:40
  384.1 5.4 shard_map.291.refs_10_
  392.6 66.9 %collective-permute-done.30.refs_1_ = bf16[544,1536]{1,0:T(8,128)(2,1)S(1)} collective-permute-done((bf16[544,1536]{1,0:T(8,128)(2,1)S(1)}, bf16[544,1536]{1,0:T(8,128)(2,1)S(1)}, u32[]{:S(2)}, u32[]{:S(2)}) %collective-permute-start.30) | collective-permute-done | bytes 1671200 | tf_op jit(solution)/shard_map/ppermute | solution.py:40
  461.8 13.8 %shard_map.292 = (f32[512,1536]{1,0:T(8,128)}, bf16[512,1536]{1,0:T(8,128)(2,1)}, bf16[512,1536]{1,0:T(8,128)(2,1)}, f32[40,1536]{1,0:T(8,128)}) custom-call(bf16[544,1536]{1,0:T(8,128)(2,1)} %shard_map.284.refs_2_.refs_0_, bf16[544,1536]{1,0:T(8,128)(2,1)} %copy-done.24, bf16[544,1536]{1,0:T(8,128)(2,1)} %copy-done.25, ...), custom_call_target="tpu_custom_call" | custom-call | flops 138000000 | bytes 455400 | tf_op jit(solution)/shard_map/pallas_call | solution.py:91
  475.7 5.5 shard_map.293.refs_6_
  496.2 28.6 %shard_map.298 = (bf16[2,256,1536]{2,1,0:T(8,128)(2,1)}, bf16[2,256,512]{2,1,0:T(8,128)(2,1)}, bf16[2,256,512]{2,1,0:T(8,128)(2,1)}, bf16[2,256,512]{2,1,0:T(8,128)(2,1)}, bf16[2,256,512]{2,1,0:T(8,128)(2,1)}) custom-call(s32[2]{0:T(128)} %refs_0_.3, s32[5]{0:T(128)} %pad_add_fusion.3.refs_1_, bf16[2,256,1536]{2,1,0:T(8,128)(2,1)} %bitcast.69, ...), custom_call_target="tpu_custom_call" | custom-call | flops 286000000 | bytes 943800 | tf_op jit(solution)/shard_map/pallas_call | solution.py:91
  528.9 8.2 shard_map.300
  537.1 8.3 %shard_map.301 = (bf16[2,8,192,768]{3,2,1,0:T(8,128)(2,1)}, bf16[2,8,192,768]{3,2,1,0:T(8,128)(2,1)}) custom-call(s32[5]{0:T(128)} %pad_add_fusion.4.refs_0_, bf16[512,1536]{1,0:T(8,128)(2,1)} %get-tuple-element.107.refs_0_.refs_1_, bf16[512,1536]{1,0:T(8,128)(2,1)} %bitcast.71, ...), custom_call_target="tpu_custom_call", output_to_operand_aliasing={{0}: (3, {}), {1}: (4, {})} | custom-call | flops 70000000 | bytes 231000 | tf_op jit(solution)/shard_map/pallas_call | solution.py:91
  546.4 6.3 collective-permute-done.40
  557.0 20.4 %collective-permute-done.41.refs_0_ = bf16[512,512]{1,0:T(8,128)(2,1)S(1)} collective-permute-done((bf16[512,512]{1,0:T(8,128)(2,1)S(1)}, bf16[512,512]{1,0:T(8,128)(2,1)S(1)}, u32[]{:S(2)}, u32[]{:S(2)}) %collective-permute-start.41) | collective-permute-done | bytes 524320 | tf_op jit(solution)/shard_map/ppermute | solution.py:40
  577.3 4.7 collective-permute-done.43.refs_3_.refs_7_
  586.4 5.5 shard_map.304.refs_4_
  592.5 6.6 shard_map.305
  600.7 4.2 shard_map.307
  605.0 4.2 shard_map.308
  609.5 6.0 shard_map.309
  615.6 12.5 %shard_map.310 = (f32[512,1536]{1,0:T(8,128)}, f32[40,1536]{1,0:T(8,128)}) custom-call(bf16[512,1536]{1,0:T(8,128)(2,1)} %bitcast.72, bf16[512,512]{1,0:T(8,128)(2,1)} %get-tuple-element.166.refs_2_.refs_1_, bf16[1536,1536]{1,0:T(8,128)(2,1)} %refs_2_.5, bf16[1536,256]{1,0:T(8,128)(2,1)} %refs_3_.3, bf16[1536,256]{1,0:T(8,128)(2,1)} %refs_4_.1, ...), custom_call_target="tpu_custom_call" | custom-call | flops 130000000 | bytes 429000 | tf_op jit(solution)/shard_map/pallas_call | solution.py:91
  632.2 21.2 %collective-permute-done.48 = bf16[1,8,192,768]{3,2,1,0:T(8,128)(2,1)S(1)} collective-permute-done((bf16[1,8,192,768]{3,2,1,0:T(8,128)(2,1)}, bf16[1,8,192,768]{3,2,1,0:T(8,128)(2,1)S(1)}, u32[]{:S(2)}, u32[]{:S(2)}) %collective-permute-start.48) | collective-permute-done | bytes 2359328 | tf_op jit(solution)/shard_map/ppermute | solution.py:40
  654.7 4.4 shard_map.311
  659.1 19.7 %collective-permute-done.45.refs_2_ = bf16[512,1536]{1,0:T(8,128)(2,1)} collective-permute-done((bf16[512,1536]{1,0:T(8,128)(2,1)}, bf16[512,1536]{1,0:T(8,128)(2,1)}, u32[]{:S(2)}, u32[]{:S(2)}) %collective-permute-start.45) | collective-permute-done | bytes 1572896 | tf_op jit(solution)/shard_map/ppermute | solution.py:40
  678.8 7.7 collective-permute-done.47.refs_3_
  686.4 5.1 shard_map.312.refs_1_
  711.5 6.4 collective-permute-done.56
  722.1 10.4 %collective-permute-done.51 = f32[40,1536]{1,0:T(8,128)S(1)} collective-permute-done((f32[40,1536]{1,0:T(8,128)S(1)}, f32[40,1536]{1,0:T(8,128)S(1)}, u32[]{:S(2)}, u32[]{:S(2)}) %collective-permute-start.51) | collective-permute-done | bytes 245792 | tf_op jit(solution)/shard_map/ppermute | solution.py:40
  744.5 4.1 shard_map.321
  748.6 4.1 shard_map.322
  765.6 15.6 %collective-permute-done.63.refs_1_.refs_3_ = bf16[2,192,128]{2,1,0:T(8,128)(2,1)S(1)} collective-permute-done((bf16[2,192,128]{2,1,0:T(8,128)(2,1)}, bf16[2,192,128]{2,1,0:T(8,128)(2,1)S(1)}, u32[]{:S(2)}, u32[]{:S(2)}) %collective-permute-start.63) | collective-permute-done | bytes 98336 | tf_op jit(solution)/shard_map/ppermute | solution.py:40
  787.0 5.6 collective-permute-done.64
  806.6 12.2 %collective-permute-done.62 = bf16[1,192,768]{2,1,0:T(8,128)(2,1)S(1)} collective-permute-done((bf16[1,192,768]{2,1,0:T(8,128)(2,1)}, bf16[1,192,768]{2,1,0:T(8,128)(2,1)S(1)}, u32[]{:S(2)}, u32[]{:S(2)}) %collective-permute-start.62) | collective-permute-done | bytes 294944 | tf_op jit(solution)/shard_map/ppermute | solution.py:40
  (312 shorter events, 234.7 us)
Async XLA Ops:
  7.2 684.4 %reduce-scatter.9.cloned.1.call-start = ((), (), s32[]{:S(2)}) async-start(), calls=%async_computation.6 | async-start | bytes 5308416 | tf_op jit(solution)/shard_map/reduce_scatter | solution.py:1197
  17.7 19.5 %collective-permute-start.3 = (bf16[2,256,512]{2,1,0:T(8,128)(2,1)}, bf16[2,256,512]{2,1,0:T(8,128)(2,1)S(1)}, u32[]{:S(2)}, u32[]{:S(2)}) collective-permute-start(bf16[2,256,512]{2,1,0:T(8,128)(2,1)} %bitcast.89), channel_id=1, source_target_pairs={{0,2},{1,3},{2,0},{3,1},{4,6},{5,7},{6,4},{7,5},{8,10},{9,11},{10,... | collective-permute-start | bytes 1572872 | tf_op jit(solution)/shard_map/ppermute | solution.py:40
  35.4 40.1 %collective-permute-start.6 = (bf16[512,1536]{1,0:T(8,128)(2,1)}, bf16[512,1536]{1,0:T(8,128)(2,1)S(1)}, u32[]{:S(2)}, u32[]{:S(2)}) collective-permute-start(bf16[512,1536]{1,0:T(8,128)(2,1)} %shard_map.250), channel_id=1, source_target_pairs={{0,8},{4,12},{8,0},{12,4},{16,24},{20,28},{24,16},{28,20},{1,9},{5... | collective-permute-start | bytes 4718600 | tf_op jit(solution)/shard_map/ppermute | solution.py:40
  38.0 37.5 %collective-permute-start.7 = (bf16[512,1536]{1,0:T(8,128)(2,1)}, bf16[512,1536]{1,0:T(8,128)(2,1)}, u32[]{:S(2)}, u32[]{:S(2)}) collective-permute-start(bf16[512,1536]{1,0:T(8,128)(2,1)} %shard_map.251), channel_id=1, source_target_pairs={{0,2},{1,3},{2,0},{3,1},{4,6},{5,7},{6,4},{7,5},{8,10},{9,11},{10,... | collective-permute-start | bytes 4718600 | tf_op jit(solution)/shard_map/ppermute | solution.py:40
  39.6 48.9 %collective-permute-start.10 = (bf16[512,1536]{1,0:T(8,128)(2,1)S(1)}, bf16[512,1536]{1,0:T(8,128)(2,1)}, u32[]{:S(2)}, u32[]{:S(2)}) collective-permute-start(bf16[512,1536]{1,0:T(8,128)(2,1)S(1)} %bitcast.66), channel_id=1, source_target_pairs={{0,1},{1,0},{2,3},{3,2},{4,5},{5,4},{6,7},{7,6},{8,9},{9,8},{10,11... | collective-permute-start | bytes 4718600 | tf_op jit(solution)/shard_map/ppermute | solution.py:40
  86.9 23.4 %collective-permute-start.12 = (bf16[544,1536]{1,0:T(8,128)(2,1)}, bf16[544,1536]{1,0:T(8,128)(2,1)}, u32[]{:S(2)}, u32[]{:S(2)}) collective-permute-start(bf16[544,1536]{1,0:T(8,128)(2,1)} %get-tuple-element.112.refs_1_.refs_2_.refs_8_), channel_id=1, source_target_pairs={{0,1},{1,0},{2,3},{3,2},{4,5},{5,4},{6,7},{7,6},{8,9},{9,8},{10,11... | collective-permute-start | bytes 5013512 | tf_op jit(solution)/shard_map/ppermute | solution.py:40
  87.5 38.7 %collective-permute-start.11 = (bf16[544,1536]{1,0:T(8,128)(2,1)}, bf16[544,1536]{1,0:T(8,128)(2,1)S(1)}, u32[]{:S(2)}, u32[]{:S(2)}) collective-permute-start(bf16[544,1536]{1,0:T(8,128)(2,1)} %get-tuple-element.112.refs_1_.refs_2_.refs_8_), channel_id=1, source_target_pairs={{0,8},{4,12},{8,0},{12,4},{16,24},{20,28},{24,16},{28,20},{1,9},{5... | collective-permute-start | bytes 5013512 | tf_op jit(solution)/shard_map/ppermute | solution.py:40
  87.9 16.0 %collective-permute-start.8 = (bf16[512,1536]{1,0:T(8,128)(2,1)}, bf16[512,1536]{1,0:T(8,128)(2,1)}, u32[]{:S(2)}, u32[]{:S(2)}) collective-permute-start(bf16[512,1536]{1,0:T(8,128)(2,1)} %shard_map.254.refs_1_), channel_id=1, source_target_pairs={{0,1},{1,0},{2,3},{3,2},{4,5},{5,4},{6,7},{7,6},{8,9},{9,8},{10,11... | collective-permute-start | bytes 4718600 | tf_op jit(solution)/shard_map/ppermute | solution.py:40
  88.5 38.9 %collective-permute-start.13 = (bf16[544,1536]{1,0:T(8,128)(2,1)}, bf16[544,1536]{1,0:T(8,128)(2,1)S(1)}, u32[]{:S(2)}, u32[]{:S(2)}) collective-permute-start(bf16[544,1536]{1,0:T(8,128)(2,1)} %get-tuple-element.112.refs_1_.refs_2_.refs_8_), channel_id=1, source_target_pairs={{0,2},{1,3},{2,0},{3,1},{4,6},{5,7},{6,4},{7,5},{8,10},{9,11},{10,... | collective-permute-start | bytes 5013512 | tf_op jit(solution)/shard_map/ppermute | solution.py:40
  128.6 21.6 %collective-permute-start.16 = (bf16[544,1536]{1,0:T(8,128)(2,1)}, bf16[544,1536]{1,0:T(8,128)(2,1)}, u32[]{:S(2)}, u32[]{:S(2)}) collective-permute-start(bf16[544,1536]{1,0:T(8,128)(2,1)} %shard_map.266.refs_1_.refs_2_), channel_id=1, source_target_pairs={{0,1},{1,0},{2,3},{3,2},{4,5},{5,4},{6,7},{7,6},{8,9},{9,8},{10,11... | collective-permute-start | bytes 5013512 | tf_op jit(solution)/shard_map/ppermute | solution.py:40
  131.2 41.9 %collective-permute-start.19 = (bf16[288,1536]{1,0:T(8,128)(2,1)}, bf16[288,1536]{1,0:T(8,128)(2,1)S(1)}, u32[]{:S(2)}, u32[]{:S(2)}) collective-permute-start(bf16[288,1536]{1,0:T(8,128)(2,1)} %slice.84), channel_id=1, source_target_pairs={{0,8},{4,12},{8,0},{12,4},{16,24},{20,28},{24,16},{28,20},{1,9},{5... | collective-permute-start | bytes 2654216 | tf_op jit(solution)/shard_map/ppermute | solution.py:40
  134.2 35.8 %collective-permute-start.18 = (bf16[256,1536]{1,0:T(8,128)(2,1)}, bf16[256,1536]{1,0:T(8,128)(2,1)}, u32[]{:S(2)}, u32[]{:S(2)}) collective-permute-start(bf16[256,1536]{1,0:T(8,128)(2,1)} %slice.83), channel_id=1, source_target_pairs={{0,8},{4,12},{8,0},{12,4},{16,24},{20,28},{24,16},{28,20},{1,9},{5... | collective-permute-start | bytes 2359304 | tf_op jit(solution)/shard_map/ppermute | solution.py:40
  136.3 33.8 %collective-permute-start.15 = (bf16[256,1536]{1,0:T(8,128)(2,1)}, bf16[256,1536]{1,0:T(8,128)(2,1)}, u32[]{:S(2)}, u32[]{:S(2)}) collective-permute-start(bf16[256,1536]{1,0:T(8,128)(2,1)} %slice.82), channel_id=1, source_target_pairs={{0,2},{1,3},{2,0},{3,1},{4,6},{5,7},{6,4},{7,5},{8,10},{9,11},{10,... | collective-permute-start | bytes 2359304 | tf_op jit(solution)/shard_map/ppermute | solution.py:40
  138.9 35.6 %collective-permute-start.14 = (bf16[256,1536]{1,0:T(8,128)(2,1)}, bf16[256,1536]{1,0:T(8,128)(2,1)S(1)}, u32[]{:S(2)}, u32[]{:S(2)}) collective-permute-start(bf16[256,1536]{1,0:T(8,128)(2,1)} %slice.81), channel_id=1, source_target_pairs={{0,2},{1,3},{2,0},{3,1},{4,6},{5,7},{6,4},{7,5},{8,10},{9,11},{10,... | collective-permute-start | bytes 2359304 | tf_op jit(solution)/shard_map/ppermute | solution.py:40
  216.5 79.8 %collective-permute-start.25 = (bf16[4,3,192,768]{3,2,1,0:T(8,128)(2,1)}, bf16[4,3,192,768]{3,2,1,0:T(8,128)(2,1)S(1)}, u32[]{:S(2)}, u32[]{:S(2)}) collective-permute-start(bf16[4,3,192,768]{3,2,1,0:T(8,128)(2,1)} %get-tuple-element.144), channel_id=1, source_target_pairs={{0,4},{4,0},{8,12},{12,8},{16,20},{20,16},{24,28},{28,24},{1,5},{5... | collective-permute-start | bytes 10616840 | tf_op jit(solution)/shard_map/ppermute | solution.py:40
  303.7 390.6 %reduce-scatter.7.cloned.1.call-start = ((), (), s32[]{:S(2)}) async-start(), calls=%async_computation.5 | async-start | bytes 5308416 | tf_op jit(solution)/shard_map/reduce_scatter | solution.py:1197
  303.7 78.6 %collective-permute-start.34 = (bf16[4,3,192,768]{3,2,1,0:T(8,128)(2,1)}, bf16[4,3,192,768]{3,2,1,0:T(8,128)(2,1)S(1)}, u32[]{:S(2)}, u32[]{:S(2)}) collective-permute-start(bf16[4,3,192,768]{3,2,1,0:T(8,128)(2,1)} %get-tuple-element.149), channel_id=1, source_target_pairs={{0,4},{4,0},{8,12},{12,8},{16,20},{20,16},{24,28},{28,24},{1,5},{5... | collective-permute-start | bytes 10616840 | tf_op jit(solution)/shard_map/ppermute | solution.py:40
  311.7 13.2 %collective-permute-start.26 = (bf16[544,1536]{1,0:T(8,128)(2,1)}, bf16[544,1536]{1,0:T(8,128)(2,1)}, u32[]{:S(2)}, u32[]{:S(2)}) collective-permute-start(bf16[544,1536]{1,0:T(8,128)(2,1)} %shard_map.283), channel_id=1, source_target_pairs={{0,1},{1,0},{2,3},{3,2},{4,5},{5,4},{6,7},{7,6},{8,9},{9,8},{10,11... | collective-permute-start | bytes 5013512 | tf_op jit(solution)/shard_map/ppermute | solution.py:40
  315.8 13.6 %collective-permute-start.27 = (bf16[544,1536]{1,0:T(8,128)(2,1)}, bf16[544,1536]{1,0:T(8,128)(2,1)}, u32[]{:S(2)}, u32[]{:S(2)}) collective-permute-start(bf16[544,1536]{1,0:T(8,128)(2,1)} %shard_map.285), channel_id=1, source_target_pairs={{0,1},{1,0},{2,3},{3,2},{4,5},{5,4},{6,7},{7,6},{8,9},{9,8},{10,11... | collective-permute-start | bytes 5013512 | tf_op jit(solution)/shard_map/ppermute | solution.py:40
  319.4 29.5 %collective-permute-start.31 = (bf16[544,1536]{1,0:T(8,128)(2,1)}, bf16[544,1536]{1,0:T(8,128)(2,1)}, u32[]{:S(2)}, u32[]{:S(2)}) collective-permute-start(bf16[544,1536]{1,0:T(8,128)(2,1)} %shard_map.289), channel_id=1, source_target_pairs={{0,1},{1,0},{2,3},{3,2},{4,5},{5,4},{6,7},{7,6},{8,9},{9,8},{10,11... | collective-permute-start | bytes 5013512 | tf_op jit(solution)/shard_map/ppermute | solution.py:40
  324.0 39.9 %collective-permute-start.32 = (bf16[288,1536]{1,0:T(8,128)(2,1)}, bf16[288,1536]{1,0:T(8,128)(2,1)}, u32[]{:S(2)}, u32[]{:S(2)}) collective-permute-start(bf16[288,1536]{1,0:T(8,128)(2,1)} %get-tuple-element.146), channel_id=1, source_target_pairs={{0,8},{4,12},{8,0},{12,4},{16,24},{20,28},{24,16},{28,20},{1,9},{5... | collective-permute-start | bytes 2654216 | tf_op jit(solution)/shard_map/ppermute | solution.py:40
  325.0 19.5 %collective-permute-start.29 = (bf16[256,1536]{1,0:T(8,128)(2,1)}, bf16[256,1536]{1,0:T(8,128)(2,1)}, u32[]{:S(2)}, u32[]{:S(2)}) collective-permute-start(bf16[256,1536]{1,0:T(8,128)(2,1)} %get-tuple-element.145), channel_id=1, source_target_pairs={{0,2},{1,3},{2,0},{3,1},{4,6},{5,7},{6,4},{7,5},{8,10},{9,11},{10,... | collective-permute-start | bytes 2359304 | tf_op jit(solution)/shard_map/ppermute | solution.py:40
  389.5 309.6 %reduce-scatter.5.cloned.1.call-start = ((), (), s32[]{:S(2)}) async-start(), calls=%async_computation.4 | async-start | bytes 5308416 | tf_op jit(solution)/shard_map/reduce_scatter | solution.py:1197
  389.6 86.1 %collective-permute-start.24 = (bf16[4,3,192,768]{3,2,1,0:T(8,128)(2,1)}, bf16[4,3,192,768]{3,2,1,0:T(8,128)(2,1)}, u32[]{:S(2)}, u32[]{:S(2)}) collective-permute-start(bf16[4,3,192,768]{3,2,1,0:T(8,128)(2,1)} %get-tuple-element.137), channel_id=1, source_target_pairs={{0,4},{4,0},{8,12},{12,8},{16,20},{20,16},{24,28},{28,24},{1,5},{5... | collective-permute-start | bytes 10616840 | tf_op jit(solution)/shard_map/ppermute | solution.py:40
  391.0 68.5 %collective-permute-start.30 = (bf16[544,1536]{1,0:T(8,128)(2,1)S(1)}, bf16[544,1536]{1,0:T(8,128)(2,1)S(1)}, u32[]{:S(2)}, u32[]{:S(2)}) collective-permute-start(bf16[544,1536]{1,0:T(8,128)(2,1)S(1)} %copy-done.11), channel_id=1, source_target_pairs={{0,8},{4,12},{8,0},{12,4},{16,24},{20,28},{24,16},{28,20},{1,9},{5... | collective-permute-start | bytes 5013512 | tf_op jit(solution)/shard_map/ppermute | solution.py:40
  392.1 67.4 %collective-permute-start.33 = (bf16[544,1536]{1,0:T(8,128)(2,1)S(1)}, bf16[544,1536]{1,0:T(8,128)(2,1)S(1)}, u32[]{:S(2)}, u32[]{:S(2)}) collective-permute-start(bf16[544,1536]{1,0:T(8,128)(2,1)S(1)} %copy-done.12), channel_id=1, source_target_pairs={{0,2},{1,3},{2,0},{3,1},{4,6},{5,7},{6,4},{7,5},{8,10},{9,11},{10,... | collective-permute-start | bytes 5013512 | tf_op jit(solution)/shard_map/ppermute | solution.py:40
  481.2 237.8 %reduce-scatter.11.cloned.1.call-start = ((), (), s32[]{:S(2)}) async-start(), calls=%async_computation.7 | async-start | bytes 5308416 | tf_op jit(solution)/shard_map/reduce_scatter | solution.py:1197
  481.2 103.4 %collective-permute-start.38 = (bf16[4,3,192,768]{3,2,1,0:T(8,128)(2,1)}, bf16[4,3,192,768]{3,2,1,0:T(8,128)(2,1)S(1)}, u32[]{:S(2)}, u32[]{:S(2)}) collective-permute-start(bf16[4,3,192,768]{3,2,1,0:T(8,128)(2,1)} %get-tuple-element.160), channel_id=1, source_target_pairs={{0,4},{4,0},{8,12},{12,8},{16,20},{20,16},{24,28},{28,24},{1,5},{5... | collective-permute-start | bytes 10616840 | tf_op jit(solution)/shard_map/ppermute | solution.py:40
  484.8 40.0 %collective-permute-start.36 = (bf16[512,1536]{1,0:T(8,128)(2,1)}, bf16[512,1536]{1,0:T(8,128)(2,1)}, u32[]{:S(2)}, u32[]{:S(2)}) collective-permute-start(bf16[512,1536]{1,0:T(8,128)(2,1)} %shard_map.295.refs_11_), channel_id=1, source_target_pairs={{0,1},{1,0},{2,3},{3,2},{4,5},{5,4},{6,7},{7,6},{8,9},{9,8},{10,11... | collective-permute-start | bytes 4718600 | tf_op jit(solution)/shard_map/ppermute | solution.py:40
  545.4 47.1 %collective-permute-start.37 = (bf16[2,8,192,768]{3,2,1,0:T(8,128)(2,1)}, bf16[2,8,192,768]{3,2,1,0:T(8,128)(2,1)}, u32[]{:S(2)}, u32[]{:S(2)}) collective-permute-start(bf16[2,8,192,768]{3,2,1,0:T(8,128)(2,1)} %get-tuple-element.158), channel_id=1, source_target_pairs={{0,1},{1,0},{2,3},{3,2},{4,5},{5,4},{6,7},{7,6},{8,9},{9,8},{10,11... | collective-permute-start | bytes 14155784 | tf_op jit(solution)/shard_map/ppermute | solution.py:40
  546.3 35.6 %collective-permute-start.42 = (bf16[256,1536]{1,0:T(8,128)(2,1)}, bf16[256,1536]{1,0:T(8,128)(2,1)}, u32[]{:S(2)}, u32[]{:S(2)}) collective-permute-start(bf16[256,1536]{1,0:T(8,128)(2,1)} %get-tuple-element.154.refs_3_), channel_id=1, source_target_pairs={{0,2},{1,3},{2,0},{3,1},{4,6},{5,7},{6,4},{7,5},{8,10},{9,11},{10,... | collective-permute-start | bytes 2359304 | tf_op jit(solution)/shard_map/ppermute | solution.py:40
  552.7 29.3 %collective-permute-start.43 = (bf16[256,1536]{1,0:T(8,128)(2,1)}, bf16[256,1536]{1,0:T(8,128)(2,1)}, u32[]{:S(2)}, u32[]{:S(2)}) collective-permute-start(bf16[256,1536]{1,0:T(8,128)(2,1)} %get-tuple-element.165), channel_id=1, source_target_pairs={{0,8},{4,12},{8,0},{12,4},{16,24},{20,28},{24,16},{28,20},{1,9},{5... | collective-permute-start | bytes 2359304 | tf_op jit(solution)/shard_map/ppermute | solution.py:40
  555.9 21.4 %collective-permute-start.41 = (bf16[512,512]{1,0:T(8,128)(2,1)S(1)}, bf16[512,512]{1,0:T(8,128)(2,1)S(1)}, u32[]{:S(2)}, u32[]{:S(2)}) collective-permute-start(bf16[512,512]{1,0:T(8,128)(2,1)S(1)} %bitcast.97), channel_id=1, source_target_pairs={{0,2},{1,3},{2,0},{3,1},{4,6},{5,7},{6,4},{7,5},{8,10},{9,11},{10,... | collective-permute-start | bytes 1572872 | tf_op jit(solution)/shard_map/ppermute | solution.py:40
  599.0 54.3 %collective-permute-start.48 = (bf16[1,8,192,768]{3,2,1,0:T(8,128)(2,1)}, bf16[1,8,192,768]{3,2,1,0:T(8,128)(2,1)S(1)}, u32[]{:S(2)}, u32[]{:S(2)}) collective-permute-start(bf16[1,8,192,768]{3,2,1,0:T(8,128)(2,1)} %get-tuple-element.173), channel_id=1, source_target_pairs={{0,2},{1,3},{2,0},{3,1},{4,6},{5,7},{6,4},{7,5},{8,10},{9,11},{10,... | collective-permute-start | bytes 7077896 | tf_op jit(solution)/shard_map/ppermute | solution.py:40
  600.7 27.4 %collective-permute-start.35 = (bf16[512,1536]{1,0:T(8,128)(2,1)S(1)}, bf16[512,1536]{1,0:T(8,128)(2,1)}, u32[]{:S(2)}, u32[]{:S(2)}) collective-permute-start(bf16[512,1536]{1,0:T(8,128)(2,1)S(1)} %copy-done.13), channel_id=1, source_target_pairs={{0,1},{1,0},{2,3},{3,2},{4,5},{5,4},{6,7},{7,6},{8,9},{9,8},{10,11... | collective-permute-start | bytes 4718600 | tf_op jit(solution)/shard_map/ppermute | solution.py:40
  605.0 73.8 %collective-permute-start.45 = (bf16[512,1536]{1,0:T(8,128)(2,1)}, bf16[512,1536]{1,0:T(8,128)(2,1)}, u32[]{:S(2)}, u32[]{:S(2)}) collective-permute-start(bf16[512,1536]{1,0:T(8,128)(2,1)} %shard_map.307), channel_id=1, source_target_pairs={{0,8},{4,12},{8,0},{12,4},{16,24},{20,28},{24,16},{28,20},{1,9},{5... | collective-permute-start | bytes 4718600 | tf_op jit(solution)/shard_map/ppermute | solution.py:40
  609.2 77.2 %collective-permute-start.47 = (bf16[512,1536]{1,0:T(8,128)(2,1)}, bf16[512,1536]{1,0:T(8,128)(2,1)}, u32[]{:S(2)}, u32[]{:S(2)}) collective-permute-start(bf16[512,1536]{1,0:T(8,128)(2,1)} %shard_map.308), channel_id=1, source_target_pairs={{0,2},{1,3},{2,0},{3,1},{4,6},{5,7},{6,4},{7,5},{8,10},{9,11},{10,... | collective-permute-start | bytes 4718600 | tf_op jit(solution)/shard_map/ppermute | solution.py:40
  694.3 50.2 %collective-permute-start.54 = (bf16[3,192,768]{2,1,0:T(8,128)(2,1)}, bf16[3,192,768]{2,1,0:T(8,128)(2,1)}, u32[]{:S(2)}, u32[]{:S(2)}) collective-permute-start(bf16[3,192,768]{2,1,0:T(8,128)(2,1)} %get-tuple-element.242), channel_id=1, source_target_pairs={{0,8},{4,12},{8,0},{12,4},{16,24},{20,28},{24,16},{28,20},{1,9},{5... | collective-permute-start | bytes 2654216 | tf_op jit(solution)/shard_map/ppermute | solution.py:40
  697.1 51.4 %collective-permute-start.53 = (bf16[3,192,768]{2,1,0:T(8,128)(2,1)}, bf16[3,192,768]{2,1,0:T(8,128)(2,1)}, u32[]{:S(2)}, u32[]{:S(2)}) collective-permute-start(bf16[3,192,768]{2,1,0:T(8,128)(2,1)} %get-tuple-element.244), channel_id=1, source_target_pairs={{0,8},{4,12},{8,0},{12,4},{16,24},{20,28},{24,16},{28,20},{1,9},{5... | collective-permute-start | bytes 2654216 | tf_op jit(solution)/shard_map/ppermute | solution.py:40
  699.2 62.8 %collective-permute-start.60 = (bf16[4,192,768]{2,1,0:T(8,128)(2,1)}, bf16[4,192,768]{2,1,0:T(8,128)(2,1)S(1)}, u32[]{:S(2)}, u32[]{:S(2)}) collective-permute-start(bf16[4,192,768]{2,1,0:T(8,128)(2,1)} %get-tuple-element.189), channel_id=1, source_target_pairs={{0,4},{4,0},{8,12},{12,8},{16,20},{20,16},{24,28},{28,24},{1,5},{5... | collective-permute-start | bytes 3538952 | tf_op jit(solution)/shard_map/ppermute | solution.py:40
  710.1 44.7 %collective-permute-start.52 = (bf16[3,192,768]{2,1,0:T(8,128)(2,1)}, bf16[3,192,768]{2,1,0:T(8,128)(2,1)S(1)}, u32[]{:S(2)}, u32[]{:S(2)}) collective-permute-start(bf16[3,192,768]{2,1,0:T(8,128)(2,1)} %get-tuple-element.246), channel_id=1, source_target_pairs={{0,8},{4,12},{8,0},{12,4},{16,24},{20,28},{24,16},{28,20},{1,9},{5... | collective-permute-start | bytes 2654216 | tf_op jit(solution)/shard_map/ppermute | solution.py:40
  717.9 14.6 %collective-permute-start.51 = (f32[40,1536]{1,0:T(8,128)S(1)}, f32[40,1536]{1,0:T(8,128)S(1)}, u32[]{:S(2)}, u32[]{:S(2)}) collective-permute-start(f32[40,1536]{1,0:T(8,128)S(1)} %add.97), channel_id=1, source_target_pairs={{0,4},{4,0},{8,12},{12,8},{16,20},{20,16},{24,28},{28,24},{1,5},{5... | collective-permute-start | bytes 737288 | tf_op jit(solution)/shard_map/ppermute | solution.py:40
  739.4 55.6 %collective-permute-start.65 = (bf16[3,192,768]{2,1,0:T(8,128)(2,1)S(1)}, bf16[3,192,768]{2,1,0:T(8,128)(2,1)}, u32[]{:S(2)}, u32[]{:S(2)}) collective-permute-start(bf16[3,192,768]{2,1,0:T(8,128)(2,1)S(1)} %get-tuple-element.240), channel_id=1, source_target_pairs={{0,8},{4,12},{8,0},{12,4},{16,24},{20,28},{24,16},{28,20},{1,9},{5... | collective-permute-start | bytes 2654216 | tf_op jit(solution)/shard_map/ppermute | solution.py:40
  759.9 24.1 %collective-permute-start.58 = (f32[40,1536]{1,0:T(8,128)}, f32[40,1536]{1,0:T(8,128)S(1)}, u32[]{:S(2)}, u32[]{:S(2)}) collective-permute-start(f32[40,1536]{1,0:T(8,128)} %shard_map.324), channel_id=1, source_target_pairs={{0,8},{4,12},{8,0},{12,4},{16,24},{20,28},{24,16},{28,20},{1,9},{5... | collective-permute-start | bytes 737288 | tf_op jit(solution)/shard_map/ppermute | solution.py:40
  760.0 21.2 %collective-permute-start.63 = (bf16[2,192,128]{2,1,0:T(8,128)(2,1)}, bf16[2,192,128]{2,1,0:T(8,128)(2,1)S(1)}, u32[]{:S(2)}, u32[]{:S(2)}) collective-permute-start(bf16[2,192,128]{2,1,0:T(8,128)(2,1)} %shard_map.327), channel_id=1, source_target_pairs={{0,8},{4,12},{8,0},{12,4},{16,24},{20,28},{24,16},{28,20},{1,9},{5... | collective-permute-start | bytes 294920 | tf_op jit(solution)/shard_map/ppermute | solution.py:40
  765.5 34.3 %collective-permute-start.61 = (bf16[2,192,768]{2,1,0:T(8,128)(2,1)}, bf16[2,192,768]{2,1,0:T(8,128)(2,1)S(1)}, u32[]{:S(2)}, u32[]{:S(2)}) collective-permute-start(bf16[2,192,768]{2,1,0:T(8,128)(2,1)} %get-tuple-element.191), channel_id=1, source_target_pairs={{0,8},{4,12},{8,0},{12,4},{16,24},{20,28},{24,16},{28,20},{1,9},{5... | collective-permute-start | bytes 1769480 | tf_op jit(solution)/shard_map/ppermute | solution.py:40
  784.0 21.2 %collective-permute-start.59 = (f32[40,1536]{1,0:T(8,128)S(1)}, f32[40,1536]{1,0:T(8,128)S(1)}, u32[]{:S(2)}, u32[]{:S(2)}) collective-permute-start(f32[40,1536]{1,0:T(8,128)S(1)} %add.101), channel_id=1, source_target_pairs={{0,16},{4,20},{8,24},{12,28},{16,0},{20,4},{24,8},{28,12},{1,17},{... | collective-permute-start | bytes 737288 | tf_op jit(solution)/shard_map/ppermute | solution.py:40
  802.7 16.1 %collective-permute-start.62 = (bf16[1,192,768]{2,1,0:T(8,128)(2,1)}, bf16[1,192,768]{2,1,0:T(8,128)(2,1)S(1)}, u32[]{:S(2)}, u32[]{:S(2)}) collective-permute-start(bf16[1,192,768]{2,1,0:T(8,128)(2,1)} %get-tuple-element.193), channel_id=1, source_target_pairs={{0,16},{4,20},{8,24},{12,28},{16,0},{20,4},{24,8},{28,12},{1,17},{... | collective-permute-start | bytes 884744 | tf_op jit(solution)/shard_map/ppermute | solution.py:40
  (63 other events, 365.8 us)
Sparse Core Ops, SparseCore 0:
  303.8 85.4 reduce-scatter.8
  391.6 85.5 reduce-scatter.6
  481.3 85.5 reduce-scatter.4
  592.0 85.5 reduce-scatter.10
